TPU v7x, 256 devices: a whole 4x4x8 slice. The times are simulated.
256 devices in a mesh: rep: 32 (over z, x), section: 4 (over y), tp: 2 (over core).
Axes of the slice: x: 4, y: 4, z: 8, core: 2. Of those that a mesh axis runs over, the one named last changes fastest.
Arguments:
- inputs: bfloat16 [4, 16384, 768], P('section', 'rep', 'tp'), may hold values from -6 to 6
- loss_grad: bfloat16 [16384, 768], P('rep', 'tp'), may hold values from -6 to 6
- w_in: bfloat16 [32, 4, 3072, 768], P('rep', 'section', 'tp'), may hold values from -6 to 6
- w_out: bfloat16 [32, 4, 3072, 768], P('rep', 'section', 'tp'), may hold values from -6 to 6
- mixing: float32 [32, 32], replicated, may hold values from 0 to 1, as said below
Outputs:
- input_grads: bfloat16 [4, 16384, 768], P('section', 'rep', 'tp')
- mixed_in: bfloat16 [32, 4, 3072, 768], P('rep', 'section', 'tp')
- mixed_out: bfloat16 [32, 4, 3072, 768], P('rep', 'section', 'tp')
Inputs may be any that keep to these rules, and one draw needn't show every extreme that they name: `mixing`: every row and every column sums to one; every entry is positive.
All inputs are finite; a program needn't handle non-finite values.
Results may differ from a plain program's by a relative error of at most 0.023.
Values may be sent and summed in bfloat16 or wider, within the bound.
No kernel may reach another device: no remote copies, remote signals or barrier semaphores. Data moves between devices by JAX's collectives and lax.ppermute only.
A program may use at most 128 MiB of HBM per device.

v0:
```python
import jax
import jax.numpy as jnp
from jax import lax
from jax.sharding import PartitionSpec as P

D = 768
FF = 3072


step_size = 4.0
root_half = 0.7071067811865476
inv_root_two_pi = 0.3989422804014327


def passed_along(shard, axis, by):
    length = lax.axis_size(axis)
    pairs = [(i, i + by) for i in range(length) if 0 <= i + by < length]
    return lax.ppermute(shard, axis, pairs)


def gelu_parts(preact):
    normal_cdf = 0.5 * (1.0 + lax.erf(preact * root_half))
    density = jnp.exp(-0.5 * preact * preact) * inv_root_two_pi
    return (preact * normal_cdf, normal_cdf + preact * density)


def contract_last(left, right):
    return lax.dot_general(
        left, right, (((1,), (1,)), ((), ())), preferred_element_type=jnp.float32
    )


def contract_first(left, right):
    return lax.dot_general(
        left, right, (((0,), (0,)), ((), ())), preferred_element_type=jnp.float32
    )


def shards(inputs, loss_grad, w_in, w_out, mixing):
    segments = lax.axis_size("section")
    segment_index = lax.axis_index("section")
    weight_in = w_in[0, 0]
    weight_out = w_out[0, 0]
    in_scale = D ** (-0.5)
    out_scale = FF ** (-0.5)
    gathered_x = lax.all_gather(inputs[0], "tp", axis=1, tiled=True)
    preact = contract_last(gathered_x, weight_in) * in_scale
    values, slopes = gelu_parts(preact)
    act_rows = values.astype(jnp.bfloat16)
    cot_share = loss_grad
    kept_dy = jnp.zeros_like(gathered_x)
    kept_delta = jnp.zeros(preact.shape, jnp.bfloat16)
    kept_dx = jnp.zeros_like(loss_grad)
    zero_grad = jnp.zeros(weight_in.shape, jnp.float32)
    grad_pair = (zero_grad, zero_grad)
    for turn_index in range(segments):
        gathered_dy = lax.all_gather(cot_share, "tp", axis=1, tiled=True)
        backward = contract_last(gathered_dy, weight_out) * out_scale
        delta_rows = (slopes * backward).astype(jnp.bfloat16)
        partial_value = (
            jnp.dot(delta_rows, weight_in, preferred_element_type=jnp.float32) * in_scale
        )
        branch = lax.psum_scatter(
            partial_value.astype(jnp.bfloat16), "tp", scatter_dimension=1, tiled=True
        ).astype(jnp.float32)
        result = (cot_share.astype(jnp.float32) + branch).astype(jnp.bfloat16)
        active = segment_index == segments - 1 - turn_index
        kept_dx = jnp.where(active, result, kept_dx)
        kept_dy = jnp.where(active, gathered_dy, kept_dy)
        kept_delta = jnp.where(active, delta_rows, kept_delta)
        if turn_index + 1 < segments:
            cot_share = passed_along(result, "section", -1)
    grad_pair = (
        contract_first(kept_delta, gathered_x) * in_scale,
        contract_first(act_rows, kept_dy) * out_scale,
    )
    updated_in = (weight_in.astype(jnp.float32) - step_size * grad_pair[0]).astype(jnp.bfloat16)
    updated_out = (weight_out.astype(jnp.float32) - step_size * grad_pair[1]).astype(jnp.bfloat16)
    pieces = (
        lax.all_to_all(updated_in[None], "rep", split_axis=2, concat_axis=0, tiled=True),
        lax.all_to_all(updated_out[None], "rep", split_axis=2, concat_axis=0, tiled=True),
    )
    mixed_pair = tuple(
        (
            jnp.einsum(
                "rq,qwc->rwc", mixing, block.astype(jnp.float32), precision=lax.Precision.HIGHEST
            ).astype(jnp.bfloat16)
            for block in pieces
        )
    )
    mixed_in = lax.all_to_all(mixed_pair[0], "rep", split_axis=0, concat_axis=2, tiled=True)
    mixed_out = lax.all_to_all(mixed_pair[1], "rep", split_axis=0, concat_axis=2, tiled=True)
    return (kept_dx[None], mixed_in[None], mixed_out[None])


def solution(mesh):
    in_specs = (
        P("section", "rep", "tp"),
        P("rep", "tp"),
        P("rep", "section", "tp", None),
        P("rep", "section", "tp", None),
        P(),
    )
    out_specs = (
        P("section", "rep", "tp"),
        P("rep", "section", "tp", None),
        P("rep", "section", "tp", None),
    )
    return jax.shard_map(shards, mesh=mesh, in_specs=in_specs, out_specs=out_specs, check_vma=False)
```

profile of v0, /device:TPU:16, one launch (start us, length us, event | category | flops | bytes accessed | tf_op | source)
XLA Modules:
  0.0 438.2 jit_solution(858455732843157696)
XLA Ops:
  12.4 5.4 %multiply_add_fusion = (f32[512,1536]{1,0:T(8,128)S(1)}, f32[512,1536]{1,0:T(8,128)}) fusion(bf16[1,1,1536,768]{3,2,1,0:T(8,128)(2,1)} %param.7, bf16[1,512,768]{2,1,0:T(8,128)(2,1)S(1)} %all-gather), kind=kOutput, calls=%fused_computation.13 | convolution fusion | flops 1215037440 | bytes 9437184 | tf_op jit(solution)/shard_map/dot_general | solution.py:28
  25.1 16.4 %reduce-scatter.13.cloned.1.call-done = bf16[384,512]{1,0:T(8,128)(2,1)} async-done(((bf16[768,512]{1,0:T(8,128)(2,1)}), bf16[384,512]{1,0:T(8,128)(2,1)}) %reduce-scatter.13.cloned.1.call-update) | async-done | bytes 393232
  46.3 10.8 %collective-permute-done = bf16[512,384]{1,0:T(8,128)(2,1)S(1)} collective-permute-done((bf16[512,384]{1,0:T(8,128)(2,1)S(1)}, bf16[512,384]{1,0:T(8,128)(2,1)S(1)}, u32[]{:S(2)}, u32[]{:S(2)}) %collective-permute-start) | collective-permute-done | bytes 393248 | tf_op jit(solution)/shard_map/ppermute | solution.py:18
  69.4 15.0 %reduce-scatter.15.cloned.1.call-done = bf16[384,512]{1,0:T(8,128)(2,1)} async-done(((bf16[768,512]{1,0:T(8,128)(2,1)}), bf16[384,512]{1,0:T(8,128)(2,1)}) %reduce-scatter.15.cloned.1.call-update) | async-done | bytes 393232
  89.2 10.8 %collective-permute-done.1 = bf16[512,384]{1,0:T(8,128)(2,1)S(1)} collective-permute-done((bf16[512,384]{1,0:T(8,128)(2,1)S(1)}, bf16[512,384]{1,0:T(8,128)(2,1)S(1)}, u32[]{:S(2)}, u32[]{:S(2)}) %collective-permute-start.1) | collective-permute-done | bytes 393248 | tf_op jit(solution)/shard_map/ppermute | solution.py:18
  112.3 15.0 %reduce-scatter.17.cloned.1.call-done = bf16[384,512]{1,0:T(8,128)(2,1)} async-done(((bf16[768,512]{1,0:T(8,128)(2,1)}), bf16[384,512]{1,0:T(8,128)(2,1)}) %reduce-scatter.17.cloned.1.call-update) | async-done | bytes 393232
  132.8 11.0 %collective-permute-done.2 = bf16[512,384]{1,0:T(8,128)(2,1)S(1)} collective-permute-done((bf16[512,384]{1,0:T(8,128)(2,1)}, bf16[512,384]{1,0:T(8,128)(2,1)S(1)}, u32[]{:S(2)}, u32[]{:S(2)}) %collective-permute-start.2) | collective-permute-done | bytes 393248 | tf_op jit(solution)/shard_map/ppermute | solution.py:18
  153.3 8.6 %copy.18 = bf16[1,1536,768]{1,0,2:T(2,128)(2,1)} copy(bf16[1,1536,768]{2,1,0:T(8,128)(2,1)S(1)} %fusion.10) | data formatting | bytes 4718592 | tf_op jit(solution)/shard_map/broadcast_in_dim | solution.py:80
  162.4 15.6 %reduce = bf16[768,1536]{1,0:T(8,128)(2,1)S(1)} reduce(bf16[768,1,1536]{2,1,0:T(2,128)(2,1)} %bitcast.96, bf16[]{:T(256)} %broadcast.21), dimensions={1}, to_apply=%bitcast.80.reduce_sub_computation | reduce | bytes 4718594
  180.4 10.2 %all-to-all-start = ((bf16[32,2,18432]{2,1,0:T(2,128)(2,1)}), bf16[32,2,18432]{2,1,0:T(2,128)(2,1)}, u32[]{:S(2)}, u32[]{:S(2)}) async-start(bf16[32,2,18432]{2,1,0:T(2,128)(2,1)} %reshape.18), calls=%async_computation | async-start | bytes 4718592 | tf_op jit(solution)/shard_map/all_to_all | solution.py:80
  190.6 5.2 %fusion.11 = bf16[1,1536,768]{2,1,0:T(8,128)(2,1)} fusion(bf16[1,1,1536,768]{3,2,1,0:T(8,128)(2,1)S(1)} %copy-done.2, f32[512,1536]{1,0:T(8,128)} %get-tuple-element.10, bf16[512,768]{1,0:T(8,128)(2,1)} %copy-done.7, bf16[512,768]{1,0:T(8,128)(2,1)} %copy-done.6, bf16[512,768]{1,0:T(8,128)(2,1)} %copy-done.5, bf16[512,768]{1,0:T(8,128)(2,1)S(1)} %copy-done.4, ...), kind=kOutput, calls=%fused_computation.22 | convolution fusion | flops 1218969600 | bytes 11010052 | tf_op jit(solution)/shard_map/dot_general | solution.py:34
  195.8 12.1 %copy.21 = bf16[1,1536,768]{1,0,2:T(2,128)(2,1)} copy(bf16[1,1536,768]{2,1,0:T(8,128)(2,1)} %fusion.11) | data formatting | bytes 4718592 | tf_op jit(solution)/shard_map/broadcast_in_dim | solution.py:81
  207.9 15.6 %reduce.1 = bf16[768,1536]{1,0:T(8,128)(2,1)S(1)} reduce(bf16[768,1,1536]{2,1,0:T(2,128)(2,1)} %bitcast.97, bf16[]{:T(256)} %broadcast.21), dimensions={1}, to_apply=%bitcast.82.reduce_sub_computation | reduce | bytes 4718594
  225.9 20.7 %all-to-all-done = bf16[32,2,18432]{2,1,0:T(2,128)(2,1)} async-done(((bf16[32,2,18432]{2,1,0:T(2,128)(2,1)}), bf16[32,2,18432]{2,1,0:T(2,128)(2,1)}, u32[]{:S(2)}, u32[]{:S(2)}) %all-to-all-start) | async-done | bytes 2359328 | tf_op jit(solution)/shard_map/all_to_all | solution.py:80
  246.6 5.7 %all-to-all-start.2 = ((bf16[32,2,18432]{2,1,0:T(2,128)(2,1)}), bf16[32,2,18432]{2,1,0:T(2,128)(2,1)S(1)}, u32[]{:S(2)}, u32[]{:S(2)}) async-start(bf16[32,2,18432]{2,1,0:T(2,128)(2,1)} %reshape.20), calls=%async_computation.2 | async-start | bytes 4718592 | tf_op jit(solution)/shard_map/all_to_all | solution.py:81
  252.3 10.7 %reshape.19 = bf16[768,1,1536]{2,1,0:T(2,128)(2,1)} reshape(bf16[32,2,18432]{2,1,0:T(2,128)(2,1)} %all-to-all-done) | data formatting | bytes 4718592
  270.8 37.0 %all-to-all-done.2 = bf16[32,2,18432]{2,1,0:T(2,128)(2,1)S(1)} async-done(((bf16[32,2,18432]{2,1,0:T(2,128)(2,1)}), bf16[32,2,18432]{2,1,0:T(2,128)(2,1)S(1)}, u32[]{:S(2)}, u32[]{:S(2)}) %all-to-all-start.2) | async-done | bytes 2359328 | tf_op jit(solution)/shard_map/all_to_all | solution.py:81
  307.8 5.6 %all-to-all-start.1 = ((bf16[32,1536,24]{1,2,0:T(8,128)(2,1)}), bf16[32,1536,24]{1,2,0:T(8,128)(2,1)}, u32[]{:S(2)}, u32[]{:S(2)}) async-start(bf16[32,1536,24]{1,2,0:T(8,128)(2,1)} %copy.20), calls=%async_computation.1 | async-start | bytes 4718592 | tf_op jit(solution)/shard_map/all_to_all | solution.py:91
  313.4 7.0 %reshape.21 = bf16[768,1,1536]{2,1,0:T(2,128)(2,1)} reshape(bf16[32,2,18432]{2,1,0:T(2,128)(2,1)S(1)} %all-to-all-done.2) | data formatting | bytes 4718592
  328.3 40.5 %all-to-all-done.1 = bf16[32,1536,24]{1,2,0:T(8,128)(2,1)} async-done(((bf16[32,1536,24]{1,2,0:T(8,128)(2,1)}), bf16[32,1536,24]{1,2,0:T(8,128)(2,1)}, u32[]{:S(2)}, u32[]{:S(2)}) %all-to-all-start.1) | async-done | bytes 2359328 | tf_op jit(solution)/shard_map/all_to_all | solution.py:91
  368.8 6.0 %all-to-all-start.3 = ((bf16[32,1536,24]{1,2,0:T(8,128)(2,1)}), bf16[32,1536,24]{1,2,0:T(8,128)(2,1)S(1)}, u32[]{:S(2)}, u32[]{:S(2)}) async-start(bf16[32,1536,24]{1,2,0:T(8,128)(2,1)} %copy.23), calls=%async_computation.3 | async-start | bytes 4718592 | tf_op jit(solution)/shard_map/all_to_all | solution.py:92
  374.9 4.4 %multiply_convert_fusion.2 = bf16[512,768]{1,0:T(8,128)(2,1)} fusion(bf16[512,1536]{1,0:T(8,128)(2,1)} %copy-done.19, bf16[1,1,1536,768]{3,2,1,0:T(8,128)(2,1)} %param.7), kind=kOutput, calls=%fused_computation.45 | convolution fusion | flops 1208745984 | bytes 4718592 | tf_op jit(solution)/shard_map/dot_general | solution.py:61
  381.7 15.0 %reduce-scatter.19.cloned.1.call-done = bf16[384,512]{1,0:T(8,128)(2,1)} async-done(((bf16[768,512]{1,0:T(8,128)(2,1)}), bf16[384,512]{1,0:T(8,128)(2,1)}) %reduce-scatter.19.cloned.1.call-update) | async-done | bytes 393232
  404.1 25.2 %all-to-all-done.3 = bf16[32,1536,24]{1,2,0:T(8,128)(2,1)S(1)} async-done(((bf16[32,1536,24]{1,2,0:T(8,128)(2,1)}), bf16[32,1536,24]{1,2,0:T(8,128)(2,1)S(1)}, u32[]{:S(2)}, u32[]{:S(2)}) %all-to-all-start.3) | async-done | bytes 2359328 | tf_op jit(solution)/shard_map/all_to_all | solution.py:92
  (103 shorter events, 94.6 us)
Async XLA Ops:
  7.2 258.8 %copy-start = (f32[32,32]{1,0:T(8,128)S(1)}, f32[32,32]{1,0:T(8,128)}, u32[]{:S(2)}) copy-start(f32[32,32]{1,0:T(8,128)} %param.9) | copy-start | bytes 12292
  7.2 34.4 %reduce-scatter.13.cloned.1.call-start = ((), (), s32[]{:S(2)}) async-start(), calls=%async_computation.8 | async-start | bytes 1179648
  9.8 8.0 %copy-start.22 = (bf16[1,512,768]{2,1,0:T(8,128)(2,1)}, bf16[1,512,768]{2,1,0:T(8,128)(2,1)S(1)}, u32[]{:S(2)}) copy-start(bf16[1,512,768]{2,1,0:T(8,128)(2,1)S(1)} %all-gather) | copy-start | bytes 2359300
  12.4 5.4 %copy-start.3 = (bf16[512,768]{1,0:T(8,128)(2,1)}, bf16[512,768]{1,0:T(8,128)(2,1)S(1)}, u32[]{:S(2)}) copy-start(bf16[512,768]{1,0:T(8,128)(2,1)S(1)} %all_gather.16) | copy-start | bytes 2359300
  12.4 5.4 %copy-start.1 = (bf16[1,1,1536,768]{3,2,1,0:T(8,128)(2,1)S(1)}, bf16[1,1,1536,768]{3,2,1,0:T(8,128)(2,1)}, u32[]{:S(2)}) copy-start(bf16[1,1,1536,768]{3,2,1,0:T(8,128)(2,1)} %param.8) | copy-start | bytes 7077892
  25.0 59.4 %reduce-scatter.15.cloned.1.call-start = ((), (), s32[]{:S(2)}) async-start(), calls=%async_computation.9 | async-start | bytes 1179648
  43.8 13.2 %copy-start.10 = (bf16[512,384]{1,0:T(8,128)(2,1)}, bf16[512,384]{1,0:T(8,128)(2,1)S(1)}, u32[]{:S(2)}) copy-start(bf16[512,384]{1,0:T(8,128)(2,1)S(1)} %add_convert_fusion.3) | copy-start | bytes 1179652
  43.9 13.2 %collective-permute-start = (bf16[512,384]{1,0:T(8,128)(2,1)S(1)}, bf16[512,384]{1,0:T(8,128)(2,1)S(1)}, u32[]{:S(2)}, u32[]{:S(2)}) collective-permute-start(bf16[512,384]{1,0:T(8,128)(2,1)S(1)} %add_convert_fusion.3), channel_id=1, source_target_pairs={{2,0},{4,2},{6,4},{3,1},{5,3},{7,5},{10,8},{12,10},{14,12},{11,9},... | collective-permute-start | bytes 1179656 | tf_op jit(solution)/shard_map/ppermute | solution.py:18
  60.2 4.6 %copy-start.25 = (bf16[1,1,1536,768]{3,2,1,0:T(8,128)(2,1)S(1)}, bf16[1,1,1536,768]{3,2,1,0:T(8,128)(2,1)}, u32[]{:S(2)}) copy-start(bf16[1,1,1536,768]{3,2,1,0:T(8,128)(2,1)} %param.7) | copy-start | bytes 7077892
  69.4 57.9 %reduce-scatter.17.cloned.1.call-start = ((), (), s32[]{:S(2)}) async-start(), calls=%async_computation.10 | async-start | bytes 1179648
  86.7 13.3 %copy-start.12 = (bf16[512,384]{1,0:T(8,128)(2,1)}, bf16[512,384]{1,0:T(8,128)(2,1)S(1)}, u32[]{:S(2)}) copy-start(bf16[512,384]{1,0:T(8,128)(2,1)S(1)} %add_convert_fusion.2) | copy-start | bytes 1179652
  86.7 13.2 %collective-permute-start.1 = (bf16[512,384]{1,0:T(8,128)(2,1)S(1)}, bf16[512,384]{1,0:T(8,128)(2,1)S(1)}, u32[]{:S(2)}, u32[]{:S(2)}) collective-permute-start(bf16[512,384]{1,0:T(8,128)(2,1)S(1)} %add_convert_fusion.2), channel_id=1, source_target_pairs={{2,0},{4,2},{6,4},{3,1},{5,3},{7,5},{10,8},{12,10},{14,12},{11,9},... | collective-permute-start | bytes 1179656 | tf_op jit(solution)/shard_map/ppermute | solution.py:18
  103.1 4.6 %copy-start.26 = (bf16[1,1,1536,768]{3,2,1,0:T(8,128)(2,1)S(1)}, bf16[1,1,1536,768]{3,2,1,0:T(8,128)(2,1)}, u32[]{:S(2)}) copy-start(bf16[1,1,1536,768]{3,2,1,0:T(8,128)(2,1)} %param.7) | copy-start | bytes 7077892
  130.3 13.4 %collective-permute-start.2 = (bf16[512,384]{1,0:T(8,128)(2,1)}, bf16[512,384]{1,0:T(8,128)(2,1)S(1)}, u32[]{:S(2)}, u32[]{:S(2)}) collective-permute-start(bf16[512,384]{1,0:T(8,128)(2,1)} %add_convert_fusion.1), channel_id=1, source_target_pairs={{2,0},{4,2},{6,4},{3,1},{5,3},{7,5},{10,8},{12,10},{14,12},{11,9},... | collective-permute-start | bytes 1179656 | tf_op jit(solution)/shard_map/ppermute | solution.py:18
  143.7 6.7 %copy-start.14 = (bf16[512,384]{1,0:T(8,128)(2,1)}, bf16[512,384]{1,0:T(8,128)(2,1)S(1)}, u32[]{:S(2)}) copy-start(bf16[512,384]{1,0:T(8,128)(2,1)S(1)} %collective-permute-done.2) | copy-start | bytes 1179652
  180.4 10.2 %copy-start.2 = (bf16[1,1,1536,768]{3,2,1,0:T(8,128)(2,1)S(1)}, bf16[1,1,1536,768]{3,2,1,0:T(8,128)(2,1)}, u32[]{:S(2)}) copy-start(bf16[1,1,1536,768]{3,2,1,0:T(8,128)(2,1)} %param.8) | copy-start | bytes 7077892
  180.4 10.2 %copy-start.4 = (bf16[512,768]{1,0:T(8,128)(2,1)S(1)}, bf16[512,768]{1,0:T(8,128)(2,1)}, u32[]{:S(2)}) copy-start(bf16[512,768]{1,0:T(8,128)(2,1)} %copy-done.3) | copy-start | bytes 2359300
  180.4 66.2 %all-to-all-start = ((bf16[32,2,18432]{2,1,0:T(2,128)(2,1)}), bf16[32,2,18432]{2,1,0:T(2,128)(2,1)}, u32[]{:S(2)}, u32[]{:S(2)}) async-start(bf16[32,2,18432]{2,1,0:T(2,128)(2,1)} %reshape.18), calls=%async_computation | async-start | bytes 4718592 | tf_op jit(solution)/shard_map/all_to_all | solution.py:80
  246.6 61.2 %all-to-all-start.2 = ((bf16[32,2,18432]{2,1,0:T(2,128)(2,1)}), bf16[32,2,18432]{2,1,0:T(2,128)(2,1)S(1)}, u32[]{:S(2)}, u32[]{:S(2)}) async-start(bf16[32,2,18432]{2,1,0:T(2,128)(2,1)} %reshape.20), calls=%async_computation.2 | async-start | bytes 4718592 | tf_op jit(solution)/shard_map/all_to_all | solution.py:81
  307.8 61.0 %all-to-all-start.1 = ((bf16[32,1536,24]{1,2,0:T(8,128)(2,1)}), bf16[32,1536,24]{1,2,0:T(8,128)(2,1)}, u32[]{:S(2)}, u32[]{:S(2)}) async-start(bf16[32,1536,24]{1,2,0:T(8,128)(2,1)} %copy.20), calls=%async_computation.1 | async-start | bytes 4718592 | tf_op jit(solution)/shard_map/all_to_all | solution.py:91
  368.8 60.4 %all-to-all-start.3 = ((bf16[32,1536,24]{1,2,0:T(8,128)(2,1)}), bf16[32,1536,24]{1,2,0:T(8,128)(2,1)S(1)}, u32[]{:S(2)}, u32[]{:S(2)}) async-start(bf16[32,1536,24]{1,2,0:T(8,128)(2,1)} %copy.23), calls=%async_computation.3 | async-start | bytes 4718592 | tf_op jit(solution)/shard_map/all_to_all | solution.py:92
  374.8 21.8 %reduce-scatter.19.cloned.1.call-start = ((), (), s32[]{:S(2)}) async-start(), calls=%async_computation.11 | async-start | bytes 1179648
  379.3 18.6 %copy-start.11 = (bf16[512,384]{1,0:T(8,128)(2,1)S(1)}, bf16[512,384]{1,0:T(8,128)(2,1)}, u32[]{:S(2)}) copy-start(bf16[512,384]{1,0:T(8,128)(2,1)} %copy-done.10) | copy-start | bytes 1179652
  379.3 18.6 %copy-start.13 = (bf16[512,384]{1,0:T(8,128)(2,1)S(1)}, bf16[512,384]{1,0:T(8,128)(2,1)}, u32[]{:S(2)}) copy-start(bf16[512,384]{1,0:T(8,128)(2,1)} %copy-done.12) | copy-start | bytes 1179652
  (15 other events, 38.7 us)
Sparse Core Ops, SparseCore 0:
  25.2 16.3 reduce-scatter.12
  69.5 14.8 reduce-scatter.14
  112.4 14.8 reduce-scatter.16
  381.8 14.8 reduce-scatter.18
where the time goes:
time: 440 us; the launch traced here: 438 us
  waiting for transfers between devices  217 us (49%)
  local copies, waits for them, and re-layouts  82.8 us (19%)
  matrix products  39.3 us (9%)
  other arithmetic  37.2 us (8%)
  starting transfers between devices  35 us (8%)
  between operations  14.1 us (3%)
  blocking collectives  12.4 us (3%)
    unnamed x8, waiting for transfers between devices  61.5 us
    unnamed x73, local copies, waits for them, and re-layouts  56.7 us
    all_to_all x1, waiting for transfers between devices, shards(): lax.all_to_all(mixed_pair[0], 'rep', split_axis=0, concat_axis=2, tiled=T...  40.5 us
    all_to_all x1, waiting for transfers between devices, shards(): lax.all_to_all(updated_out[None], 'rep', split_axis=2, concat_axis=0, til...  37 us
    ppermute x3, waiting for transfers between devices, passed_along(): return lax.ppermute(shard, axis, pairs)  32.5 us
    unnamed x2, other arithmetic  31.3 us
    all_to_all x1, waiting for transfers between devices, shards(): lax.all_to_all(mixed_pair[1], 'rep', split_axis=0, concat_axis=2, tiled=T...  25.2 us
    all_to_all x1, waiting for transfers between devices, shards(): lax.all_to_all(updated_in[None], 'rep', split_axis=2, concat_axis=0, tile...  20.7 us
  transfers between devices with their start and end apart: 11, of which 11 were waited for; matrix products, arithmetic and copies ran while one was open for 19% of the time, Pallas kernels for 0%

commit v1 on v0

v1 whole, which is shorter than its diff:
```python
import jax
import jax.numpy as jnp
from jax import lax
from jax.experimental import pallas as pl
from jax.experimental.pallas import tpu as pltpu
from jax.sharding import PartitionSpec as P

D = 768
FF = 3072
BF = jnp.bfloat16
F32 = jnp.float32

step_size = 4.0
root_half = 0.7071067811865476
inv_root_two_pi = 0.3989422804014327
in_scale = D ** (-0.5)
out_scale = FF ** (-0.5)

CHUNKS = 2
BLOCK = 512
MIB = 1024 * 1024
VMEM = pl.BlockSpec(memory_space=pltpu.VMEM)
HBM = pl.BlockSpec(memory_space=pltpu.HBM)
ANY = pl.BlockSpec(memory_space=pl.ANY)


def params(mib=20):
    return pltpu.CompilerParams(vmem_limit_bytes=mib * MIB)


def cost(flops, nbytes, trans=0):
    return pl.CostEstimate(flops=flops, bytes_accessed=nbytes, transcendentals=trans)


def nt(left, right):
    return lax.dot_general(left, right, (((1,), (1,)), ((), ())), preferred_element_type=F32)


def nn(left, right):
    return lax.dot_general(left, right, (((1,), (0,)), ((), ())), preferred_element_type=F32)


def gelu_parts(preact):
    normal_cdf = 0.5 * (1.0 + lax.erf(preact * root_half))
    density = jnp.exp(-0.5 * preact * preact) * inv_root_two_pi
    return preact * normal_cdf, normal_cdf + preact * density


def blocks(h):
    return [pl.ds(i * BLOCK, BLOCK) for i in range(h // BLOCK)]


def token_slopes_kernel(x_ref, w_ref, s_ref):
    x = x_ref[...]
    for at in blocks(w_ref.shape[0]):
        s_ref[at, :] = gelu_parts(nt(w_ref[at, :], x) * in_scale)[1]


def token_slopes(x_rows, weight_in):
    m, h = x_rows.shape[0], weight_in.shape[0]
    return pl.pallas_call(
        token_slopes_kernel,
        out_shape=jax.ShapeDtypeStruct((h, m), F32),
        in_specs=[VMEM, VMEM],
        out_specs=VMEM,
        compiler_params=params(),
        cost_estimate=cost(2 * m * h * D, 2 * h * D + 4 * m * h, 2 * m * h),
        name="token_slopes",
    )(x_rows, weight_in)


def unit_parts_kernel(w_ref, x_ref, a_ref, s_ref):
    x = x_ref[...]
    for at in blocks(w_ref.shape[0]):
        values, slopes = gelu_parts(nt(w_ref[at, :], x) * in_scale)
        a_ref[at, :] = values.astype(BF)
        s_ref[at, :] = slopes


def unit_parts(weight_in, x_rows):
    m, h = x_rows.shape[0], weight_in.shape[0]
    return pl.pallas_call(
        unit_parts_kernel,
        out_shape=[jax.ShapeDtypeStruct((h, m), BF), jax.ShapeDtypeStruct((h, m), F32)],
        in_specs=[VMEM, VMEM],
        out_specs=[VMEM, VMEM],
        compiler_params=params(),
        cost_estimate=cost(2 * m * h * D, 2 * h * D + 6 * m * h, 2 * m * h),
        name="unit_parts",
    )(weight_in, x_rows)


def turn_kernel(row0, c_ref, wo0_ref, wo1_ref, wi0_ref, wi1_ref, s0_ref, s1_ref, after_ref, o_ref):
    m = c_ref.shape[0]
    cot_t = jnp.transpose(c_ref[...])
    total = c_ref[...].astype(F32)
    branch = None
    for wo_ref, wi_ref, s_ref in ((wo0_ref, wi0_ref, s0_ref), (wo1_ref, wi1_ref, s1_ref)):
        acc = None
        for at in blocks(wo_ref.shape[0]):
            backward = nn(wo_ref[at, :], cot_t) * out_scale
            delta = jnp.transpose(s_ref[at, pl.ds(row0, m)] * backward).astype(BF)
            part = nn(delta, wi_ref[at, :])
            acc = part if acc is None else acc + part
        partial = (acc * in_scale).astype(BF).astype(F32)
        branch = partial if branch is None else branch + partial
    o_ref[...] = (total + branch).astype(BF)


def turn(cot, wouts, wins, slopes, row0, after):
    m = cot.shape[0]
    h = wouts[0].shape[0]
    return pl.pallas_call(
        lambda *refs: turn_kernel(row0, *refs),
        out_shape=jax.ShapeDtypeStruct((m, D), BF),
        in_specs=[VMEM] * 7 + [ANY],
        out_specs=VMEM,
        compiler_params=params(),
        cost_estimate=cost(8 * m * h * D, 8 * h * D + 8 * m * h),
        name="turn",
    )(cot, wouts[0], wouts[1], wins[0], wins[1], slopes[0], slopes[1], after)


def copies_out(scratch, o_ref, sems, i):
    at = pl.ds(i * BLOCK, BLOCK)
    return pltpu.make_async_copy(scratch.at[at, :], o_ref.at[at, :], sems.at[i])


def update_out_kernel(a_ref, c_ref, w_ref, o_ref, scratch, sems):
    cot = c_ref[...]
    parts = blocks(a_ref.shape[0])
    for i, at in enumerate(parts):
        grad = nn(a_ref[at, :], cot) * out_scale
        scratch[at, :] = (w_ref[at, :].astype(F32) - step_size * grad).astype(BF)
        copies_out(scratch, o_ref, sems, i).start()
    for i in range(len(parts)):
        copies_out(scratch, o_ref, sems, i).wait()


def update_out(act_t, cot, weight_out):
    h, m = act_t.shape
    return pl.pallas_call(
        update_out_kernel,
        out_shape=pltpu.HBM((h, D), BF),
        in_specs=[VMEM] * 3,
        out_specs=HBM,
        scratch_shapes=[pltpu.VMEM((h, D), BF), pltpu.SemaphoreType.DMA((h // BLOCK,))],
        compiler_params=params(),
        cost_estimate=cost(2 * m * h * D, 2 * m * h + 4 * h * D),
        name="update_out",
    )(act_t, cot, weight_out)


def update_in_kernel(s_ref, c_ref, x_ref, wo_ref, wi_ref, after_ref, o_ref, scratch, sems):
    cot, x = c_ref[...], x_ref[...]
    parts = blocks(s_ref.shape[0])
    for i, at in enumerate(parts):
        backward = nt(wo_ref[at, :], cot) * out_scale
        delta = (s_ref[at, :] * backward).astype(BF)
        grad = nn(delta, x) * in_scale
        scratch[at, :] = (wi_ref[at, :].astype(F32) - step_size * grad).astype(BF)
        copies_out(scratch, o_ref, sems, i).start()
    for i in range(len(parts)):
        copies_out(scratch, o_ref, sems, i).wait()


def update_in(slopes_t, cot, x_rows, weight_out, weight_in, after):
    h, m = slopes_t.shape
    return pl.pallas_call(
        update_in_kernel,
        out_shape=pltpu.HBM((h, D), BF),
        in_specs=[VMEM] * 5 + [ANY],
        out_specs=HBM,
        scratch_shapes=[pltpu.VMEM((h, D), BF), pltpu.SemaphoreType.DMA((h // BLOCK,))],
        compiler_params=params(),
        cost_estimate=cost(4 * m * h * D, 4 * m * h + 6 * h * D),
        name="update_in",
    )(slopes_t, cot, x_rows, weight_out, weight_in, after)


def mix_kernel(hi_ref, lo_ref, u_ref, o_ref):
    replicas, rows, width = u_ref.shape
    u = u_ref[...].reshape(replicas * rows, width)
    mixed = nn(hi_ref[...], u) + nn(lo_ref[...], u)
    o_ref[...] = mixed.astype(BF).reshape(replicas, rows, width)


def mix(hi, lo, pieces):
    replicas, rows, width = pieces.shape
    block = 16
    n = hi.shape[0]
    matrix = pl.BlockSpec((n, n), lambda i: (0, 0))
    piece = pl.BlockSpec((replicas, block, width), lambda i: (0, i, 0))
    return pl.pallas_call(
        mix_kernel,
        grid=(rows // block,),
        out_shape=pltpu.HBM(pieces.shape, BF),
        in_specs=[matrix, matrix, piece],
        out_specs=piece,
        compiler_params=params(),
        cost_estimate=cost(4 * n * n * width * rows // block, 4 * pieces.size + 4 * n * n),
        name="mix",
    )(hi, lo, pieces)


def spread_kernel(m_ref, hi_ref, lo_ref):
    n, replicas = hi_ref.shape[0], m_ref.shape[0]
    narrow = n // replicas

    def chosen(shape, along):
        group = lax.broadcasted_iota(jnp.int32, shape, along) // narrow
        return jnp.where(lax.broadcasted_iota(jnp.int32, shape, 1 - along) == group, 1.0, 0.0).astype(BF)

    rows, columns = chosen((n, replicas), 0), chosen((replicas, n), 1)
    same = lax.broadcasted_iota(jnp.int32, (n, n), 0) % narrow == lax.broadcasted_iota(jnp.int32, (n, n), 1) % narrow
    left = m_ref[...]
    for ref in (hi_ref, lo_ref):
        part = left.astype(BF)
        left = left - part.astype(F32)
        ref[...] = jnp.where(same, nn(nn(rows, part).astype(BF), columns), 0.0).astype(BF)


def spread_matrix(matrix):
    n = 16 * matrix.shape[0]
    return pl.pallas_call(
        spread_kernel,
        out_shape=[jax.ShapeDtypeStruct((n, n), BF)] * 2,
        in_specs=[VMEM],
        out_specs=[VMEM, VMEM],
        compiler_params=params(),
        cost_estimate=cost(2 * n * n * matrix.shape[0], 4 * n * n),
        name="spread",
    )(matrix)


def landed_kernel(u_ref, o_ref):
    o_ref[...] = u_ref[...]


def landed(array):
    h = array.shape[0]
    rows = pl.BlockSpec((h // 4, D), lambda i: (i, 0))
    return pl.pallas_call(
        landed_kernel,
        grid=(4,),
        out_shape=pltpu.HBM(array.shape, BF),
        in_specs=[rows],
        out_specs=rows,
        compiler_params=params(),
        cost_estimate=cost(0, 4 * h * D),
        name="landed",
    )(array)


def passed_along(shard):
    length = lax.axis_size("section")
    return lax.ppermute(shard, "section", [(i, i - 1) for i in range(1, length)])


def other_core(shard):
    return lax.ppermute(shard, "tp", [(0, 1), (1, 0)])


def sent_out(block):
    return lax.all_to_all(block, "rep", split_axis=0, concat_axis=0, tiled=True)


def shards(inputs, loss_grad, w_in, w_out, mixing):
    segments = lax.axis_size("section")
    segment_index = lax.axis_index("section")
    core = lax.axis_index("tp")
    replicas = lax.axis_size("rep")
    weight_in = w_in[0, 0]
    weight_out = w_out[0, 0]
    units = weight_in.shape[0]
    tokens = loss_grad.shape[0]
    own = tokens // 2

    other_in = other_core(weight_in)
    other_out = other_core(weight_out)
    x_rows = lax.all_gather(inputs[0], "tp", axis=1, tiled=True)
    x_own = lax.dynamic_slice_in_dim(x_rows, core * own, own, 0)
    cot = lax.dynamic_slice_in_dim(lax.all_gather(loss_grad, "tp", axis=1, tiled=True), core * own, own, 0)
    cot = jnp.where(segment_index == segments - 1, cot, jnp.zeros_like(cot))
    slopes = (token_slopes(x_own, weight_in), token_slopes(x_own, other_in))
    wouts, wins = (weight_out, other_out), (weight_in, other_in)

    act_t, slopes_t = unit_parts(weight_in, x_rows)
    hi, lo = spread_matrix(mixing)

    rows = own // CHUNKS
    cots = [cot[c * rows:(c + 1) * rows] for c in range(CHUNKS)]
    kept_cot = []
    kept_result = []
    for turn_index in range(segments - 1):
        results = [turn(cots[c], wouts, wins, slopes, c * rows, mixing) for c in range(CHUNKS)]
        kept_cot.append(cots)
        kept_result.append(results)
        cots = [passed_along(r) for r in results]
    kept_cot.append(cots)

    def summed(kept):
        parts = []
        for c in range(CHUNKS):
            total = kept[0][c]
            for t in range(1, segments):
                total = total + kept[t][c]
            parts.append(total)
        return jnp.concatenate(parts, axis=0)

    cot_rows = lax.all_gather(summed(kept_cot), "tp", axis=0, tiled=True)
    updated_out = update_out(act_t, cot_rows, weight_out)
    pieces_out = sent_out(updated_out.reshape(replicas, units // replicas, D))
    updated_in = update_in(slopes_t, cot_rows, x_rows, weight_out, weight_in, updated_out)
    pieces_in = sent_out(updated_in.reshape(replicas, units // replicas, D))
    kept_result.append([turn(cots[c], wouts, wins, slopes, c * rows, updated_in) for c in range(CHUNKS)])
    back_out = sent_out(mix(hi, lo, pieces_out))
    back_in = sent_out(mix(hi, lo, pieces_in))
    mixed_out = landed(back_out.reshape(units, D))[None, None]
    mixed_in = back_in.reshape(1, 1, units, D)

    result = summed(kept_result)
    width = D // 2
    mine = lax.dynamic_slice_in_dim(result, core * width, width, 1)
    theirs = other_core(lax.dynamic_slice_in_dim(result, (1 - core) * width, width, 1))
    dx = jnp.where(core == 0, jnp.concatenate([mine, theirs], axis=0), jnp.concatenate([theirs, mine], axis=0))
    return dx[None], mixed_in, mixed_out


def solution(mesh):
    in_specs = (
        P("section", "rep", "tp"),
        P("rep", "tp"),
        P("rep", "section", "tp", None),
        P("rep", "section", "tp", None),
        P(),
    )
    out_specs = (
        P("section", "rep", "tp"),
        P("rep", "section", "tp", None),
        P("rep", "section", "tp", None),
    )
    return jax.shard_map(shards, mesh=mesh, in_specs=in_specs, out_specs=out_specs, check_vma=False)
```

time: 440 us -> 332 us (0.75)
  waiting for transfers between devices: 217 us -> 133 us
  Pallas kernels: 0 us -> 67.5 us
  blocking collectives: 12.4 us -> 77.8 us
  local copies, waits for them, and re-layouts: 82.8 us -> 18.1 us
  matrix products: 39.3 us -> 0 us
  other arithmetic: 37.2 us -> 1.18 us
  between operations: 14.1 us -> 1.13 us
    all_to_all x0 -> x1, blocking collectives: none -> 67.7 us  [sent_out(): return lax.all_to_all(block, 'rep', split_axis=0, concat_axis=0, tiled=True)]
    pallas_call x0 -> x17, Pallas kernels: none -> 67.5 us  [the longest x8 40.8 us: turn(): pl.pallas_call(lambda *refs: turn_kernel(row0, *refs), out_shape=jax.Shap...]
    unnamed x8 -> x0, waiting for transfers between devices: 61.5 us -> none
    dot_general x13 -> x0, matrix products: 39.3 us -> none  [the longest x5 16.9 us: contract_last(): lax.dot_general(left, right, (((1,), (1,)), ((), ())), preferred_element_...]
    unnamed x73 -> x43, local copies, waits for them, and re-layouts: 56.7 us -> 18.1 us
    unnamed x2 -> x0, other arithmetic: 31.3 us -> none
    ppermute x3 -> x9, waiting for transfers between devices: 32.5 us -> 5.3 us  [the longest x6 3.87 us: passed_along(): lax.ppermute(shard, 'section', [(i, i - 1) for i in range(1, length)])]
    broadcast_in_dim x2 -> x0, local copies, waits for them, and re-layouts: 20.7 us -> none  [the longest x1 12.1 us: shards(): updated_out[None]]
  transfers between devices with their start and end apart: 11 -> 12, of which waited for: 11 -> 5; matrix products, arithmetic and copies ran while one was open for 19% -> 0% of each run, Pallas kernels for 0% -> 16%
where the time goes in v1:
time: 332 us; the launch traced here: 331 us
  waiting for transfers between devices  133 us (40%)
  blocking collectives  77.8 us (23%)
  Pallas kernels  67.5 us (20%)
  starting transfers between devices  31.5 us (9%)
  local copies, waits for them, and re-layouts  18.1 us (5%)
    all_to_all x3, waiting for transfers between devices, sent_out(): return lax.all_to_all(block, 'rep', split_axis=0, concat_axis=0, tiled=True)  128 us
    all_to_all x1, blocking collectives, sent_out(): return lax.all_to_all(block, 'rep', split_axis=0, concat_axis=0, tiled=True)  67.7 us
    pallas_call x8, Pallas kernels, turn(): pl.pallas_call(lambda *refs: turn_kernel(row0, *refs), out_shape=jax.Shap...  40.8 us
    unnamed x43, local copies, waits for them, and re-layouts  18.1 us
    all_to_all x3, starting transfers between devices, sent_out(): return lax.all_to_all(block, 'rep', split_axis=0, concat_axis=0, tiled=True)  16.5 us
    ppermute x6, starting transfers between devices, passed_along(): lax.ppermute(shard, 'section', [(i, i - 1) for i in range(1, length)])  14.3 us
    pallas_call x2, Pallas kernels, mix(): pl.pallas_call(mix_kernel, grid=(rows // block,), out_shape=pltpu.HBM(pie...  9.47 us
  transfers between devices with their start and end apart: 12, of which 5 were waited for; matrix products, arithmetic and copies ran while one was open for 0% of the time, Pallas kernels for 16%

profile of v1, /device:TPU:16, one launch (start us, length us, event | category | flops | bytes accessed | tf_op | source)
XLA Modules:
  0.0 330.6 jit_solution(13872904018420704193)
XLA Ops:
  1.2 5.4 %all-gather = bf16[1,512,768]{2,1,0:T(8,128)(2,1)S(1)} all-gather(bf16[1,512,384]{2,1,0:T(8,128)(2,1)} %param.5), channel_id=2, replica_groups=mesh['rep'=32,'section'=4,'tp'=2] {'tp'}, dimensions={2}, use_global_device_ids=true | all-gather | bytes 1179648 | tf_op jit(solution)/shard_map/all_gather | solution.py:281
  12.0 3.0 token_slopes.3.refs_6_
  15.0 5.6 %turn.11 = bf16[128,768]{1,0:T(8,128)(2,1)S(1)} custom-call(bf16[128,768]{1,0:T(8,128)(2,1)S(1)} %get-tuple-element.15.refs_0_, bf16[1536,768]{1,0:T(8,128)(2,1)S(1)} %bitcast.14, bf16[1536,768]{1,0:T(8,128)(2,1)} %collective-permute-done.refs_2_, bf16[1536,768]{1,0:T(8,128)(2,1)S(1)} %bitcast.26, bf16[1536,768]{1,0:T(8,128)(2,1)} %collective-permute-done.1.w_ref.refs_4_, ...), custom_call_target="tpu_custom_call" | custom-call | flops 1207959552 | bytes 11010048 | tf_op jit(solution)/shard_map/turn/pallas_call | solution.py:113
  23.0 5.0 %turn.8 = bf16[128,768]{1,0:T(8,128)(2,1)S(1)} custom-call(bf16[128,768]{1,0:T(8,128)(2,1)S(1)} %get-tuple-element.16.refs_0_, bf16[1536,768]{1,0:T(8,128)(2,1)S(1)} %bitcast.15, bf16[1536,768]{1,0:T(8,128)(2,1)} %collective-permute-done.refs_2_, bf16[1536,768]{1,0:T(8,128)(2,1)S(1)} %bitcast.27, bf16[1536,768]{1,0:T(8,128)(2,1)} %collective-permute-done.1.w_ref.refs_4_, ...), custom_call_target="tpu_custom_call" | custom-call | flops 1207959552 | bytes 11010048 | tf_op jit(solution)/shard_map/turn/pallas_call | solution.py:113
  28.0 4.1 %collective-permute-start.2 = (bf16[128,768]{1,0:T(8,128)(2,1)S(1)}, bf16[128,768]{1,0:T(8,128)(2,1)S(1)}, u32[]{:S(2)}, u32[]{:S(2)}) collective-permute-start(bf16[128,768]{1,0:T(8,128)(2,1)S(1)} %turn.8), channel_id=1, source_target_pairs={{2,0},{4,2},{6,4},{3,1},{5,3},{7,5},{10,8},{12,10},{14,12},{11,9},... | collective-permute-start | bytes 589832 | tf_op jit(solution)/shard_map/ppermute | solution.py:257
  32.1 5.0 %turn.12 = bf16[128,768]{1,0:T(8,128)(2,1)S(1)} custom-call(bf16[128,768]{1,0:T(8,128)(2,1)S(1)} %collective-permute-done.5.refs_0_, bf16[1536,768]{1,0:T(8,128)(2,1)S(1)} %bitcast.16, bf16[1536,768]{1,0:T(8,128)(2,1)} %collective-permute-done.refs_2_, bf16[1536,768]{1,0:T(8,128)(2,1)S(1)} %bitcast.28, ...), custom_call_target="tpu_custom_call" | custom-call | flops 1207959552 | bytes 11010048 | tf_op jit(solution)/shard_map/turn/pallas_call | solution.py:113
  39.1 5.0 %turn.9 = bf16[128,768]{1,0:T(8,128)(2,1)S(1)} custom-call(bf16[128,768]{1,0:T(8,128)(2,1)S(1)} %collective-permute-done.2.refs_0_, bf16[1536,768]{1,0:T(8,128)(2,1)S(1)} %bitcast.17, bf16[1536,768]{1,0:T(8,128)(2,1)} %collective-permute-done.refs_2_, bf16[1536,768]{1,0:T(8,128)(2,1)S(1)} %bitcast.29, ...), custom_call_target="tpu_custom_call" | custom-call | flops 1207959552 | bytes 11010048 | tf_op jit(solution)/shard_map/turn/pallas_call | solution.py:113
  46.2 5.0 %turn.13 = bf16[128,768]{1,0:T(8,128)(2,1)S(1)} custom-call(bf16[128,768]{1,0:T(8,128)(2,1)S(1)} %collective-permute-done.6.refs_0_, bf16[1536,768]{1,0:T(8,128)(2,1)S(1)} %bitcast.18, bf16[1536,768]{1,0:T(8,128)(2,1)} %collective-permute-done.refs_2_, bf16[1536,768]{1,0:T(8,128)(2,1)S(1)} %bitcast.30, ...), custom_call_target="tpu_custom_call" | custom-call | flops 1207959552 | bytes 11010048 | tf_op jit(solution)/shard_map/turn/pallas_call | solution.py:113
  53.3 5.0 %turn.10 = bf16[128,768]{1,0:T(8,128)(2,1)S(1)} custom-call(bf16[128,768]{1,0:T(8,128)(2,1)S(1)} %collective-permute-done.3.refs_0_, bf16[1536,768]{1,0:T(8,128)(2,1)S(1)} %bitcast.19, bf16[1536,768]{1,0:T(8,128)(2,1)} %collective-permute-done.refs_2_, bf16[1536,768]{1,0:T(8,128)(2,1)S(1)} %bitcast.31, ...), custom_call_target="tpu_custom_call" | custom-call | flops 1207959552 | bytes 11010048 | tf_op jit(solution)/shard_map/turn/pallas_call | solution.py:113
  62.7 3.9 %collective-permute-done.4.refs_0_ = bf16[128,768]{1,0:T(8,128)(2,1)S(1)} collective-permute-done((bf16[128,768]{1,0:T(8,128)(2,1)S(1)}, bf16[128,768]{1,0:T(8,128)(2,1)S(1)}, u32[]{:S(2)}, u32[]{:S(2)}) %collective-permute-start.4) | collective-permute-done | bytes 196640 | tf_op jit(solution)/shard_map/ppermute | solution.py:257
  73.2 3.7 %update_in.1.refs_7_ = bf16[1536,768]{1,0:T(8,128)(2,1)} custom-call(f32[1536,512]{1,0:T(8,128)S(1)} %get-tuple-element.7.s_ref, bf16[512,768]{1,0:T(8,128)(2,1)S(1)} %all_gather.11.c_ref, bf16[512,768]{1,0:T(8,128)(2,1)S(1)} %bitcast.39, bf16[1536,768]{1,0:T(8,128)(2,1)S(1)} %bitcast.21, bf16[1536,768]{1,0:T(8,128)(2,1)S(1)} %bitcast.33, ...), custom_call_target="tpu_custom_call" | custom-call | flops 2415919104 | bytes 10223616 | tf_op jit(solution)/shard_map/update_in/pallas_call | solution.py:169
  76.9 67.7 %all_to_all.20.u_ref = bf16[32,48,768]{2,1,0:T(8,128)(2,1)} all-to-all(bf16[32,48,768]{2,1,0:T(8,128)(2,1)} %bitcast.36), channel_id=1, replica_groups=mesh['rep'=32,'section'=4,'tp'=2] {'rep'}, dimensions={0} | all-to-all | bytes 4718592 | tf_op jit(solution)/shard_map/all_to_all | solution.py:265
  144.6 4.8 %all-to-all-start.2 = ((bf16[32,48,768]{2,1,0:T(8,128)(2,1)}), bf16[32,48,768]{2,1,0:T(8,128)(2,1)}, u32[]{:S(2)}, u32[]{:S(2)}) async-start(bf16[32,48,768]{2,1,0:T(8,128)(2,1)} %bitcast.37), calls=%async_computation.2 | async-start | bytes 4718592 | tf_op jit(solution)/shard_map/all_to_all | solution.py:265
  151.7 4.1 %mix.2 = bf16[32,48,768]{2,1,0:T(8,128)(2,1)} custom-call(bf16[512,512]{1,0:T(8,128)(2,1)S(1)} %get-tuple-element.9.hi_ref, bf16[512,512]{1,0:T(8,128)(2,1)S(1)} %get-tuple-element.10.lo_ref, bf16[32,48,768]{2,1,0:T(8,128)(2,1)S(1)} %copy-done.10), custom_call_target="tpu_custom_call" | custom-call | flops 2415919104 | bytes 5767168 | tf_op jit(solution)/shard_map/mix/pallas_call | solution.py:194
  157.4 47.3 %all-to-all-done.2.u_ref = bf16[32,48,768]{2,1,0:T(8,128)(2,1)} async-done(((bf16[32,48,768]{2,1,0:T(8,128)(2,1)}), bf16[32,48,768]{2,1,0:T(8,128)(2,1)}, u32[]{:S(2)}, u32[]{:S(2)}) %all-to-all-start.2) | async-done | bytes 2359328 | tf_op jit(solution)/shard_map/all_to_all | solution.py:265
  204.7 5.6 %all-to-all-start.1 = ((bf16[32,48,768]{2,1,0:T(8,128)(2,1)}), bf16[32,48,768]{2,1,0:T(8,128)(2,1)}, u32[]{:S(2)}, u32[]{:S(2)}) async-start(bf16[32,48,768]{2,1,0:T(8,128)(2,1)} %mix.2), calls=%async_computation.1 | async-start | bytes 4718592 | tf_op jit(solution)/shard_map/all_to_all | solution.py:265
  212.4 5.4 %mix.3 = bf16[32,48,768]{2,1,0:T(8,128)(2,1)} custom-call(bf16[512,512]{1,0:T(8,128)(2,1)S(1)} %copy-done.17, bf16[512,512]{1,0:T(8,128)(2,1)S(1)} %copy-done.19, bf16[32,48,768]{2,1,0:T(8,128)(2,1)} %all-to-all-done.2.u_ref), custom_call_target="tpu_custom_call" | custom-call | flops 2415919104 | bytes 5767168 | tf_op jit(solution)/shard_map/mix/pallas_call | solution.py:194
  217.8 46.5 %all-to-all-done.1 = bf16[32,48,768]{2,1,0:T(8,128)(2,1)} async-done(((bf16[32,48,768]{2,1,0:T(8,128)(2,1)}), bf16[32,48,768]{2,1,0:T(8,128)(2,1)}, u32[]{:S(2)}, u32[]{:S(2)}) %all-to-all-start.1) | async-done | bytes 2359328 | tf_op jit(solution)/shard_map/all_to_all | solution.py:265
  264.3 6.1 %all-to-all-start.3 = ((bf16[32,48,768]{2,1,0:T(8,128)(2,1)}), bf16[32,48,768]{2,1,0:T(8,128)(2,1)}, u32[]{:S(2)}, u32[]{:S(2)}) async-start(bf16[32,48,768]{2,1,0:T(8,128)(2,1)} %mix.3), calls=%async_computation.3 | async-start | bytes 4718592 | tf_op jit(solution)/shard_map/all_to_all | solution.py:265
  276.6 5.0 %turn.15 = bf16[128,768]{1,0:T(8,128)(2,1)S(1)} custom-call(bf16[128,768]{1,0:T(8,128)(2,1)S(1)} %collective-permute-done.7.refs_0_, bf16[1536,768]{1,0:T(8,128)(2,1)S(1)} %bitcast.22, bf16[1536,768]{1,0:T(8,128)(2,1)} %collective-permute-done.refs_2_, bf16[1536,768]{1,0:T(8,128)(2,1)S(1)} %bitcast.34, ...), custom_call_target="tpu_custom_call" | custom-call | flops 1207959552 | bytes 11010048 | tf_op jit(solution)/shard_map/turn/pallas_call | solution.py:113
  281.7 5.1 %turn.14 = bf16[128,768]{1,0:T(8,128)(2,1)S(1)} custom-call(bf16[128,768]{1,0:T(8,128)(2,1)S(1)} %collective-permute-done.4.refs_0_, bf16[1536,768]{1,0:T(8,128)(2,1)S(1)} %bitcast.23, bf16[1536,768]{1,0:T(8,128)(2,1)} %collective-permute-done.refs_2_, bf16[1536,768]{1,0:T(8,128)(2,1)S(1)} %bitcast.35, ...), custom_call_target="tpu_custom_call" | custom-call | flops 1207959552 | bytes 11010048 | tf_op jit(solution)/shard_map/turn/pallas_call | solution.py:113
  289.4 34.1 %all-to-all-done.3 = bf16[32,48,768]{2,1,0:T(8,128)(2,1)} async-done(((bf16[32,48,768]{2,1,0:T(8,128)(2,1)}), bf16[32,48,768]{2,1,0:T(8,128)(2,1)}, u32[]{:S(2)}, u32[]{:S(2)}) %all-to-all-start.3) | async-done | bytes 2359328 | tf_op jit(solution)/shard_map/all_to_all | solution.py:265
  323.5 3.9 %landed.1 = bf16[1536,768]{1,0:T(8,128)(2,1)} custom-call(bf16[1536,768]{1,0:T(8,128)(2,1)} %bitcast.9.u_ref), custom_call_target="tpu_custom_call" | custom-call | bytes 4718592 | tf_op jit(solution)/shard_map/landed/pallas_call | solution.py:243
  327.4 3.2 copy.9
  (72 shorter events, 39.9 us)
Async XLA Ops:
  0.6 11.4 %collective-permute-start.1 = (bf16[1536,768]{1,0:T(8,128)(2,1)}, bf16[1536,768]{1,0:T(8,128)(2,1)}, u32[]{:S(2)}, u32[]{:S(2)}) collective-permute-start(bf16[1536,768]{1,0:T(8,128)(2,1)} %bitcast.24), channel_id=1, source_target_pairs={{0,1},{1,0},{2,3},{3,2},{4,5},{5,4},{6,7},{7,6},{8,9},{9,8},{10,11... | collective-permute-start | bytes 7077896 | tf_op jit(solution)/shard_map/ppermute | solution.py:261
  0.7 14.3 %collective-permute-start = (bf16[1536,768]{1,0:T(8,128)(2,1)}, bf16[1536,768]{1,0:T(8,128)(2,1)}, u32[]{:S(2)}, u32[]{:S(2)}) collective-permute-start(bf16[1536,768]{1,0:T(8,128)(2,1)} %bitcast.13), channel_id=1, source_target_pairs={{0,1},{1,0},{2,3},{3,2},{4,5},{5,4},{6,7},{7,6},{8,9},{9,8},{10,11... | collective-permute-start | bytes 7077896 | tf_op jit(solution)/shard_map/ppermute | solution.py:261
  6.6 1.7 copy-start.1
  9.5 43.8 %copy-start.4 = (f32[1536,256]{1,0:T(8,128)}, f32[1536,256]{1,0:T(8,128)S(1)}, u32[]{:S(2)}) copy-start(f32[1536,256]{1,0:T(8,128)S(1)} %token_slopes.2.refs_5_) | copy-start | bytes 4718596
  11.9 3.1 copy-start.2
  12.0 3.1 copy-start
  12.0 3.0 copy-start.15
  15.0 38.3 %copy-start.6 = (f32[1536,256]{1,0:T(8,128)}, f32[1536,256]{1,0:T(8,128)S(1)}, u32[]{:S(2)}) copy-start(f32[1536,256]{1,0:T(8,128)S(1)} %token_slopes.3.refs_6_) | copy-start | bytes 4718596
  20.6 11.5 %collective-permute-start.5 = (bf16[128,768]{1,0:T(8,128)(2,1)S(1)}, bf16[128,768]{1,0:T(8,128)(2,1)S(1)}, u32[]{:S(2)}, u32[]{:S(2)}) collective-permute-start(bf16[128,768]{1,0:T(8,128)(2,1)S(1)} %turn.11), channel_id=1, source_target_pairs={{2,0},{4,2},{6,4},{3,1},{5,3},{7,5},{10,8},{12,10},{14,12},{11,9},... | collective-permute-start | bytes 589832 | tf_op jit(solution)/shard_map/ppermute | solution.py:257
  28.0 11.1 %collective-permute-start.2 = (bf16[128,768]{1,0:T(8,128)(2,1)S(1)}, bf16[128,768]{1,0:T(8,128)(2,1)S(1)}, u32[]{:S(2)}, u32[]{:S(2)}) collective-permute-start(bf16[128,768]{1,0:T(8,128)(2,1)S(1)} %turn.8), channel_id=1, source_target_pairs={{2,0},{4,2},{6,4},{3,1},{5,3},{7,5},{10,8},{12,10},{14,12},{11,9},... | collective-permute-start | bytes 589832 | tf_op jit(solution)/shard_map/ppermute | solution.py:257
  37.1 9.1 %collective-permute-start.6 = (bf16[128,768]{1,0:T(8,128)(2,1)S(1)}, bf16[128,768]{1,0:T(8,128)(2,1)S(1)}, u32[]{:S(2)}, u32[]{:S(2)}) collective-permute-start(bf16[128,768]{1,0:T(8,128)(2,1)S(1)} %turn.12), channel_id=1, source_target_pairs={{2,0},{4,2},{6,4},{3,1},{5,3},{7,5},{10,8},{12,10},{14,12},{11,9},... | collective-permute-start | bytes 589832 | tf_op jit(solution)/shard_map/ppermute | solution.py:257
  44.1 9.1 %collective-permute-start.3 = (bf16[128,768]{1,0:T(8,128)(2,1)S(1)}, bf16[128,768]{1,0:T(8,128)(2,1)S(1)}, u32[]{:S(2)}, u32[]{:S(2)}) collective-permute-start(bf16[128,768]{1,0:T(8,128)(2,1)S(1)} %turn.9), channel_id=1, source_target_pairs={{2,0},{4,2},{6,4},{3,1},{5,3},{7,5},{10,8},{12,10},{14,12},{11,9},... | collective-permute-start | bytes 589832 | tf_op jit(solution)/shard_map/ppermute | solution.py:257
  51.3 7.0 %copy-start.11 = (bf16[128,768]{1,0:T(8,128)(2,1)}, bf16[128,768]{1,0:T(8,128)(2,1)S(1)}, u32[]{:S(2)}) copy-start(bf16[128,768]{1,0:T(8,128)(2,1)S(1)} %turn.13) | copy-start | bytes 589828
  51.3 11.4 %collective-permute-start.7 = (bf16[128,768]{1,0:T(8,128)(2,1)S(1)}, bf16[128,768]{1,0:T(8,128)(2,1)S(1)}, u32[]{:S(2)}, u32[]{:S(2)}) collective-permute-start(bf16[128,768]{1,0:T(8,128)(2,1)S(1)} %turn.13), channel_id=1, source_target_pairs={{2,0},{4,2},{6,4},{3,1},{5,3},{7,5},{10,8},{12,10},{14,12},{11,9},... | collective-permute-start | bytes 589832 | tf_op jit(solution)/shard_map/ppermute | solution.py:257
  58.3 8.4 %copy-start.13 = (bf16[128,768]{1,0:T(8,128)(2,1)}, bf16[128,768]{1,0:T(8,128)(2,1)S(1)}, u32[]{:S(2)}) copy-start(bf16[128,768]{1,0:T(8,128)(2,1)S(1)} %turn.10) | copy-start | bytes 589828
  58.3 8.3 %collective-permute-start.4 = (bf16[128,768]{1,0:T(8,128)(2,1)S(1)}, bf16[128,768]{1,0:T(8,128)(2,1)S(1)}, u32[]{:S(2)}, u32[]{:S(2)}) collective-permute-start(bf16[128,768]{1,0:T(8,128)(2,1)S(1)} %turn.10), channel_id=1, source_target_pairs={{2,0},{4,2},{6,4},{3,1},{5,3},{7,5},{10,8},{12,10},{14,12},{11,9},... | collective-permute-start | bytes 589832 | tf_op jit(solution)/shard_map/ppermute | solution.py:257
  71.5 1.7 copy-start.9
  144.6 60.2 %all-to-all-start.2 = ((bf16[32,48,768]{2,1,0:T(8,128)(2,1)}), bf16[32,48,768]{2,1,0:T(8,128)(2,1)}, u32[]{:S(2)}, u32[]{:S(2)}) async-start(bf16[32,48,768]{2,1,0:T(8,128)(2,1)} %bitcast.37), calls=%async_computation.2 | async-start | bytes 4718592 | tf_op jit(solution)/shard_map/all_to_all | solution.py:265
  204.7 59.6 %all-to-all-start.1 = ((bf16[32,48,768]{2,1,0:T(8,128)(2,1)}), bf16[32,48,768]{2,1,0:T(8,128)(2,1)}, u32[]{:S(2)}, u32[]{:S(2)}) async-start(bf16[32,48,768]{2,1,0:T(8,128)(2,1)} %mix.2), calls=%async_computation.1 | async-start | bytes 4718592 | tf_op jit(solution)/shard_map/all_to_all | solution.py:265
  264.3 59.2 %all-to-all-start.3 = ((bf16[32,48,768]{2,1,0:T(8,128)(2,1)}), bf16[32,48,768]{2,1,0:T(8,128)(2,1)}, u32[]{:S(2)}, u32[]{:S(2)}) async-start(bf16[32,48,768]{2,1,0:T(8,128)(2,1)} %mix.3), calls=%async_computation.3 | async-start | bytes 4718592 | tf_op jit(solution)/shard_map/all_to_all | solution.py:265
  270.5 1.7 copy-start.3
  281.7 5.1 %copy-start.12 = (bf16[128,768]{1,0:T(8,128)(2,1)S(1)}, bf16[128,768]{1,0:T(8,128)(2,1)}, u32[]{:S(2)}) copy-start(bf16[128,768]{1,0:T(8,128)(2,1)} %copy-done.11) | copy-start | bytes 589828
  281.7 5.1 %copy-start.14 = (bf16[128,768]{1,0:T(8,128)(2,1)S(1)}, bf16[128,768]{1,0:T(8,128)(2,1)}, u32[]{:S(2)}) copy-start(bf16[128,768]{1,0:T(8,128)(2,1)} %copy-done.13) | copy-start | bytes 589828
  287.0 1.5 collective-permute-start.8
  (9 other events, 11.0 us)

commit v2 on v1

--- a/solution.py
+++ b/solution.py
@@ -22,6 +22,7 @@
 VMEM = pl.BlockSpec(memory_space=pltpu.VMEM)
 HBM = pl.BlockSpec(memory_space=pltpu.HBM)
 ANY = pl.BlockSpec(memory_space=pl.ANY)
+SMEM = pl.BlockSpec(memory_space=pltpu.SMEM)
 
 
 def params(mib=20):
@@ -50,23 +51,74 @@
     return [pl.ds(i * BLOCK, BLOCK) for i in range(h // BLOCK)]
 
 
-def token_slopes_kernel(x_ref, w_ref, s_ref):
+def joined(core, mine, theirs):
+    return jnp.where(core == 0, jnp.concatenate([mine, theirs], axis=1), jnp.concatenate([theirs, mine], axis=1))
+
+
+def entering_kernel(at, x_ref, other_x_ref, dy_ref, other_dy_ref, whole_ref, own_ref, *outs):
+    core = at[0]
+    own, m = own_ref.shape[0], outs[0].shape[1]
+    whole_ref[...] = joined(core, x_ref[...], other_x_ref[...])
+    start = pl.multiple_of(core * own, own)
+    own_ref[...] = whole_ref[pl.ds(start, own), :]
+    dy = joined(core, dy_ref[pl.ds(start, own), :], other_dy_ref[...])
+    dy = jnp.transpose(jnp.where(at[1] == 1, dy, jnp.zeros_like(dy)))
+    for c, o_ref in enumerate(outs):
+        o_ref[...] = dy[:, c * m : (c + 1) * m]
+
+
+def entering(at, x, other_x, dy, other_dy):
+    own = dy.shape[0] // 2
+    shapes = [(2 * own, D), (own, D)] + [(D, own // CHUNKS)] * CHUNKS
+    return pl.pallas_call(
+        entering_kernel,
+        out_shape=[jax.ShapeDtypeStruct(s, BF) for s in shapes],
+        in_specs=[SMEM] + [VMEM] * 4,
+        out_specs=[VMEM] * len(shapes),
+        compiler_params=params(),
+        cost_estimate=cost(0, 16 * own * D),
+        name="entering",
+    )(at, x, other_x, dy, other_dy)
+
+
+def token_slopes_kernel(x_ref, w_ref, s_ref, t_ref):
     x = x_ref[...]
     for at in blocks(w_ref.shape[0]):
-        s_ref[at, :] = gelu_parts(nt(w_ref[at, :], x) * in_scale)[1]
+        weight = w_ref[at, :]
+        s_ref[at, :] = gelu_parts(nt(weight, x) * in_scale)[1]
+        t_ref[:, at] = jnp.transpose(weight)
 
 
 def token_slopes(x_rows, weight_in):
     m, h = x_rows.shape[0], weight_in.shape[0]
     return pl.pallas_call(
         token_slopes_kernel,
-        out_shape=jax.ShapeDtypeStruct((h, m), F32),
+        out_shape=[jax.ShapeDtypeStruct((h, m), F32), jax.ShapeDtypeStruct((D, h), BF)],
         in_specs=[VMEM, VMEM],
-        out_specs=VMEM,
-        compiler_params=params(),
-        cost_estimate=cost(2 * m * h * D, 2 * h * D + 4 * m * h, 2 * m * h),
+        out_specs=[VMEM, VMEM],
+        compiler_params=params(),
+        cost_estimate=cost(2 * m * h * D, 4 * h * D + 4 * m * h, 2 * m * h),
         name="token_slopes",
     )(x_rows, weight_in)
+
+
+def kept_kernel(w_ref, o_ref, sems):
+    copy = pltpu.make_async_copy(w_ref, o_ref, sems.at[0])
+    copy.start()
+    copy.wait()
+
+
+def kept(array):
+    return pl.pallas_call(
+        kept_kernel,
+        out_shape=pltpu.VMEM(array.shape, BF),
+        in_specs=[ANY],
+        out_specs=VMEM,
+        scratch_shapes=[pltpu.SemaphoreType.DMA((1,))],
+        compiler_params=params(),
+        cost_estimate=cost(0, 4 * array.size),
+        name="kept",
+    )(array)
 
 
 def unit_parts_kernel(w_ref, x_ref, a_ref, s_ref):
@@ -90,35 +142,51 @@
     )(weight_in, x_rows)
 
 
-def turn_kernel(row0, c_ref, wo0_ref, wo1_ref, wi0_ref, wi1_ref, s0_ref, s1_ref, after_ref, o_ref):
-    m = c_ref.shape[0]
-    cot_t = jnp.transpose(c_ref[...])
-    total = c_ref[...].astype(F32)
+def turn_kernel(col0, c_ref, wo0_ref, wo1_ref, wt0_ref, wt1_ref, s0_ref, s1_ref, after_ref, o_ref, delta):
+    cot = c_ref[...]
+    m = cot.shape[1]
     branch = None
-    for wo_ref, wi_ref, s_ref in ((wo0_ref, wi0_ref, s0_ref), (wo1_ref, wi1_ref, s1_ref)):
-        acc = None
+    for wo_ref, wt_ref, s_ref in ((wo0_ref, wt0_ref, s0_ref), (wo1_ref, wt1_ref, s1_ref)):
         for at in blocks(wo_ref.shape[0]):
-            backward = nn(wo_ref[at, :], cot_t) * out_scale
-            delta = jnp.transpose(s_ref[at, pl.ds(row0, m)] * backward).astype(BF)
-            part = nn(delta, wi_ref[at, :])
-            acc = part if acc is None else acc + part
-        partial = (acc * in_scale).astype(BF).astype(F32)
+            backward = nn(wo_ref[at, :], cot) * out_scale
+            delta[at, :] = (s_ref[at, pl.ds(col0, m)] * backward).astype(BF)
+        partial = (nn(wt_ref[...], delta[...]) * in_scale).astype(BF).astype(F32)
         branch = partial if branch is None else branch + partial
-    o_ref[...] = (total + branch).astype(BF)
-
-
-def turn(cot, wouts, wins, slopes, row0, after):
-    m = cot.shape[0]
+    o_ref[...] = (cot.astype(F32) + branch).astype(BF)
+
+
+def turn(cot, wouts, wins_t, slopes, col0, after):
+    m = cot.shape[1]
     h = wouts[0].shape[0]
     return pl.pallas_call(
-        lambda *refs: turn_kernel(row0, *refs),
-        out_shape=jax.ShapeDtypeStruct((m, D), BF),
+        lambda *refs: turn_kernel(col0, *refs),
+        out_shape=jax.ShapeDtypeStruct((D, m), BF),
         in_specs=[VMEM] * 7 + [ANY],
         out_specs=VMEM,
+        scratch_shapes=[pltpu.VMEM((h, m), BF)],
         compiler_params=params(),
         cost_estimate=cost(8 * m * h * D, 8 * h * D + 8 * m * h),
         name="turn",
-    )(cot, wouts[0], wouts[1], wins[0], wins[1], slopes[0], slopes[1], after)
+    )(cot, wouts[0], wouts[1], wins_t[0], wins_t[1], slopes[0], slopes[1], after)
+
+
+def leaving_kernel(core, mine_ref, theirs_ref, o_ref):
+    own = mine_ref.shape[1]
+    o_ref[pl.ds(pl.multiple_of(core[0] * own, own), own), :] = jnp.transpose(mine_ref[...])
+    o_ref[pl.ds(pl.multiple_of((1 - core[0]) * own, own), own), :] = jnp.transpose(theirs_ref[...])
+
+
+def leaving(core, mine, theirs):
+    width, own = mine.shape
+    return pl.pallas_call(
+        leaving_kernel,
+        out_shape=jax.ShapeDtypeStruct((2 * own, width), BF),
+        in_specs=[SMEM, VMEM, VMEM],
+        out_specs=VMEM,
+        compiler_params=params(),
+        cost_estimate=cost(0, 8 * own * width),
+        name="leaving",
+    )(core, mine, theirs)
 
 
 def copies_out(scratch, o_ref, sems, i):
@@ -127,7 +195,7 @@
 
 
 def update_out_kernel(a_ref, c_ref, w_ref, o_ref, scratch, sems):
-    cot = c_ref[...]
+    cot = jnp.transpose(c_ref[...])
     parts = blocks(a_ref.shape[0])
     for i, at in enumerate(parts):
         grad = nn(a_ref[at, :], cot) * out_scale
@@ -151,11 +219,11 @@
     )(act_t, cot, weight_out)
 
 
-def update_in_kernel(s_ref, c_ref, x_ref, wo_ref, wi_ref, after_ref, o_ref, scratch, sems):
+def update_in_kernel(s_ref, c_ref, x_ref, wo_ref, wi_ref, o_ref, scratch, sems):
     cot, x = c_ref[...], x_ref[...]
     parts = blocks(s_ref.shape[0])
     for i, at in enumerate(parts):
-        backward = nt(wo_ref[at, :], cot) * out_scale
+        backward = nn(wo_ref[at, :], cot) * out_scale
         delta = (s_ref[at, :] * backward).astype(BF)
         grad = nn(delta, x) * in_scale
         scratch[at, :] = (wi_ref[at, :].astype(F32) - step_size * grad).astype(BF)
@@ -164,28 +232,28 @@
         copies_out(scratch, o_ref, sems, i).wait()
 
 
-def update_in(slopes_t, cot, x_rows, weight_out, weight_in, after):
+def update_in(slopes_t, cot, x_rows, weight_out, weight_in):
     h, m = slopes_t.shape
     return pl.pallas_call(
         update_in_kernel,
         out_shape=pltpu.HBM((h, D), BF),
-        in_specs=[VMEM] * 5 + [ANY],
+        in_specs=[VMEM] * 5,
         out_specs=HBM,
         scratch_shapes=[pltpu.VMEM((h, D), BF), pltpu.SemaphoreType.DMA((h // BLOCK,))],
         compiler_params=params(),
         cost_estimate=cost(4 * m * h * D, 4 * m * h + 6 * h * D),
         name="update_in",
-    )(slopes_t, cot, x_rows, weight_out, weight_in, after)
-
-
-def mix_kernel(hi_ref, lo_ref, u_ref, o_ref):
+    )(slopes_t, cot, x_rows, weight_out, weight_in)
+
+
+def mix_kernel(hi_ref, lo_ref, u_ref, after_ref, o_ref):
     replicas, rows, width = u_ref.shape
     u = u_ref[...].reshape(replicas * rows, width)
     mixed = nn(hi_ref[...], u) + nn(lo_ref[...], u)
     o_ref[...] = mixed.astype(BF).reshape(replicas, rows, width)
 
 
-def mix(hi, lo, pieces):
+def mix(hi, lo, pieces, after):
     replicas, rows, width = pieces.shape
     block = 16
     n = hi.shape[0]
@@ -195,12 +263,12 @@
         mix_kernel,
         grid=(rows // block,),
         out_shape=pltpu.HBM(pieces.shape, BF),
-        in_specs=[matrix, matrix, piece],
+        in_specs=[matrix, matrix, piece, ANY],
         out_specs=piece,
         compiler_params=params(),
         cost_estimate=cost(4 * n * n * width * rows // block, 4 * pieces.size + 4 * n * n),
         name="mix",
-    )(hi, lo, pieces)
+    )(hi, lo, pieces, after)
 
 
 def spread_kernel(m_ref, hi_ref, lo_ref):
@@ -233,21 +301,36 @@
     )(matrix)
 
 
-def landed_kernel(u_ref, o_ref):
-    o_ref[...] = u_ref[...]
+LANDINGS = 6
+
+
+def landed_kernel(u_ref, o_ref, held, into, out_of):
+    rows = u_ref.shape[0] // LANDINGS
+    at = [pl.ds(i * rows, rows) for i in range(LANDINGS)]
+    loads = [pltpu.make_async_copy(u_ref.at[at[i], :], held.at[at[i], :], into.at[i]) for i in range(LANDINGS)]
+    stores = [pltpu.make_async_copy(held.at[at[i], :], o_ref.at[at[i], :], out_of.at[i]) for i in range(LANDINGS)]
+    for load in loads:
+        load.start()
+    for load, store in zip(loads, stores):
+        load.wait()
+        store.start()
+    for store in stores:
+        store.wait()
 
 
 def landed(array):
-    h = array.shape[0]
-    rows = pl.BlockSpec((h // 4, D), lambda i: (i, 0))
     return pl.pallas_call(
         landed_kernel,
-        grid=(4,),
         out_shape=pltpu.HBM(array.shape, BF),
-        in_specs=[rows],
-        out_specs=rows,
-        compiler_params=params(),
-        cost_estimate=cost(0, 4 * h * D),
+        in_specs=[ANY],
+        out_specs=HBM,
+        scratch_shapes=[
+            pltpu.VMEM(array.shape, BF),
+            pltpu.SemaphoreType.DMA((LANDINGS,)),
+            pltpu.SemaphoreType.DMA((LANDINGS,)),
+        ],
+        compiler_params=params(),
+        cost_estimate=cost(0, 4 * array.size),
         name="landed",
     )(array)
 
@@ -276,24 +359,26 @@
     tokens = loss_grad.shape[0]
     own = tokens // 2
 
+    core_at = jnp.reshape(core, (1,)).astype(jnp.int32)
+    last = (segment_index == segments - 1).astype(jnp.int32)
+    other_x = other_core(inputs[0])
+    other_dy = other_core(lax.dynamic_slice_in_dim(loss_grad, (1 - core) * own, own, 0))
     other_in = other_core(weight_in)
     other_out = other_core(weight_out)
-    x_rows = lax.all_gather(inputs[0], "tp", axis=1, tiled=True)
-    x_own = lax.dynamic_slice_in_dim(x_rows, core * own, own, 0)
-    cot = lax.dynamic_slice_in_dim(lax.all_gather(loss_grad, "tp", axis=1, tiled=True), core * own, own, 0)
-    cot = jnp.where(segment_index == segments - 1, cot, jnp.zeros_like(cot))
-    slopes = (token_slopes(x_own, weight_in), token_slopes(x_own, other_in))
-    wouts, wins = (weight_out, other_out), (weight_in, other_in)
+    at = jnp.stack([core.astype(jnp.int32), last])
+    x_rows, x_own, *cots = entering(at, inputs[0], other_x, loss_grad, other_dy)
+    own_slopes, own_in_t = token_slopes(x_own, weight_in)
+    other_slopes, other_in_t = token_slopes(x_own, other_in)
+    slopes, wouts, wins_t = (own_slopes, other_slopes), (weight_out, kept(other_out)), (own_in_t, other_in_t)
 
     act_t, slopes_t = unit_parts(weight_in, x_rows)
     hi, lo = spread_matrix(mixing)
 
-    rows = own // CHUNKS
-    cots = [cot[c * rows:(c + 1) * rows] for c in range(CHUNKS)]
+    columns = own // CHUNKS
     kept_cot = []
     kept_result = []
     for turn_index in range(segments - 1):
-        results = [turn(cots[c], wouts, wins, slopes, c * rows, mixing) for c in range(CHUNKS)]
+        results = [turn(cots[c], wouts, wins_t, slopes, c * columns, mixing) for c in range(CHUNKS)]
         kept_cot.append(cots)
         kept_result.append(results)
         cots = [passed_along(r) for r in results]
@@ -306,25 +391,26 @@
             for t in range(1, segments):
                 total = total + kept[t][c]
             parts.append(total)
-        return jnp.concatenate(parts, axis=0)
-
-    cot_rows = lax.all_gather(summed(kept_cot), "tp", axis=0, tiled=True)
-    updated_out = update_out(act_t, cot_rows, weight_out)
+        return jnp.concatenate(parts, axis=1)
+
+    cot_t = lax.all_gather(summed(kept_cot), "tp", axis=1, tiled=True)
+    updated_in = update_in(slopes_t, cot_t, x_rows, weight_out, weight_in)
+    pieces_in = sent_out(updated_in.reshape(replicas, units // replicas, D))
+    updated_out = update_out(act_t, cot_t, weight_out)
     pieces_out = sent_out(updated_out.reshape(replicas, units // replicas, D))
-    updated_in = update_in(slopes_t, cot_rows, x_rows, weight_out, weight_in, updated_out)
-    pieces_in = sent_out(updated_in.reshape(replicas, units // replicas, D))
-    kept_result.append([turn(cots[c], wouts, wins, slopes, c * rows, updated_in) for c in range(CHUNKS)])
-    back_out = sent_out(mix(hi, lo, pieces_out))
-    back_in = sent_out(mix(hi, lo, pieces_in))
-    mixed_out = landed(back_out.reshape(units, D))[None, None]
-    mixed_in = back_in.reshape(1, 1, units, D)
-
+    mixture_in = mix(hi, lo, pieces_in, mixing)
+    back_in = sent_out(mixture_in)
+    back_out = sent_out(mix(hi, lo, pieces_out, mixture_in))
+    mixed_in = landed(back_in.reshape(units, D))
+    mixed_out = landed(back_out.reshape(units, D))
+
+    kept_result.append([turn(cots[c], wouts, wins_t, slopes, c * columns, mixed_in) for c in range(CHUNKS)])
     result = summed(kept_result)
     width = D // 2
-    mine = lax.dynamic_slice_in_dim(result, core * width, width, 1)
-    theirs = other_core(lax.dynamic_slice_in_dim(result, (1 - core) * width, width, 1))
-    dx = jnp.where(core == 0, jnp.concatenate([mine, theirs], axis=0), jnp.concatenate([theirs, mine], axis=0))
-    return dx[None], mixed_in, mixed_out
+    mine = lax.dynamic_slice_in_dim(result, core * width, width, 0)
+    theirs = other_core(lax.dynamic_slice_in_dim(result, (1 - core) * width, width, 0))
+    dx = leaving(core_at, mine, theirs)
+    return dx[None], mixed_in[None, None], mixed_out[None, None]
 
 
 def solution(mesh):

time: 332 us -> 325 us (0.979)
  blocking collectives: 77.8 us -> 2.37 us
  waiting for transfers between devices: 133 us -> 197 us
  starting transfers between devices: 31.5 us -> 45 us
  Pallas kernels: 67.5 us -> 59.2 us
    all_to_all x1 -> x0, blocking collectives: 67.7 us -> none  [sent_out(): return lax.all_to_all(block, 'rep', split_axis=0, concat_axis=0, tiled=True)]
    all_to_all x3 -> x4, waiting for transfers between devices: 128 us -> 185 us  [sent_out(): return lax.all_to_all(block, 'rep', split_axis=0, concat_axis=0, tiled=True)]
    all_to_all x3 -> x4, starting transfers between devices: 16.5 us -> 27.2 us  [sent_out(): return lax.all_to_all(block, 'rep', split_axis=0, concat_axis=0, tiled=True)]
    pallas_call x11 -> x15, Pallas kernels: 48.8 us -> 39.1 us  [the longest x8 26.7 us: turn(): pl.pallas_call(lambda *refs: turn_kernel(col0, *refs), out_shape=jax.Shap...]
    all_gather x3 -> x1, blocking collectives: 10.1 us -> 2.37 us  [shards(): cot_t = lax.all_gather(summed(kept_cot), 'tp', axis=1, tiled=True)]
    ppermute x3 -> x5, waiting for transfers between devices: 1.43 us -> 6.37 us  [other_core(): return lax.ppermute(shard, 'tp', [(0, 1), (1, 0)])]
    unnamed x43 -> x68, local copies, waits for them, and re-layouts: 18.1 us -> 18 us
  transfers between devices with their start and end apart: 12 -> 15, of which waited for: 5 -> 7; matrix products, arithmetic and copies ran while one was open for 0% -> 0% of each run, Pallas kernels for 16% -> 15%
where the time goes in v2:
time: 325 us; the launch traced here: 324 us
  waiting for transfers between devices  197 us (61%)
  Pallas kernels  59.2 us (18%)
  starting transfers between devices  45 us (14%)
  local copies, waits for them, and re-layouts  18.9 us (6%)
    all_to_all x4, waiting for transfers between devices, sent_out(): return lax.all_to_all(block, 'rep', split_axis=0, concat_axis=0, tiled=True)  185 us
    all_to_all x4, starting transfers between devices, sent_out(): return lax.all_to_all(block, 'rep', split_axis=0, concat_axis=0, tiled=True)  27.2 us
    pallas_call x8, Pallas kernels, turn(): pl.pallas_call(lambda *refs: turn_kernel(col0, *refs), out_shape=jax.Shap...  26.7 us
    unnamed x68, local copies, waits for them, and re-layouts  18 us
    ppermute x6, starting transfers between devices, passed_along(): lax.ppermute(shard, 'section', [(i, i - 1) for i in range(1, length)])  16.5 us
    pallas_call x2, Pallas kernels, mix(): pl.pallas_call(mix_kernel, grid=(rows // block,), out_shape=pltpu.HBM(pie...  10.9 us
  transfers between devices with their start and end apart: 15, of which 7 were waited for; matrix products, arithmetic and copies ran while one was open for 0% of the time, Pallas kernels for 15%

profile of v2, /device:TPU:16, one launch (start us, length us, event | category | flops | bytes accessed | tf_op | source)
XLA Modules:
  0.0 323.8 jit_solution(8121094531318771593)
XLA Ops:
  2.8 5.6 %collective-permute-done.1.other_dy_ref = bf16[256,384]{1,0:T(8,128)(2,1)S(1)} collective-permute-done((bf16[256,384]{1,0:T(8,128)(2,1)S(1)}, bf16[256,384]{1,0:T(8,128)(2,1)S(1)}, u32[]{:S(2)}, u32[]{:S(2)}) %collective-permute-start.1) | collective-permute-done | bytes 196640 | tf_op jit(solution)/shard_map/ppermute | solution.py:344
  16.3 3.1 kept.1.refs_2_
  20.0 3.3 %turn.8 = bf16[768,128]{1,0:T(8,128)(2,1)S(1)} custom-call(bf16[768,128]{1,0:T(8,128)(2,1)S(1)} %get-tuple-element.15.refs_0_, bf16[1536,768]{1,0:T(8,128)(2,1)S(1)} %bitcast.13, bf16[1536,768]{1,0:T(8,128)(2,1)S(1)} %kept.1.refs_2_, bf16[768,1536]{1,0:T(8,128)(2,1)S(1)} %get-tuple-element.17.refs_3_, bf16[768,1536]{1,0:T(8,128)(2,1)S(1)} %get-tuple-element.18.refs_4_, ...), custom_call_target="tpu_custom_call" | custom-call | flops 1207959552 | bytes 11010048 | tf_op jit(solution)/shard_map/turn/pallas_call | solution.py:161
  25.7 3.3 %turn.11 = bf16[768,128]{1,0:T(8,128)(2,1)S(1)} custom-call(bf16[768,128]{1,0:T(8,128)(2,1)S(1)} %get-tuple-element.25.refs_0_, bf16[1536,768]{1,0:T(8,128)(2,1)S(1)} %bitcast.14, bf16[1536,768]{1,0:T(8,128)(2,1)S(1)} %kept.1.refs_2_, bf16[768,1536]{1,0:T(8,128)(2,1)S(1)} %get-tuple-element.17.refs_3_, bf16[768,1536]{1,0:T(8,128)(2,1)S(1)} %get-tuple-element.18.refs_4_, ...), custom_call_target="tpu_custom_call" | custom-call | flops 1207959552 | bytes 11010048 | tf_op jit(solution)/shard_map/turn/pallas_call | solution.py:161
  29.1 4.1 %collective-permute-start.7 = (bf16[768,128]{1,0:T(8,128)(2,1)S(1)}, bf16[768,128]{1,0:T(8,128)(2,1)S(1)}, u32[]{:S(2)}, u32[]{:S(2)}) collective-permute-start(bf16[768,128]{1,0:T(8,128)(2,1)S(1)} %turn.11), channel_id=1, source_target_pairs={{2,0},{4,2},{6,4},{3,1},{5,3},{7,5},{10,8},{12,10},{14,12},{11,9},... | collective-permute-start | bytes 589832 | tf_op jit(solution)/shard_map/ppermute | solution.py:340
  33.2 3.3 %turn.9 = bf16[768,128]{1,0:T(8,128)(2,1)S(1)} custom-call(bf16[768,128]{1,0:T(8,128)(2,1)S(1)} %collective-permute-done.4.refs_0_, bf16[1536,768]{1,0:T(8,128)(2,1)S(1)} %bitcast.15, bf16[1536,768]{1,0:T(8,128)(2,1)S(1)} %kept.1.refs_2_, bf16[768,1536]{1,0:T(8,128)(2,1)S(1)} %get-tuple-element.17.refs_3_, bf16[768,1536]{1,0:T(8,128)(2,1)S(1)} %get-tuple-element.18.refs_4_, ...), custom_call_target="tpu_custom_call" | custom-call | flops 1207959552 | bytes 11010048 | tf_op jit(solution)/shard_map/turn/pallas_call | solution.py:161
  38.7 3.3 %turn.12 = bf16[768,128]{1,0:T(8,128)(2,1)S(1)} custom-call(bf16[768,128]{1,0:T(8,128)(2,1)S(1)} %collective-permute-done.7.refs_0_, bf16[1536,768]{1,0:T(8,128)(2,1)S(1)} %bitcast.16, bf16[1536,768]{1,0:T(8,128)(2,1)S(1)} %kept.1.refs_2_, bf16[768,1536]{1,0:T(8,128)(2,1)S(1)} %get-tuple-element.17.refs_3_, bf16[768,1536]{1,0:T(8,128)(2,1)S(1)} %get-tuple-element.18.refs_4_, ...), custom_call_target="tpu_custom_call" | custom-call | flops 1207959552 | bytes 11010048 | tf_op jit(solution)/shard_map/turn/pallas_call | solution.py:161
  42.1 3.6 %collective-permute-start.8 = (bf16[768,128]{1,0:T(8,128)(2,1)S(1)}, bf16[768,128]{1,0:T(8,128)(2,1)S(1)}, u32[]{:S(2)}, u32[]{:S(2)}) collective-permute-start(bf16[768,128]{1,0:T(8,128)(2,1)S(1)} %turn.12), channel_id=1, source_target_pairs={{2,0},{4,2},{6,4},{3,1},{5,3},{7,5},{10,8},{12,10},{14,12},{11,9},... | collective-permute-start | bytes 589832 | tf_op jit(solution)/shard_map/ppermute | solution.py:340
  45.7 3.3 %turn.10 = bf16[768,128]{1,0:T(8,128)(2,1)S(1)} custom-call(bf16[768,128]{1,0:T(8,128)(2,1)S(1)} %collective-permute-done.5.refs_0_, bf16[1536,768]{1,0:T(8,128)(2,1)S(1)} %bitcast.17, bf16[1536,768]{1,0:T(8,128)(2,1)S(1)} %kept.1.refs_2_, bf16[768,1536]{1,0:T(8,128)(2,1)S(1)} %get-tuple-element.17.refs_3_, bf16[768,1536]{1,0:T(8,128)(2,1)S(1)} %get-tuple-element.18.refs_4_, ...), custom_call_target="tpu_custom_call" | custom-call | flops 1207959552 | bytes 11010048 | tf_op jit(solution)/shard_map/turn/pallas_call | solution.py:161
  54.8 3.3 %turn.13 = bf16[768,128]{1,0:T(8,128)(2,1)S(1)} custom-call(bf16[768,128]{1,0:T(8,128)(2,1)S(1)} %collective-permute-done.8.refs_0_, bf16[1536,768]{1,0:T(8,128)(2,1)S(1)} %bitcast.18, bf16[1536,768]{1,0:T(8,128)(2,1)S(1)} %kept.1.refs_2_, bf16[768,1536]{1,0:T(8,128)(2,1)S(1)} %get-tuple-element.17.refs_3_, bf16[768,1536]{1,0:T(8,128)(2,1)S(1)} %get-tuple-element.18.refs_4_, ...), custom_call_target="tpu_custom_call" | custom-call | flops 1207959552 | bytes 11010048 | tf_op jit(solution)/shard_map/turn/pallas_call | solution.py:161
  60.6 5.1 %collective-permute-done.9.refs_0_ = bf16[768,128]{1,0:T(8,128)(2,1)S(1)} collective-permute-done((bf16[768,128]{1,0:T(8,128)(2,1)S(1)}, bf16[768,128]{1,0:T(8,128)(2,1)S(1)}, u32[]{:S(2)}, u32[]{:S(2)}) %collective-permute-start.9) | collective-permute-done | bytes 196640 | tf_op jit(solution)/shard_map/ppermute | solution.py:340
  68.2 3.7 %update_in.1 = bf16[1536,768]{1,0:T(8,128)(2,1)} custom-call(f32[1536,512]{1,0:T(8,128)S(1)} %get-tuple-element.24.s_ref, bf16[768,512]{1,0:T(8,128)(2,1)S(1)} %all_gather.3.c_ref, bf16[512,768]{1,0:T(8,128)(2,1)S(1)} %get-tuple-element.23.x_ref, bf16[1536,768]{1,0:T(8,128)(2,1)S(1)} %bitcast.19, bf16[1536,768]{1,0:T(8,128)(2,1)S(1)} %bitcast.27), custom_call_target="tpu_custom_call" | custom-call | flops 2415919104 | bytes 10223616 | tf_op jit(solution)/shard_map/update_in/pallas_call | solution.py:237
  71.9 9.9 %all-to-all-start = ((bf16[32,48,768]{2,1,0:T(8,128)(2,1)}), bf16[32,48,768]{2,1,0:T(8,128)(2,1)}, u32[]{:S(2)}, u32[]{:S(2)}) async-start(bf16[32,48,768]{2,1,0:T(8,128)(2,1)} %bitcast.31), calls=%async_computation | async-start | bytes 4718592 | tf_op jit(solution)/shard_map/all_to_all | solution.py:348
  85.7 51.9 %all-to-all-done.u_ref = bf16[32,48,768]{2,1,0:T(8,128)(2,1)} async-done(((bf16[32,48,768]{2,1,0:T(8,128)(2,1)}), bf16[32,48,768]{2,1,0:T(8,128)(2,1)}, u32[]{:S(2)}, u32[]{:S(2)}) %all-to-all-start) | async-done | bytes 2359328 | tf_op jit(solution)/shard_map/all_to_all | solution.py:348
  137.6 5.6 %all-to-all-start.2 = ((bf16[32,48,768]{2,1,0:T(8,128)(2,1)}), bf16[32,48,768]{2,1,0:T(8,128)(2,1)}, u32[]{:S(2)}, u32[]{:S(2)}) async-start(bf16[32,48,768]{2,1,0:T(8,128)(2,1)} %bitcast.30), calls=%async_computation.2 | async-start | bytes 4718592 | tf_op jit(solution)/shard_map/all_to_all | solution.py:348
  143.9 5.4 %mix.2.after_ref = bf16[32,48,768]{2,1,0:T(8,128)(2,1)} custom-call(bf16[512,512]{1,0:T(8,128)(2,1)S(1)} %get-tuple-element.21.hi_ref, bf16[512,512]{1,0:T(8,128)(2,1)S(1)} %get-tuple-element.22.lo_ref, bf16[32,48,768]{2,1,0:T(8,128)(2,1)} %all-to-all-done.u_ref, f32[32,32]{1,0:T(8,128)S(1)} %copy-done.30), custom_call_target="tpu_custom_call" | custom-call | flops 2415919104 | bytes 5767168 | tf_op jit(solution)/shard_map/mix/pallas_call | solution.py:262
  150.1 48.8 %all-to-all-done.2.u_ref = bf16[32,48,768]{2,1,0:T(8,128)(2,1)} async-done(((bf16[32,48,768]{2,1,0:T(8,128)(2,1)}), bf16[32,48,768]{2,1,0:T(8,128)(2,1)}, u32[]{:S(2)}, u32[]{:S(2)}) %all-to-all-start.2) | async-done | bytes 2359328 | tf_op jit(solution)/shard_map/all_to_all | solution.py:348
  198.9 5.6 %all-to-all-start.1 = ((bf16[32,48,768]{2,1,0:T(8,128)(2,1)}), bf16[32,48,768]{2,1,0:T(8,128)(2,1)}, u32[]{:S(2)}, u32[]{:S(2)}) async-start(bf16[32,48,768]{2,1,0:T(8,128)(2,1)} %mix.2.after_ref), calls=%async_computation.1 | async-start | bytes 4718592 | tf_op jit(solution)/shard_map/all_to_all | solution.py:348
  207.2 5.4 %mix.3 = bf16[32,48,768]{2,1,0:T(8,128)(2,1)} custom-call(bf16[512,512]{1,0:T(8,128)(2,1)S(1)} %get-tuple-element.21.hi_ref, bf16[512,512]{1,0:T(8,128)(2,1)S(1)} %copy-done.33, bf16[32,48,768]{2,1,0:T(8,128)(2,1)} %all-to-all-done.2.u_ref, bf16[32,48,768]{2,1,0:T(8,128)(2,1)S(1)} %copy-done.14), custom_call_target="tpu_custom_call" | custom-call | flops 2415919104 | bytes 5767168 | tf_op jit(solution)/shard_map/mix/pallas_call | solution.py:262
  212.7 47.2 %all-to-all-done.1 = bf16[32,48,768]{2,1,0:T(8,128)(2,1)} async-done(((bf16[32,48,768]{2,1,0:T(8,128)(2,1)}), bf16[32,48,768]{2,1,0:T(8,128)(2,1)}, u32[]{:S(2)}, u32[]{:S(2)}) %all-to-all-start.1) | async-done | bytes 2359328 | tf_op jit(solution)/shard_map/all_to_all | solution.py:348
  259.9 6.1 %all-to-all-start.3 = ((bf16[32,48,768]{2,1,0:T(8,128)(2,1)}), bf16[32,48,768]{2,1,0:T(8,128)(2,1)}, u32[]{:S(2)}, u32[]{:S(2)}) async-start(bf16[32,48,768]{2,1,0:T(8,128)(2,1)} %mix.3), calls=%async_computation.3 | async-start | bytes 4718592 | tf_op jit(solution)/shard_map/all_to_all | solution.py:348
  276.1 3.3 %turn.14 = bf16[768,128]{1,0:T(8,128)(2,1)S(1)} custom-call(bf16[768,128]{1,0:T(8,128)(2,1)S(1)} %collective-permute-done.6.refs_0_, bf16[1536,768]{1,0:T(8,128)(2,1)S(1)} %bitcast.21, bf16[1536,768]{1,0:T(8,128)(2,1)S(1)} %copy-done.2, bf16[768,1536]{1,0:T(8,128)(2,1)S(1)} %copy-done.4, bf16[768,1536]{1,0:T(8,128)(2,1)S(1)} %copy-done.6, ...), custom_call_target="tpu_custom_call" | custom-call | flops 1207959552 | bytes 11010048 | tf_op jit(solution)/shard_map/turn/pallas_call | solution.py:161
  279.5 3.3 %turn.15 = bf16[768,128]{1,0:T(8,128)(2,1)S(1)} custom-call(bf16[768,128]{1,0:T(8,128)(2,1)S(1)} %collective-permute-done.9.refs_0_, bf16[1536,768]{1,0:T(8,128)(2,1)S(1)} %bitcast.22, bf16[1536,768]{1,0:T(8,128)(2,1)S(1)} %copy-done.2, bf16[768,1536]{1,0:T(8,128)(2,1)S(1)} %copy-done.4, bf16[768,1536]{1,0:T(8,128)(2,1)S(1)} %copy-done.6, ...), custom_call_target="tpu_custom_call" | custom-call | flops 1207959552 | bytes 11010048 | tf_op jit(solution)/shard_map/turn/pallas_call | solution.py:161
  283.2 37.3 %all-to-all-done.3 = bf16[32,48,768]{2,1,0:T(8,128)(2,1)} async-done(((bf16[32,48,768]{2,1,0:T(8,128)(2,1)}), bf16[32,48,768]{2,1,0:T(8,128)(2,1)}, u32[]{:S(2)}, u32[]{:S(2)}) %all-to-all-start.3) | async-done | bytes 2359328 | tf_op jit(solution)/shard_map/all_to_all | solution.py:348
  (103 shorter events, 47.4 us)
Async XLA Ops:
  0.6 14.4 %collective-permute-start.3 = (bf16[1536,768]{1,0:T(8,128)(2,1)}, bf16[1536,768]{1,0:T(8,128)(2,1)S(1)}, u32[]{:S(2)}, u32[]{:S(2)}) collective-permute-start(bf16[1536,768]{1,0:T(8,128)(2,1)} %bitcast.24), channel_id=1, source_target_pairs={{0,1},{1,0},{2,3},{3,2},{4,5},{5,4},{6,7},{7,6},{8,9},{9,8},{10,11... | collective-permute-start | bytes 7077896 | tf_op jit(solution)/shard_map/ppermute | solution.py:344
  0.7 15.6 %collective-permute-start.2 = (bf16[1536,768]{1,0:T(8,128)(2,1)}, bf16[1536,768]{1,0:T(8,128)(2,1)}, u32[]{:S(2)}, u32[]{:S(2)}) collective-permute-start(bf16[1536,768]{1,0:T(8,128)(2,1)} %bitcast.12), channel_id=1, source_target_pairs={{0,1},{1,0},{2,3},{3,2},{4,5},{5,4},{6,7},{7,6},{8,9},{9,8},{10,11... | collective-permute-start | bytes 7077896 | tf_op jit(solution)/shard_map/ppermute | solution.py:344
  1.2 8.0 %collective-permute-start = (bf16[512,384]{1,0:T(8,128)(2,1)}, bf16[512,384]{1,0:T(8,128)(2,1)S(1)}, u32[]{:S(2)}, u32[]{:S(2)}) collective-permute-start(bf16[512,384]{1,0:T(8,128)(2,1)} %bitcast.28), channel_id=1, source_target_pairs={{0,1},{1,0},{2,3},{3,2},{4,5},{5,4},{6,7},{7,6},{8,9},{9,8},{10,11... | collective-permute-start | bytes 1179656 | tf_op jit(solution)/shard_map/ppermute | solution.py:344
  2.3 6.2 %collective-permute-start.1 = (bf16[256,384]{1,0:T(8,128)(2,1)S(1)}, bf16[256,384]{1,0:T(8,128)(2,1)S(1)}, u32[]{:S(2)}, u32[]{:S(2)}) collective-permute-start(bf16[256,384]{1,0:T(8,128)(2,1)S(1)} %constant_dynamic-slice_fusion), channel_id=1, source_target_pairs={{0,1},{1,0},{2,3},{3,2},{4,5},{5,4},{6,7},{7,6},{8,9},{9,8},{10,11... | collective-permute-start | bytes 589832 | tf_op jit(solution)/shard_map/ppermute | solution.py:344
  15.0 39.8 %copy-start.3 = (bf16[768,1536]{1,0:T(8,128)(2,1)}, bf16[768,1536]{1,0:T(8,128)(2,1)S(1)}, u32[]{:S(2)}) copy-start(bf16[768,1536]{1,0:T(8,128)(2,1)S(1)} %get-tuple-element.17.refs_3_) | copy-start | bytes 7077892
  15.0 39.8 %copy-start.7 = (f32[1536,256]{1,0:T(8,128)}, f32[1536,256]{1,0:T(8,128)S(1)}, u32[]{:S(2)}) copy-start(f32[1536,256]{1,0:T(8,128)S(1)} %get-tuple-element.19.refs_5_) | copy-start | bytes 4718596
  16.3 38.5 %copy-start.5 = (bf16[768,1536]{1,0:T(8,128)(2,1)}, bf16[768,1536]{1,0:T(8,128)(2,1)S(1)}, u32[]{:S(2)}) copy-start(bf16[768,1536]{1,0:T(8,128)(2,1)S(1)} %get-tuple-element.18.refs_4_) | copy-start | bytes 7077892
  16.3 38.5 %copy-start.9 = (f32[1536,256]{1,0:T(8,128)}, f32[1536,256]{1,0:T(8,128)S(1)}, u32[]{:S(2)}) copy-start(f32[1536,256]{1,0:T(8,128)S(1)} %get-tuple-element.20.refs_6_) | copy-start | bytes 4718596
  19.4 35.4 %copy-start.1 = (bf16[1536,768]{1,0:T(8,128)(2,1)}, bf16[1536,768]{1,0:T(8,128)(2,1)S(1)}, u32[]{:S(2)}) copy-start(bf16[1536,768]{1,0:T(8,128)(2,1)S(1)} %kept.1.refs_2_) | copy-start | bytes 7077892
  23.4 9.8 %collective-permute-start.4 = (bf16[768,128]{1,0:T(8,128)(2,1)S(1)}, bf16[768,128]{1,0:T(8,128)(2,1)S(1)}, u32[]{:S(2)}, u32[]{:S(2)}) collective-permute-start(bf16[768,128]{1,0:T(8,128)(2,1)S(1)} %turn.8), channel_id=1, source_target_pairs={{2,0},{4,2},{6,4},{3,1},{5,3},{7,5},{10,8},{12,10},{14,12},{11,9},... | collective-permute-start | bytes 589832 | tf_op jit(solution)/shard_map/ppermute | solution.py:340
  29.1 7.5 %copy-start.20 = (bf16[768,128]{1,0:T(8,128)(2,1)}, bf16[768,128]{1,0:T(8,128)(2,1)S(1)}, u32[]{:S(2)}) copy-start(bf16[768,128]{1,0:T(8,128)(2,1)S(1)} %turn.11) | copy-start | bytes 589828
  29.1 9.6 %collective-permute-start.7 = (bf16[768,128]{1,0:T(8,128)(2,1)S(1)}, bf16[768,128]{1,0:T(8,128)(2,1)S(1)}, u32[]{:S(2)}, u32[]{:S(2)}) collective-permute-start(bf16[768,128]{1,0:T(8,128)(2,1)S(1)} %turn.11), channel_id=1, source_target_pairs={{2,0},{4,2},{6,4},{3,1},{5,3},{7,5},{10,8},{12,10},{14,12},{11,9},... | collective-permute-start | bytes 589832 | tf_op jit(solution)/shard_map/ppermute | solution.py:340
  36.6 9.1 %collective-permute-start.5 = (bf16[768,128]{1,0:T(8,128)(2,1)S(1)}, bf16[768,128]{1,0:T(8,128)(2,1)S(1)}, u32[]{:S(2)}, u32[]{:S(2)}) collective-permute-start(bf16[768,128]{1,0:T(8,128)(2,1)S(1)} %turn.9), channel_id=1, source_target_pairs={{2,0},{4,2},{6,4},{3,1},{5,3},{7,5},{10,8},{12,10},{14,12},{11,9},... | collective-permute-start | bytes 589832 | tf_op jit(solution)/shard_map/ppermute | solution.py:340
  42.1 9.0 %copy-start.13 = (bf16[1,1,1536,768]{3,2,1,0:T(8,128)(2,1)S(1)}, bf16[1,1,1536,768]{3,2,1,0:T(8,128)(2,1)}, u32[]{:S(2)}) copy-start(bf16[1,1,1536,768]{3,2,1,0:T(8,128)(2,1)} %param.7) | copy-start | bytes 7077892
  42.1 12.7 %collective-permute-start.8 = (bf16[768,128]{1,0:T(8,128)(2,1)S(1)}, bf16[768,128]{1,0:T(8,128)(2,1)S(1)}, u32[]{:S(2)}, u32[]{:S(2)}) collective-permute-start(bf16[768,128]{1,0:T(8,128)(2,1)S(1)} %turn.12), channel_id=1, source_target_pairs={{2,0},{4,2},{6,4},{3,1},{5,3},{7,5},{10,8},{12,10},{14,12},{11,9},... | collective-permute-start | bytes 589832 | tf_op jit(solution)/shard_map/ppermute | solution.py:340
  49.1 9.1 %copy-start.26 = (bf16[768,128]{1,0:T(8,128)(2,1)}, bf16[768,128]{1,0:T(8,128)(2,1)S(1)}, u32[]{:S(2)}) copy-start(bf16[768,128]{1,0:T(8,128)(2,1)S(1)} %turn.10) | copy-start | bytes 589828
  49.1 11.4 %collective-permute-start.6 = (bf16[768,128]{1,0:T(8,128)(2,1)S(1)}, bf16[768,128]{1,0:T(8,128)(2,1)S(1)}, u32[]{:S(2)}, u32[]{:S(2)}) collective-permute-start(bf16[768,128]{1,0:T(8,128)(2,1)S(1)} %turn.10), channel_id=1, source_target_pairs={{2,0},{4,2},{6,4},{3,1},{5,3},{7,5},{10,8},{12,10},{14,12},{11,9},... | collective-permute-start | bytes 589832 | tf_op jit(solution)/shard_map/ppermute | solution.py:340
  58.2 13.7 %copy-start.28 = (bf16[768,128]{1,0:T(8,128)(2,1)}, bf16[768,128]{1,0:T(8,128)(2,1)S(1)}, u32[]{:S(2)}) copy-start(bf16[768,128]{1,0:T(8,128)(2,1)S(1)} %turn.13) | copy-start | bytes 589828
  58.2 7.6 %collective-permute-start.9 = (bf16[768,128]{1,0:T(8,128)(2,1)S(1)}, bf16[768,128]{1,0:T(8,128)(2,1)S(1)}, u32[]{:S(2)}, u32[]{:S(2)}) collective-permute-start(bf16[768,128]{1,0:T(8,128)(2,1)S(1)} %turn.13), channel_id=1, source_target_pairs={{2,0},{4,2},{6,4},{3,1},{5,3},{7,5},{10,8},{12,10},{14,12},{11,9},... | collective-permute-start | bytes 589832 | tf_op jit(solution)/shard_map/ppermute | solution.py:340
  71.9 65.7 %all-to-all-start = ((bf16[32,48,768]{2,1,0:T(8,128)(2,1)}), bf16[32,48,768]{2,1,0:T(8,128)(2,1)}, u32[]{:S(2)}, u32[]{:S(2)}) async-start(bf16[32,48,768]{2,1,0:T(8,128)(2,1)} %bitcast.31), calls=%async_computation | async-start | bytes 4718592 | tf_op jit(solution)/shard_map/all_to_all | solution.py:348
  137.6 61.3 %all-to-all-start.2 = ((bf16[32,48,768]{2,1,0:T(8,128)(2,1)}), bf16[32,48,768]{2,1,0:T(8,128)(2,1)}, u32[]{:S(2)}, u32[]{:S(2)}) async-start(bf16[32,48,768]{2,1,0:T(8,128)(2,1)} %bitcast.30), calls=%async_computation.2 | async-start | bytes 4718592 | tf_op jit(solution)/shard_map/all_to_all | solution.py:348
  198.9 61.0 %all-to-all-start.1 = ((bf16[32,48,768]{2,1,0:T(8,128)(2,1)}), bf16[32,48,768]{2,1,0:T(8,128)(2,1)}, u32[]{:S(2)}, u32[]{:S(2)}) async-start(bf16[32,48,768]{2,1,0:T(8,128)(2,1)} %mix.2.after_ref), calls=%async_computation.1 | async-start | bytes 4718592 | tf_op jit(solution)/shard_map/all_to_all | solution.py:348
  259.9 60.5 %all-to-all-start.3 = ((bf16[32,48,768]{2,1,0:T(8,128)(2,1)}), bf16[32,48,768]{2,1,0:T(8,128)(2,1)}, u32[]{:S(2)}, u32[]{:S(2)}) async-start(bf16[32,48,768]{2,1,0:T(8,128)(2,1)} %mix.3), calls=%async_computation.3 | async-start | bytes 4718592 | tf_op jit(solution)/shard_map/all_to_all | solution.py:348
  283.1 39.9 %collective-permute-start.10 = (bf16[384,256]{1,0:T(8,128)(2,1)S(1)}, bf16[384,256]{1,0:T(8,128)(2,1)S(1)}, u32[]{:S(2)}, u32[]{:S(2)}) collective-permute-start(bf16[384,256]{1,0:T(8,128)(2,1)S(1)} %get-tuple-element.27), channel_id=1, source_target_pairs={{0,1},{1,0},{2,3},{3,2},{4,5},{5,4},{6,7},{7,6},{8,9},{9,8},{10,11... | collective-permute-start | bytes 589832 | tf_op jit(solution)/shard_map/ppermute | solution.py:344
  (25 other events, 69.0 us)

commit v3 on v2

--- a/solution.py
+++ b/solution.py
@@ -55,21 +55,18 @@
     return jnp.where(core == 0, jnp.concatenate([mine, theirs], axis=1), jnp.concatenate([theirs, mine], axis=1))
 
 
-def entering_kernel(at, x_ref, other_x_ref, dy_ref, other_dy_ref, whole_ref, own_ref, *outs):
+def entering_kernel(at, x_ref, other_x_ref, dy_ref, other_dy_ref, whole_ref, own_ref, cot_ref):
     core = at[0]
-    own, m = own_ref.shape[0], outs[0].shape[1]
+    own = own_ref.shape[0]
     whole_ref[...] = joined(core, x_ref[...], other_x_ref[...])
-    start = pl.multiple_of(core * own, own)
-    own_ref[...] = whole_ref[pl.ds(start, own), :]
-    dy = joined(core, dy_ref[pl.ds(start, own), :], other_dy_ref[...])
-    dy = jnp.transpose(jnp.where(at[1] == 1, dy, jnp.zeros_like(dy)))
-    for c, o_ref in enumerate(outs):
-        o_ref[...] = dy[:, c * m : (c + 1) * m]
+    own_ref[...] = whole_ref[pl.ds(pl.multiple_of(core * own, own), own), :]
+    dy = joined(core, dy_ref[...], other_dy_ref[...])
+    cot_ref[...] = jnp.transpose(jnp.where(at[1] == 1, dy, jnp.zeros_like(dy)))
 
 
 def entering(at, x, other_x, dy, other_dy):
     own = dy.shape[0] // 2
-    shapes = [(2 * own, D), (own, D)] + [(D, own // CHUNKS)] * CHUNKS
+    shapes = [(2 * own, D), (own, D), (D, 2 * own)]
     return pl.pallas_call(
         entering_kernel,
         out_shape=[jax.ShapeDtypeStruct(s, BF) for s in shapes],
@@ -79,6 +76,52 @@
         cost_estimate=cost(0, 16 * own * D),
         name="entering",
     )(at, x, other_x, dy, other_dy)
+
+
+def first_turn_kernel(chunk, m, at, c_ref, wo_ref, wt_ref, s_ref, cot_ref, mine_ref, theirs_ref, delta):
+    own = c_ref.shape[1] // 2
+    lanes = [pl.ds(pl.multiple_of(side * own + chunk * m, m), m) for side in (at[0], 1 - at[0])]
+    cot = jnp.concatenate([c_ref[:, lane] for lane in lanes], axis=1)
+    for at_rows in blocks(wo_ref.shape[0]):
+        backward = nn(wo_ref[at_rows, :], cot) * out_scale
+        slopes = jnp.concatenate([s_ref[at_rows, lane] for lane in lanes], axis=1)
+        delta[at_rows, :] = (slopes * backward).astype(BF)
+    partial = (nn(wt_ref[...], delta[...]) * in_scale).astype(BF)
+    cot_ref[...] = cot[:, :m]
+    mine_ref[...] = partial[:, :m]
+    theirs_ref[...] = partial[:, m:]
+
+
+def first_turn(at, chunk, cot, weight_out, weight_in_t, slopes):
+    h, tokens = slopes.shape
+    m = tokens // 2 // CHUNKS
+    return pl.pallas_call(
+        lambda *refs: first_turn_kernel(chunk, m, *refs),
+        out_shape=[jax.ShapeDtypeStruct((D, m), BF)] * 3,
+        in_specs=[SMEM] + [VMEM] * 4,
+        out_specs=[VMEM] * 3,
+        scratch_shapes=[pltpu.VMEM((h, 2 * m), BF)],
+        compiler_params=params(),
+        cost_estimate=cost(8 * m * h * D, 4 * h * D + 8 * m * h),
+        name="first_turn",
+    )(at, cot, weight_out, weight_in_t, slopes)
+
+
+def both_parts_kernel(c_ref, mine_ref, theirs_ref, o_ref):
+    branch = mine_ref[...].astype(F32) + theirs_ref[...].astype(F32)
+    o_ref[...] = (c_ref[...].astype(F32) + branch).astype(BF)
+
+
+def both_parts(cot, mine, theirs):
+    return pl.pallas_call(
+        both_parts_kernel,
+        out_shape=jax.ShapeDtypeStruct(cot.shape, BF),
+        in_specs=[VMEM] * 3,
+        out_specs=VMEM,
+        compiler_params=params(),
+        cost_estimate=cost(0, 8 * cot.size),
+        name="both_parts",
+    )(cot, mine, theirs)
 
 
 def token_slopes_kernel(x_ref, w_ref, s_ref, t_ref):
@@ -121,53 +164,63 @@
     )(array)
 
 
-def unit_parts_kernel(w_ref, x_ref, a_ref, s_ref):
+def unit_parts_kernel(w_ref, x_ref, a_ref, s_ref, t_ref):
     x = x_ref[...]
     for at in blocks(w_ref.shape[0]):
-        values, slopes = gelu_parts(nt(w_ref[at, :], x) * in_scale)
+        weight = w_ref[at, :]
+        values, slopes = gelu_parts(nt(weight, x) * in_scale)
         a_ref[at, :] = values.astype(BF)
         s_ref[at, :] = slopes
+        t_ref[:, at] = jnp.transpose(weight)
 
 
 def unit_parts(weight_in, x_rows):
     m, h = x_rows.shape[0], weight_in.shape[0]
     return pl.pallas_call(
         unit_parts_kernel,
-        out_shape=[jax.ShapeDtypeStruct((h, m), BF), jax.ShapeDtypeStruct((h, m), F32)],
+        out_shape=[
+            jax.ShapeDtypeStruct((h, m), BF),
+            jax.ShapeDtypeStruct((h, m), F32),
+            jax.ShapeDtypeStruct((D, h), BF),
+        ],
         in_specs=[VMEM, VMEM],
-        out_specs=[VMEM, VMEM],
+        out_specs=[VMEM] * 3,
         compiler_params=params(),
         cost_estimate=cost(2 * m * h * D, 2 * h * D + 6 * m * h, 2 * m * h),
         name="unit_parts",
     )(weight_in, x_rows)
 
 
-def turn_kernel(col0, c_ref, wo0_ref, wo1_ref, wt0_ref, wt1_ref, s0_ref, s1_ref, after_ref, o_ref, delta):
+def turn_kernel(col0, at_ref, c_ref, wo0_ref, wo1_ref, wt0_ref, wt1_ref, s0_ref, s1_ref, after_ref, o_ref, delta):
     cot = c_ref[...]
     m = cot.shape[1]
+    own = pl.ds(pl.multiple_of(at_ref[0] * s1_ref.shape[1] + col0, m), m)
     branch = None
-    for wo_ref, wt_ref, s_ref in ((wo0_ref, wt0_ref, s0_ref), (wo1_ref, wt1_ref, s1_ref)):
+    for wo_ref, wt_ref, s_ref, lane in (
+        (wo0_ref, wt0_ref, s0_ref, own),
+        (wo1_ref, wt1_ref, s1_ref, pl.ds(col0, m)),
+    ):
         for at in blocks(wo_ref.shape[0]):
             backward = nn(wo_ref[at, :], cot) * out_scale
-            delta[at, :] = (s_ref[at, pl.ds(col0, m)] * backward).astype(BF)
+            delta[at, :] = (s_ref[at, lane] * backward).astype(BF)
         partial = (nn(wt_ref[...], delta[...]) * in_scale).astype(BF).astype(F32)
         branch = partial if branch is None else branch + partial
     o_ref[...] = (cot.astype(F32) + branch).astype(BF)
 
 
-def turn(cot, wouts, wins_t, slopes, col0, after):
+def turn(at, cot, wouts, wins_t, slopes, col0, after):
     m = cot.shape[1]
     h = wouts[0].shape[0]
     return pl.pallas_call(
         lambda *refs: turn_kernel(col0, *refs),
         out_shape=jax.ShapeDtypeStruct((D, m), BF),
-        in_specs=[VMEM] * 7 + [ANY],
+        in_specs=[SMEM] + [VMEM] * 7 + [ANY],
         out_specs=VMEM,
         scratch_shapes=[pltpu.VMEM((h, m), BF)],
         compiler_params=params(),
         cost_estimate=cost(8 * m * h * D, 8 * h * D + 8 * m * h),
         name="turn",
-    )(cot, wouts[0], wouts[1], wins_t[0], wins_t[1], slopes[0], slopes[1], after)
+    )(at, cot, wouts[0], wouts[1], wins_t[0], wins_t[1], slopes[0], slopes[1], after)
 
 
 def leaving_kernel(core, mine_ref, theirs_ref, o_ref):
@@ -304,7 +357,7 @@
 LANDINGS = 6
 
 
-def landed_kernel(u_ref, o_ref, held, into, out_of):
+def landed_kernel(u_ref, after_ref, o_ref, held, into, out_of):
     rows = u_ref.shape[0] // LANDINGS
     at = [pl.ds(i * rows, rows) for i in range(LANDINGS)]
     loads = [pltpu.make_async_copy(u_ref.at[at[i], :], held.at[at[i], :], into.at[i]) for i in range(LANDINGS)]
@@ -318,11 +371,11 @@
         store.wait()
 
 
-def landed(array):
+def landed(array, after):
     return pl.pallas_call(
         landed_kernel,
         out_shape=pltpu.HBM(array.shape, BF),
-        in_specs=[ANY],
+        in_specs=[ANY, ANY],
         out_specs=HBM,
         scratch_shapes=[
             pltpu.VMEM(array.shape, BF),
@@ -332,7 +385,7 @@
         compiler_params=params(),
         cost_estimate=cost(0, 4 * array.size),
         name="landed",
-    )(array)
+    )(array, after)
 
 
 def passed_along(shard):
@@ -362,23 +415,25 @@
     core_at = jnp.reshape(core, (1,)).astype(jnp.int32)
     last = (segment_index == segments - 1).astype(jnp.int32)
     other_x = other_core(inputs[0])
-    other_dy = other_core(lax.dynamic_slice_in_dim(loss_grad, (1 - core) * own, own, 0))
-    other_in = other_core(weight_in)
-    other_out = other_core(weight_out)
+    other_dy = other_core(loss_grad)
+    late_in, late_out, other_x, other_dy = lax.optimization_barrier((weight_in, weight_out, other_x, other_dy))
+    other_in = other_core(late_in)
+    other_out = other_core(late_out)
     at = jnp.stack([core.astype(jnp.int32), last])
-    x_rows, x_own, *cots = entering(at, inputs[0], other_x, loss_grad, other_dy)
-    own_slopes, own_in_t = token_slopes(x_own, weight_in)
+    x_rows, x_own, cot = entering(at, inputs[0], other_x, loss_grad, other_dy)
+    act_t, slopes_t, own_in_t = unit_parts(weight_in, x_rows)
+    hi, lo = spread_matrix(mixing)
+
+    columns = own // CHUNKS
+    halves = [first_turn(at, c, cot, weight_out, own_in_t, slopes_t) for c in range(CHUNKS)]
+    kept_cot = [[half[0] for half in halves]]
+    kept_result = [[both_parts(half[0], half[1], other_core(half[2])) for half in halves]]
+    cots = [passed_along(r) for r in kept_result[0]]
+
     other_slopes, other_in_t = token_slopes(x_own, other_in)
-    slopes, wouts, wins_t = (own_slopes, other_slopes), (weight_out, kept(other_out)), (own_in_t, other_in_t)
-
-    act_t, slopes_t = unit_parts(weight_in, x_rows)
-    hi, lo = spread_matrix(mixing)
-
-    columns = own // CHUNKS
-    kept_cot = []
-    kept_result = []
-    for turn_index in range(segments - 1):
-        results = [turn(cots[c], wouts, wins_t, slopes, c * columns, mixing) for c in range(CHUNKS)]
+    slopes, wouts, wins_t = (slopes_t, other_slopes), (weight_out, kept(other_out)), (own_in_t, other_in_t)
+    for turn_index in range(1, segments - 1):
+        results = [turn(at, cots[c], wouts, wins_t, slopes, c * columns, mixing) for c in range(CHUNKS)]
         kept_cot.append(cots)
         kept_result.append(results)
         cots = [passed_along(r) for r in results]
@@ -401,15 +456,15 @@
     mixture_in = mix(hi, lo, pieces_in, mixing)
     back_in = sent_out(mixture_in)
     back_out = sent_out(mix(hi, lo, pieces_out, mixture_in))
-    mixed_in = landed(back_in.reshape(units, D))
-    mixed_out = landed(back_out.reshape(units, D))
-
-    kept_result.append([turn(cots[c], wouts, wins_t, slopes, c * columns, mixed_in) for c in range(CHUNKS)])
+    mixed_in = landed(back_in.reshape(units, D), mixing)
+
+    kept_result.append([turn(at, cots[c], wouts, wins_t, slopes, c * columns, mixed_in) for c in range(CHUNKS)])
     result = summed(kept_result)
     width = D // 2
     mine = lax.dynamic_slice_in_dim(result, core * width, width, 0)
     theirs = other_core(lax.dynamic_slice_in_dim(result, (1 - core) * width, width, 0))
     dx = leaving(core_at, mine, theirs)
+    mixed_out = landed(back_out.reshape(units, D), dx)
     return dx[None], mixed_in[None, None], mixed_out[None, None]
 
 

time: 325 us -> 318 us (0.978)
  waiting for transfers between devices: 197 us -> 186 us
    all_to_all x4, waiting for transfers between devices: 185 us -> 177 us  [sent_out(): return lax.all_to_all(block, 'rep', split_axis=0, concat_axis=0, tiled=True)]
    pallas_call x0 -> x4, Pallas kernels: none -> 4.22 us  [the longest x2 4.07 us: first_turn(): pl.pallas_call(lambda *refs: first_turn_kernel(chunk, m, *refs), out_shap...]
    unnamed x68 -> x82, local copies, waits for them, and re-layouts: 18 us -> 22.1 us
    pallas_call x8 -> x6, Pallas kernels: 26.7 us -> 23.3 us  [turn(): pl.pallas_call(lambda *refs: turn_kernel(col0, *refs), out_shape=jax.Shap...]
  transfers between devices with their start and end apart: 15 -> 17, of which waited for: 7 -> 9; matrix products, arithmetic and copies ran while one was open for 0% -> 0% of each run, Pallas kernels for 15% -> 17%
where the time goes in v3:
time: 318 us; the launch traced here: 317 us
  waiting for transfers between devices  186 us (58%)
  Pallas kernels  60.2 us (19%)
  starting transfers between devices  44.2 us (14%)
  local copies, waits for them, and re-layouts  22.1 us (7%)
    all_to_all x4, waiting for transfers between devices, sent_out(): return lax.all_to_all(block, 'rep', split_axis=0, concat_axis=0, tiled=True)  177 us
    all_to_all x4, starting transfers between devices, sent_out(): return lax.all_to_all(block, 'rep', split_axis=0, concat_axis=0, tiled=True)  27.2 us
    pallas_call x6, Pallas kernels, turn(): pl.pallas_call(lambda *refs: turn_kernel(col0, *refs), out_shape=jax.Shap...  23.3 us
    unnamed x82, local copies, waits for them, and re-layouts  22.1 us
    ppermute x6, starting transfers between devices, passed_along(): lax.ppermute(shard, 'section', [(i, i - 1) for i in range(1, length)])  15.1 us
    pallas_call x2, Pallas kernels, mix(): pl.pallas_call(mix_kernel, grid=(rows // block,), out_shape=pltpu.HBM(pie...  10.9 us
  transfers between devices with their start and end apart: 17, of which 9 were waited for; matrix products, arithmetic and copies ran while one was open for 0% of the time, Pallas kernels for 17%

profile of v3, /device:TPU:16, one launch (start us, length us, event | category | flops | bytes accessed | tf_op | source)
XLA Modules:
  0.0 316.7 jit_solution(732670849902582842)
XLA Ops:
  8.5 2.6 unit_parts.1
  18.5 4.1 %collective-permute-start.9 = (bf16[768,128]{1,0:T(8,128)(2,1)S(1)}, bf16[768,128]{1,0:T(8,128)(2,1)S(1)}, u32[]{:S(2)}, u32[]{:S(2)}) collective-permute-start(bf16[768,128]{1,0:T(8,128)(2,1)S(1)} %both_parts.3), channel_id=1, source_target_pairs={{2,0},{4,2},{6,4},{3,1},{5,3},{7,5},{10,8},{12,10},{14,12},{11,9},... | collective-permute-start | bytes 589832 | tf_op jit(solution)/shard_map/ppermute | solution.py:393
  24.3 3.8 %token_slopes.1 = (f32[1536,256]{1,0:T(8,128)S(1)}, bf16[768,1536]{1,0:T(8,128)(2,1)S(1)}) custom-call(bf16[256,768]{1,0:T(8,128)(2,1)S(1)} %get-tuple-element.33.x_ref, bf16[1536,768]{1,0:T(8,128)(2,1)} %collective-permute-done.5.w_ref), custom_call_target="tpu_custom_call" | custom-call | flops 603979776 | bytes 6291456 | tf_op jit(solution)/shard_map/token_slopes/pallas_call | solution.py:137
  28.2 3.9 %turn.6 = bf16[768,128]{1,0:T(8,128)(2,1)S(1)} custom-call(s32[2]{0:T(128)S(1)} %pad_add_fusion.at.refs_0_, bf16[768,128]{1,0:T(8,128)(2,1)S(1)} %collective-permute-done.3.refs_1_, bf16[1536,768]{1,0:T(8,128)(2,1)S(1)} %bitcast.15, bf16[1536,768]{1,0:T(8,128)(2,1)S(1)} %kept.1.refs_3_, bf16[768,1536]{1,0:T(8,128)(2,1)S(1)} %get-tuple-element.27.refs_3_.refs_4_, ...), custom_call_target="tpu_custom_call" | custom-call | flops 1207959552 | bytes 11010048 | tf_op jit(solution)/shard_map/turn/pallas_call | solution.py:214
  34.2 3.9 %turn.8 = bf16[768,128]{1,0:T(8,128)(2,1)S(1)} custom-call(s32[2]{0:T(128)S(1)} %pad_add_fusion.at.refs_0_, bf16[768,128]{1,0:T(8,128)(2,1)S(1)} %collective-permute-done.9.refs_1_, bf16[1536,768]{1,0:T(8,128)(2,1)S(1)} %bitcast.16, bf16[1536,768]{1,0:T(8,128)(2,1)S(1)} %kept.1.refs_3_, bf16[768,1536]{1,0:T(8,128)(2,1)S(1)} %get-tuple-element.27.refs_3_.refs_4_, ...), custom_call_target="tpu_custom_call" | custom-call | flops 1207959552 | bytes 11010048 | tf_op jit(solution)/shard_map/turn/pallas_call | solution.py:214
  40.3 3.9 %turn.7 = bf16[768,128]{1,0:T(8,128)(2,1)S(1)} custom-call(s32[2]{0:T(128)S(1)} %pad_add_fusion.at.refs_0_, bf16[768,128]{1,0:T(8,128)(2,1)S(1)} %collective-permute-done.6.refs_1_, bf16[1536,768]{1,0:T(8,128)(2,1)S(1)} %bitcast.17, bf16[1536,768]{1,0:T(8,128)(2,1)S(1)} %kept.1.refs_3_, bf16[768,1536]{1,0:T(8,128)(2,1)S(1)} %get-tuple-element.27.refs_3_.refs_4_, ...), custom_call_target="tpu_custom_call" | custom-call | flops 1207959552 | bytes 11010048 | tf_op jit(solution)/shard_map/turn/pallas_call | solution.py:214
  46.5 3.9 %turn.9 = bf16[768,128]{1,0:T(8,128)(2,1)S(1)} custom-call(s32[2]{0:T(128)S(1)} %pad_add_fusion.at.refs_0_, bf16[768,128]{1,0:T(8,128)(2,1)S(1)} %collective-permute-done.10.refs_1_, bf16[1536,768]{1,0:T(8,128)(2,1)S(1)} %bitcast.18, bf16[1536,768]{1,0:T(8,128)(2,1)S(1)} %kept.1.refs_3_, bf16[768,1536]{1,0:T(8,128)(2,1)S(1)} %get-tuple-element.27.refs_3_.refs_4_, ...), custom_call_target="tpu_custom_call" | custom-call | flops 1207959552 | bytes 11010048 | tf_op jit(solution)/shard_map/turn/pallas_call | solution.py:214
  52.9 5.4 %collective-permute-done.11.refs_1_ = bf16[768,128]{1,0:T(8,128)(2,1)S(1)} collective-permute-done((bf16[768,128]{1,0:T(8,128)(2,1)S(1)}, bf16[768,128]{1,0:T(8,128)(2,1)S(1)}, u32[]{:S(2)}, u32[]{:S(2)}) %collective-permute-start.11) | collective-permute-done | bytes 196640 | tf_op jit(solution)/shard_map/ppermute | solution.py:393
  60.8 3.7 %update_in.1 = bf16[1536,768]{1,0:T(8,128)(2,1)} custom-call(f32[1536,512]{1,0:T(8,128)S(1)} %get-tuple-element.28.refs_4_.refs_6_.s_ref, bf16[768,512]{1,0:T(8,128)(2,1)S(1)} %all_gather.3.c_ref, bf16[512,768]{1,0:T(8,128)(2,1)S(1)} %get-tuple-element.26.x_ref, bf16[1536,768]{1,0:T(8,128)(2,1)S(1)} %bitcast.19, bf16[1536,768]{1,0:T(8,128)(2,1)S(1)} %bitcast.26), custom_call_target="tpu_custom_call" | custom-call | flops 2415919104 | bytes 10223616 | tf_op jit(solution)/shard_map/update_in/pallas_call | solution.py:290
  64.5 9.7 %all-to-all-start = ((bf16[32,48,768]{2,1,0:T(8,128)(2,1)}), bf16[32,48,768]{2,1,0:T(8,128)(2,1)}, u32[]{:S(2)}, u32[]{:S(2)}) async-start(bf16[32,48,768]{2,1,0:T(8,128)(2,1)} %bitcast.31), calls=%async_computation | async-start | bytes 4718592 | tf_op jit(solution)/shard_map/all_to_all | solution.py:401
  78.4 2.4 update_out.1
  80.8 49.3 %all-to-all-done.u_ref = bf16[32,48,768]{2,1,0:T(8,128)(2,1)} async-done(((bf16[32,48,768]{2,1,0:T(8,128)(2,1)}), bf16[32,48,768]{2,1,0:T(8,128)(2,1)}, u32[]{:S(2)}, u32[]{:S(2)}) %all-to-all-start) | async-done | bytes 2359328 | tf_op jit(solution)/shard_map/all_to_all | solution.py:401
  130.2 5.8 %all-to-all-start.2 = ((bf16[32,48,768]{2,1,0:T(8,128)(2,1)}), bf16[32,48,768]{2,1,0:T(8,128)(2,1)}, u32[]{:S(2)}, u32[]{:S(2)}) async-start(bf16[32,48,768]{2,1,0:T(8,128)(2,1)} %bitcast.30), calls=%async_computation.2 | async-start | bytes 4718592 | tf_op jit(solution)/shard_map/all_to_all | solution.py:401
  136.7 5.4 %mix.2.after_ref = bf16[32,48,768]{2,1,0:T(8,128)(2,1)} custom-call(bf16[512,512]{1,0:T(8,128)(2,1)S(1)} %get-tuple-element.37.hi_ref, bf16[512,512]{1,0:T(8,128)(2,1)S(1)} %get-tuple-element.38.lo_ref, bf16[32,48,768]{2,1,0:T(8,128)(2,1)} %all-to-all-done.u_ref, f32[32,32]{1,0:T(8,128)S(1)} %copy-done.32), custom_call_target="tpu_custom_call" | custom-call | flops 2415919104 | bytes 5767168 | tf_op jit(solution)/shard_map/mix/pallas_call | solution.py:315
  143.7 47.8 %all-to-all-done.2.u_ref = bf16[32,48,768]{2,1,0:T(8,128)(2,1)} async-done(((bf16[32,48,768]{2,1,0:T(8,128)(2,1)}), bf16[32,48,768]{2,1,0:T(8,128)(2,1)}, u32[]{:S(2)}, u32[]{:S(2)}) %all-to-all-start.2) | async-done | bytes 2359328 | tf_op jit(solution)/shard_map/all_to_all | solution.py:401
  191.5 5.6 %all-to-all-start.1 = ((bf16[32,48,768]{2,1,0:T(8,128)(2,1)}), bf16[32,48,768]{2,1,0:T(8,128)(2,1)}, u32[]{:S(2)}, u32[]{:S(2)}) async-start(bf16[32,48,768]{2,1,0:T(8,128)(2,1)} %mix.2.after_ref), calls=%async_computation.1 | async-start | bytes 4718592 | tf_op jit(solution)/shard_map/all_to_all | solution.py:401
  200.8 5.5 %mix.3 = bf16[32,48,768]{2,1,0:T(8,128)(2,1)} custom-call(bf16[512,512]{1,0:T(8,128)(2,1)S(1)} %copy-done.38, bf16[512,512]{1,0:T(8,128)(2,1)S(1)} %copy-done.40, bf16[32,48,768]{2,1,0:T(8,128)(2,1)} %all-to-all-done.2.u_ref, bf16[32,48,768]{2,1,0:T(8,128)(2,1)S(1)} %copy-done.14), custom_call_target="tpu_custom_call" | custom-call | flops 2415919104 | bytes 5767168 | tf_op jit(solution)/shard_map/mix/pallas_call | solution.py:315
  206.3 46.1 %all-to-all-done.1 = bf16[32,48,768]{2,1,0:T(8,128)(2,1)} async-done(((bf16[32,48,768]{2,1,0:T(8,128)(2,1)}), bf16[32,48,768]{2,1,0:T(8,128)(2,1)}, u32[]{:S(2)}, u32[]{:S(2)}) %all-to-all-start.1) | async-done | bytes 2359328 | tf_op jit(solution)/shard_map/all_to_all | solution.py:401
  252.5 6.1 %all-to-all-start.3 = ((bf16[32,48,768]{2,1,0:T(8,128)(2,1)}), bf16[32,48,768]{2,1,0:T(8,128)(2,1)}, u32[]{:S(2)}, u32[]{:S(2)}) async-start(bf16[32,48,768]{2,1,0:T(8,128)(2,1)} %mix.3), calls=%async_computation.3 | async-start | bytes 4718592 | tf_op jit(solution)/shard_map/all_to_all | solution.py:401
  258.7 2.6 landed.2.refs_8_
  269.0 3.9 %turn.10 = bf16[768,128]{1,0:T(8,128)(2,1)S(1)} custom-call(s32[2]{0:T(128)S(1)} %copy-done.36, bf16[768,128]{1,0:T(8,128)(2,1)S(1)} %collective-permute-done.7.refs_1_, bf16[1536,768]{1,0:T(8,128)(2,1)S(1)} %bitcast.21, bf16[1536,768]{1,0:T(8,128)(2,1)S(1)} %copy-done.6, bf16[768,1536]{1,0:T(8,128)(2,1)S(1)} %copy-done.4, bf16[768,1536]{1,0:T(8,128)(2,1)S(1)} %copy-done.8, ...), custom_call_target="tpu_custom_call" | custom-call | flops 1207959552 | bytes 11010048 | tf_op jit(solution)/shard_map/turn/pallas_call | solution.py:214
  272.9 3.9 %turn.11 = bf16[768,128]{1,0:T(8,128)(2,1)S(1)} custom-call(s32[2]{0:T(128)S(1)} %copy-done.36, bf16[768,128]{1,0:T(8,128)(2,1)S(1)} %collective-permute-done.11.refs_1_, bf16[1536,768]{1,0:T(8,128)(2,1)S(1)} %bitcast.22, bf16[1536,768]{1,0:T(8,128)(2,1)S(1)} %copy-done.6, bf16[768,1536]{1,0:T(8,128)(2,1)S(1)} %copy-done.4, bf16[768,1536]{1,0:T(8,128)(2,1)S(1)} %copy-done.8, ...), custom_call_target="tpu_custom_call" | custom-call | flops 1207959552 | bytes 11010048 | tf_op jit(solution)/shard_map/turn/pallas_call | solution.py:214
  279.4 33.6 %all-to-all-done.3 = bf16[32,48,768]{2,1,0:T(8,128)(2,1)} async-done(((bf16[32,48,768]{2,1,0:T(8,128)(2,1)}), bf16[32,48,768]{2,1,0:T(8,128)(2,1)}, u32[]{:S(2)}, u32[]{:S(2)}) %all-to-all-start.3) | async-done | bytes 2359328 | tf_op jit(solution)/shard_map/all_to_all | solution.py:401
  314.0 2.5 landed.3
  (121 shorter events, 49.7 us)
Async XLA Ops:
  0.6 2.0 collective-permute-start
  0.7 2.5 collective-permute-start.1
  3.2 19.4 %collective-permute-start.4 = (bf16[1536,768]{1,0:T(8,128)(2,1)}, bf16[1536,768]{1,0:T(8,128)(2,1)}, u32[]{:S(2)}, u32[]{:S(2)}) collective-permute-start(bf16[1536,768]{1,0:T(8,128)(2,1)} %bitcast.12), channel_id=1, source_target_pairs={{0,1},{1,0},{2,3},{3,2},{4,5},{5,4},{6,7},{7,6},{8,9},{9,8},{10,11... | collective-permute-start | bytes 7077896 | tf_op jit(solution)/shard_map/ppermute | solution.py:397
  3.4 21.0 %collective-permute-start.5 = (bf16[1536,768]{1,0:T(8,128)(2,1)}, bf16[1536,768]{1,0:T(8,128)(2,1)}, u32[]{:S(2)}, u32[]{:S(2)}) collective-permute-start(bf16[1536,768]{1,0:T(8,128)(2,1)} %bitcast.24), channel_id=1, source_target_pairs={{0,1},{1,0},{2,3},{3,2},{4,5},{5,4},{6,7},{7,6},{8,9},{9,8},{10,11... | collective-permute-start | bytes 7077896 | tf_op jit(solution)/shard_map/ppermute | solution.py:397
  5.8 40.7 %copy-start.35 = (s32[2]{0:T(128)}, s32[2]{0:T(128)S(1)}, u32[]{:S(2)}) copy-start(s32[2]{0:T(128)S(1)} %pad_add_fusion.at.refs_0_) | copy-start | bytes 28
  11.1 35.4 %copy-start.3 = (bf16[768,1536]{1,0:T(8,128)(2,1)}, bf16[768,1536]{1,0:T(8,128)(2,1)S(1)}, u32[]{:S(2)}) copy-start(bf16[768,1536]{1,0:T(8,128)(2,1)S(1)} %get-tuple-element.27.refs_3_.refs_4_) | copy-start | bytes 7077892
  13.2 2.7 collective-permute-start.2
  15.5 2.9 collective-permute-start.8
  16.0 12.1 %collective-permute-start.3 = (bf16[768,128]{1,0:T(8,128)(2,1)S(1)}, bf16[768,128]{1,0:T(8,128)(2,1)S(1)}, u32[]{:S(2)}, u32[]{:S(2)}) collective-permute-start(bf16[768,128]{1,0:T(8,128)(2,1)S(1)} %both_parts.2), channel_id=1, source_target_pairs={{2,0},{4,2},{6,4},{3,1},{5,3},{7,5},{10,8},{12,10},{14,12},{11,9},... | collective-permute-start | bytes 589832 | tf_op jit(solution)/shard_map/ppermute | solution.py:393
  18.5 15.7 %collective-permute-start.9 = (bf16[768,128]{1,0:T(8,128)(2,1)S(1)}, bf16[768,128]{1,0:T(8,128)(2,1)S(1)}, u32[]{:S(2)}, u32[]{:S(2)}) collective-permute-start(bf16[768,128]{1,0:T(8,128)(2,1)S(1)} %both_parts.3), channel_id=1, source_target_pairs={{2,0},{4,2},{6,4},{3,1},{5,3},{7,5},{10,8},{12,10},{14,12},{11,9},... | collective-permute-start | bytes 589832 | tf_op jit(solution)/shard_map/ppermute | solution.py:393
  24.3 22.2 %copy-start.5 = (bf16[1536,768]{1,0:T(8,128)(2,1)}, bf16[1536,768]{1,0:T(8,128)(2,1)S(1)}, u32[]{:S(2)}) copy-start(bf16[1536,768]{1,0:T(8,128)(2,1)S(1)} %kept.1.refs_3_) | copy-start | bytes 7077892
  28.1 18.4 %copy-start.7 = (bf16[768,1536]{1,0:T(8,128)(2,1)}, bf16[768,1536]{1,0:T(8,128)(2,1)S(1)}, u32[]{:S(2)}) copy-start(bf16[768,1536]{1,0:T(8,128)(2,1)S(1)} %get-tuple-element.35.refs_5_) | copy-start | bytes 7077892
  28.1 18.4 %copy-start.9 = (f32[1536,256]{1,0:T(8,128)}, f32[1536,256]{1,0:T(8,128)S(1)}, u32[]{:S(2)}) copy-start(f32[1536,256]{1,0:T(8,128)S(1)} %get-tuple-element.36.refs_7_) | copy-start | bytes 4718596
  32.1 8.3 %collective-permute-start.6 = (bf16[768,128]{1,0:T(8,128)(2,1)S(1)}, bf16[768,128]{1,0:T(8,128)(2,1)S(1)}, u32[]{:S(2)}, u32[]{:S(2)}) collective-permute-start(bf16[768,128]{1,0:T(8,128)(2,1)S(1)} %turn.6), channel_id=1, source_target_pairs={{2,0},{4,2},{6,4},{3,1},{5,3},{7,5},{10,8},{12,10},{14,12},{11,9},... | collective-permute-start | bytes 589832 | tf_op jit(solution)/shard_map/ppermute | solution.py:393
  38.1 8.4 %collective-permute-start.10 = (bf16[768,128]{1,0:T(8,128)(2,1)S(1)}, bf16[768,128]{1,0:T(8,128)(2,1)S(1)}, u32[]{:S(2)}, u32[]{:S(2)}) collective-permute-start(bf16[768,128]{1,0:T(8,128)(2,1)S(1)} %turn.8), channel_id=1, source_target_pairs={{2,0},{4,2},{6,4},{3,1},{5,3},{7,5},{10,8},{12,10},{14,12},{11,9},... | collective-permute-start | bytes 589832 | tf_op jit(solution)/shard_map/ppermute | solution.py:393
  44.3 8.5 %collective-permute-start.7 = (bf16[768,128]{1,0:T(8,128)(2,1)S(1)}, bf16[768,128]{1,0:T(8,128)(2,1)S(1)}, u32[]{:S(2)}, u32[]{:S(2)}) collective-permute-start(bf16[768,128]{1,0:T(8,128)(2,1)S(1)} %turn.7), channel_id=1, source_target_pairs={{2,0},{4,2},{6,4},{3,1},{5,3},{7,5},{10,8},{12,10},{14,12},{11,9},... | collective-permute-start | bytes 589832 | tf_op jit(solution)/shard_map/ppermute | solution.py:393
  50.4 14.0 %copy-start.26 = (bf16[768,128]{1,0:T(8,128)(2,1)}, bf16[768,128]{1,0:T(8,128)(2,1)S(1)}, u32[]{:S(2)}) copy-start(bf16[768,128]{1,0:T(8,128)(2,1)S(1)} %turn.9) | copy-start | bytes 589828
  50.4 10.3 %copy-start.16 = (bf16[1,1,1536,768]{3,2,1,0:T(8,128)(2,1)S(1)}, bf16[1,1,1536,768]{3,2,1,0:T(8,128)(2,1)}, u32[]{:S(2)}) copy-start(bf16[1,1,1536,768]{3,2,1,0:T(8,128)(2,1)} %param.7) | copy-start | bytes 7077892
  50.5 7.8 %collective-permute-start.11 = (bf16[768,128]{1,0:T(8,128)(2,1)S(1)}, bf16[768,128]{1,0:T(8,128)(2,1)S(1)}, u32[]{:S(2)}, u32[]{:S(2)}) collective-permute-start(bf16[768,128]{1,0:T(8,128)(2,1)S(1)} %turn.9), channel_id=1, source_target_pairs={{2,0},{4,2},{6,4},{3,1},{5,3},{7,5},{10,8},{12,10},{14,12},{11,9},... | collective-permute-start | bytes 589832 | tf_op jit(solution)/shard_map/ppermute | solution.py:393
  64.5 65.7 %all-to-all-start = ((bf16[32,48,768]{2,1,0:T(8,128)(2,1)}), bf16[32,48,768]{2,1,0:T(8,128)(2,1)}, u32[]{:S(2)}, u32[]{:S(2)}) async-start(bf16[32,48,768]{2,1,0:T(8,128)(2,1)} %bitcast.31), calls=%async_computation | async-start | bytes 4718592 | tf_op jit(solution)/shard_map/all_to_all | solution.py:401
  130.2 61.3 %all-to-all-start.2 = ((bf16[32,48,768]{2,1,0:T(8,128)(2,1)}), bf16[32,48,768]{2,1,0:T(8,128)(2,1)}, u32[]{:S(2)}, u32[]{:S(2)}) async-start(bf16[32,48,768]{2,1,0:T(8,128)(2,1)} %bitcast.30), calls=%async_computation.2 | async-start | bytes 4718592 | tf_op jit(solution)/shard_map/all_to_all | solution.py:401
  191.5 61.0 %all-to-all-start.1 = ((bf16[32,48,768]{2,1,0:T(8,128)(2,1)}), bf16[32,48,768]{2,1,0:T(8,128)(2,1)}, u32[]{:S(2)}, u32[]{:S(2)}) async-start(bf16[32,48,768]{2,1,0:T(8,128)(2,1)} %mix.2.after_ref), calls=%async_computation.1 | async-start | bytes 4718592 | tf_op jit(solution)/shard_map/all_to_all | solution.py:401
  252.5 60.5 %all-to-all-start.3 = ((bf16[32,48,768]{2,1,0:T(8,128)(2,1)}), bf16[32,48,768]{2,1,0:T(8,128)(2,1)}, u32[]{:S(2)}, u32[]{:S(2)}) async-start(bf16[32,48,768]{2,1,0:T(8,128)(2,1)} %mix.3), calls=%async_computation.3 | async-start | bytes 4718592 | tf_op jit(solution)/shard_map/all_to_all | solution.py:401
  277.0 1.5 collective-permute-start.12
  (34 other events, 101.8 us)

commit v4 on v3

--- a/solution.py
+++ b/solution.py
@@ -145,36 +145,42 @@
     )(x_rows, weight_in)
 
 
-def kept_kernel(w_ref, o_ref, sems):
-    copy = pltpu.make_async_copy(w_ref, o_ref, sems.at[0])
-    copy.start()
-    copy.wait()
-
-
-def kept(array):
+def kept_kernel(*refs):
+    count = len(refs) // 2
+    sems = refs[-1]
+    copies = [pltpu.make_async_copy(refs[i], refs[count + i], sems.at[i]) for i in range(count)]
+    for copy in copies:
+        copy.start()
+    for copy in copies:
+        copy.wait()
+
+
+def kept(*arrays, mib=20):
     return pl.pallas_call(
         kept_kernel,
-        out_shape=pltpu.VMEM(array.shape, BF),
-        in_specs=[ANY],
-        out_specs=VMEM,
-        scratch_shapes=[pltpu.SemaphoreType.DMA((1,))],
-        compiler_params=params(),
-        cost_estimate=cost(0, 4 * array.size),
+        out_shape=[pltpu.VMEM(array.shape, BF) for array in arrays],
+        in_specs=[ANY] * len(arrays),
+        out_specs=[VMEM] * len(arrays),
+        scratch_shapes=[pltpu.SemaphoreType.DMA((len(arrays),))],
+        compiler_params=params(mib),
+        cost_estimate=cost(0, 4 * sum(array.size for array in arrays)),
         name="kept",
-    )(array)
-
-
-def unit_parts_kernel(w_ref, x_ref, a_ref, s_ref, t_ref):
+    )(*arrays)
+
+
+def unit_parts_kernel(core, w_ref, x_ref, a_ref, s_ref, t_ref, own_ref):
+    own = own_ref.shape[1]
     x = x_ref[...]
     for at in blocks(w_ref.shape[0]):
         weight = w_ref[at, :]
         values, slopes = gelu_parts(nt(weight, x) * in_scale)
         a_ref[at, :] = values.astype(BF)
         s_ref[at, :] = slopes
+        own_ref[at, :] = jnp.where(core[0] == 0, slopes[:, :own], slopes[:, own:])
         t_ref[:, at] = jnp.transpose(weight)
 
 
-def unit_parts(weight_in, x_rows):
+def unit_parts(core, weight_in, x_rows):
     m, h = x_rows.shape[0], weight_in.shape[0]
     return pl.pallas_call(
         unit_parts_kernel,
@@ -182,45 +188,42 @@
             jax.ShapeDtypeStruct((h, m), BF),
             jax.ShapeDtypeStruct((h, m), F32),
             jax.ShapeDtypeStruct((D, h), BF),
+            jax.ShapeDtypeStruct((h, m // 2), F32),
         ],
-        in_specs=[VMEM, VMEM],
-        out_specs=[VMEM] * 3,
+        in_specs=[SMEM, VMEM, VMEM],
+        out_specs=[VMEM] * 4,
         compiler_params=params(),
         cost_estimate=cost(2 * m * h * D, 2 * h * D + 6 * m * h, 2 * m * h),
         name="unit_parts",
-    )(weight_in, x_rows)
-
-
-def turn_kernel(col0, at_ref, c_ref, wo0_ref, wo1_ref, wt0_ref, wt1_ref, s0_ref, s1_ref, after_ref, o_ref, delta):
+    )(core, weight_in, x_rows)
+
+
+def turn_kernel(col0, c_ref, wo0_ref, wo1_ref, wt0_ref, wt1_ref, s0_ref, s1_ref, after_ref, o_ref, delta):
     cot = c_ref[...]
     m = cot.shape[1]
-    own = pl.ds(pl.multiple_of(at_ref[0] * s1_ref.shape[1] + col0, m), m)
     branch = None
-    for wo_ref, wt_ref, s_ref, lane in (
-        (wo0_ref, wt0_ref, s0_ref, own),
-        (wo1_ref, wt1_ref, s1_ref, pl.ds(col0, m)),
-    ):
+    for wo_ref, wt_ref, s_ref in ((wo0_ref, wt0_ref, s0_ref), (wo1_ref, wt1_ref, s1_ref)):
         for at in blocks(wo_ref.shape[0]):
             backward = nn(wo_ref[at, :], cot) * out_scale
-            delta[at, :] = (s_ref[at, lane] * backward).astype(BF)
+            delta[at, :] = (s_ref[at, pl.ds(col0, m)] * backward).astype(BF)
         partial = (nn(wt_ref[...], delta[...]) * in_scale).astype(BF).astype(F32)
         branch = partial if branch is None else branch + partial
     o_ref[...] = (cot.astype(F32) + branch).astype(BF)
 
 
-def turn(at, cot, wouts, wins_t, slopes, col0, after):
+def turn(cot, wouts, wins_t, slopes, col0, after):
     m = cot.shape[1]
     h = wouts[0].shape[0]
     return pl.pallas_call(
         lambda *refs: turn_kernel(col0, *refs),
         out_shape=jax.ShapeDtypeStruct((D, m), BF),
-        in_specs=[SMEM] + [VMEM] * 7 + [ANY],
+        in_specs=[VMEM] * 7 + [ANY],
         out_specs=VMEM,
         scratch_shapes=[pltpu.VMEM((h, m), BF)],
         compiler_params=params(),
         cost_estimate=cost(8 * m * h * D, 8 * h * D + 8 * m * h),
         name="turn",
-    )(at, cot, wouts[0], wouts[1], wins_t[0], wins_t[1], slopes[0], slopes[1], after)
+    )(cot, wouts[0], wouts[1], wins_t[0], wins_t[1], slopes[0], slopes[1], after)
 
 
 def leaving_kernel(core, mine_ref, theirs_ref, o_ref):
@@ -416,24 +419,28 @@
     last = (segment_index == segments - 1).astype(jnp.int32)
     other_x = other_core(inputs[0])
     other_dy = other_core(loss_grad)
-    late_in, late_out, other_x, other_dy = lax.optimization_barrier((weight_in, weight_out, other_x, other_dy))
+    own_x, own_dy, own_in, own_out = kept(inputs[0], loss_grad, weight_in, weight_out, mib=54)
+    late_in, late_out, other_x, other_dy, own_x = lax.optimization_barrier(
+        (weight_in, weight_out, other_x, other_dy, own_x)
+    )
     other_in = other_core(late_in)
     other_out = other_core(late_out)
     at = jnp.stack([core.astype(jnp.int32), last])
-    x_rows, x_own, cot = entering(at, inputs[0], other_x, loss_grad, other_dy)
-    act_t, slopes_t, own_in_t = unit_parts(weight_in, x_rows)
+    x_rows, x_own, cot = entering(at, own_x, other_x, own_dy, other_dy)
+    act_t, slopes_t, own_in_t, own_slopes = unit_parts(core_at, own_in, x_rows)
     hi, lo = spread_matrix(mixing)
 
     columns = own // CHUNKS
-    halves = [first_turn(at, c, cot, weight_out, own_in_t, slopes_t) for c in range(CHUNKS)]
+    halves = [first_turn(at, c, cot, own_out, own_in_t, slopes_t) for c in range(CHUNKS)]
     kept_cot = [[half[0] for half in halves]]
     kept_result = [[both_parts(half[0], half[1], other_core(half[2])) for half in halves]]
     cots = [passed_along(r) for r in kept_result[0]]
 
+    other_in, other_out = kept(other_in, other_out)
     other_slopes, other_in_t = token_slopes(x_own, other_in)
-    slopes, wouts, wins_t = (slopes_t, other_slopes), (weight_out, kept(other_out)), (own_in_t, other_in_t)
+    slopes, wouts, wins_t = (own_slopes, other_slopes), (own_out, other_out), (own_in_t, other_in_t)
     for turn_index in range(1, segments - 1):
-        results = [turn(at, cots[c], wouts, wins_t, slopes, c * columns, mixing) for c in range(CHUNKS)]
+        results = [turn(cots[c], wouts, wins_t, slopes, c * columns, mixing) for c in range(CHUNKS)]
         kept_cot.append(cots)
         kept_result.append(results)
         cots = [passed_along(r) for r in results]
@@ -449,22 +456,22 @@
         return jnp.concatenate(parts, axis=1)
 
     cot_t = lax.all_gather(summed(kept_cot), "tp", axis=1, tiled=True)
-    updated_in = update_in(slopes_t, cot_t, x_rows, weight_out, weight_in)
+    updated_in = update_in(slopes_t, cot_t, x_rows, own_out, own_in)
     pieces_in = sent_out(updated_in.reshape(replicas, units // replicas, D))
-    updated_out = update_out(act_t, cot_t, weight_out)
+    updated_out = update_out(act_t, cot_t, own_out)
     pieces_out = sent_out(updated_out.reshape(replicas, units // replicas, D))
     mixture_in = mix(hi, lo, pieces_in, mixing)
     back_in = sent_out(mixture_in)
     back_out = sent_out(mix(hi, lo, pieces_out, mixture_in))
     mixed_in = landed(back_in.reshape(units, D), mixing)
 
-    kept_result.append([turn(at, cots[c], wouts, wins_t, slopes, c * columns, mixed_in) for c in range(CHUNKS)])
+    kept_result.append([turn(cots[c], wouts, wins_t, slopes, c * columns, mixed_in) for c in range(CHUNKS)])
     result = summed(kept_result)
     width = D // 2
     mine = lax.dynamic_slice_in_dim(result, core * width, width, 0)
     theirs = other_core(lax.dynamic_slice_in_dim(result, (1 - core) * width, width, 0))
     dx = leaving(core_at, mine, theirs)
-    mixed_out = landed(back_out.reshape(units, D), dx)
+    mixed_out = landed(back_out.reshape(units, D), dx[:16, :128])
     return dx[None], mixed_in[None, None], mixed_out[None, None]
 
 

time: 318 us -> 316 us (level)
  local copies, waits for them, and re-layouts: 22.1 us -> 18 us
    all_to_all x4, waiting for transfers between devices: 177 us -> 182 us  [sent_out(): return lax.all_to_all(block, 'rep', split_axis=0, concat_axis=0, tiled=True)]
    unnamed x82 -> x68, local copies, waits for them, and re-layouts: 22.1 us -> 17.3 us
    pallas_call x1 -> x2, Pallas kernels: 1.67 us -> 5.06 us  [kept(): pl.pallas_call(kept_kernel, out_shape=[pltpu.VMEM(array.shape, BF) for ar...]
    pallas_call x6, Pallas kernels: 23.3 us -> 20 us  [turn(): pl.pallas_call(lambda *refs: turn_kernel(col0, *refs), out_shape=jax.Shap...]
  transfers between devices with their start and end apart: 17 -> 17, of which waited for: 9 -> 6; matrix products, arithmetic and copies ran while one was open for 0% -> 0% of each run, Pallas kernels for 17% -> 16%
where the time goes in v4:
time: 316 us; the launch traced here: 315 us
  waiting for transfers between devices  189 us (60%)
  Pallas kernels  57.7 us (18%)
  starting transfers between devices  45.4 us (14%)
  local copies, waits for them, and re-layouts  18 us (6%)
    all_to_all x4, waiting for transfers between devices, sent_out(): return lax.all_to_all(block, 'rep', split_axis=0, concat_axis=0, tiled=True)  182 us
    all_to_all x4, starting transfers between devices, sent_out(): return lax.all_to_all(block, 'rep', split_axis=0, concat_axis=0, tiled=True)  27 us
    pallas_call x6, Pallas kernels, turn(): pl.pallas_call(lambda *refs: turn_kernel(col0, *refs), out_shape=jax.Shap...  20 us
    unnamed x68, local copies, waits for them, and re-layouts  17.3 us
    ppermute x6, starting transfers between devices, passed_along(): lax.ppermute(shard, 'section', [(i, i - 1) for i in range(1, length)])  16.5 us
    pallas_call x2, Pallas kernels, mix(): pl.pallas_call(mix_kernel, grid=(rows // block,), out_shape=pltpu.HBM(pie...  10.9 us
  transfers between devices with their start and end apart: 17, of which 6 were waited for; matrix products, arithmetic and copies ran while one was open for 0% of the time, Pallas kernels for 16%

profile of v4, /device:TPU:16, one launch (start us, length us, event | category | flops | bytes accessed | tf_op | source)
XLA Modules:
  0.0 314.6 jit_solution(10661468169966023978)
XLA Ops:
  1.2 2.7 kept.2
  10.2 2.6 unit_parts.1
  20.2 4.3 %collective-permute-start.9 = (bf16[768,128]{1,0:T(8,128)(2,1)S(1)}, bf16[768,128]{1,0:T(8,128)(2,1)S(1)}, u32[]{:S(2)}, u32[]{:S(2)}) collective-permute-start(bf16[768,128]{1,0:T(8,128)(2,1)S(1)} %both_parts.3), channel_id=1, source_target_pairs={{2,0},{4,2},{6,4},{3,1},{5,3},{7,5},{10,8},{12,10},{14,12},{11,9},... | collective-permute-start | bytes 589832 | tf_op jit(solution)/shard_map/ppermute | solution.py:396
  28.3 3.3 %turn.6 = bf16[768,128]{1,0:T(8,128)(2,1)S(1)} custom-call(bf16[768,128]{1,0:T(8,128)(2,1)S(1)} %collective-permute-done.3.refs_0_, bf16[1536,768]{1,0:T(8,128)(2,1)S(1)} %get-tuple-element.37.refs_2_.refs_1_.wo_ref.w_ref, bf16[1536,768]{1,0:T(8,128)(2,1)S(1)} %get-tuple-element.47.refs_2_, bf16[768,1536]{1,0:T(8,128)(2,1)S(1)} %get-tuple-element.40.refs_3_, ...), custom_call_target="tpu_custom_call" | custom-call | flops 1207959552 | bytes 11010048 | tf_op jit(solution)/shard_map/turn/pallas_call | solution.py:217
  33.5 3.3 %turn.8 = bf16[768,128]{1,0:T(8,128)(2,1)S(1)} custom-call(bf16[768,128]{1,0:T(8,128)(2,1)S(1)} %collective-permute-done.9.refs_0_, bf16[1536,768]{1,0:T(8,128)(2,1)S(1)} %get-tuple-element.37.refs_2_.refs_1_.wo_ref.w_ref, bf16[1536,768]{1,0:T(8,128)(2,1)S(1)} %get-tuple-element.47.refs_2_, bf16[768,1536]{1,0:T(8,128)(2,1)S(1)} %get-tuple-element.40.refs_3_, ...), custom_call_target="tpu_custom_call" | custom-call | flops 1207959552 | bytes 11010048 | tf_op jit(solution)/shard_map/turn/pallas_call | solution.py:217
  36.9 3.7 %collective-permute-start.10 = (bf16[768,128]{1,0:T(8,128)(2,1)S(1)}, bf16[768,128]{1,0:T(8,128)(2,1)S(1)}, u32[]{:S(2)}, u32[]{:S(2)}) collective-permute-start(bf16[768,128]{1,0:T(8,128)(2,1)S(1)} %turn.8), channel_id=1, source_target_pairs={{2,0},{4,2},{6,4},{3,1},{5,3},{7,5},{10,8},{12,10},{14,12},{11,9},... | collective-permute-start | bytes 589832 | tf_op jit(solution)/shard_map/ppermute | solution.py:396
  40.6 3.3 %turn.7 = bf16[768,128]{1,0:T(8,128)(2,1)S(1)} custom-call(bf16[768,128]{1,0:T(8,128)(2,1)S(1)} %collective-permute-done.6.refs_0_, bf16[1536,768]{1,0:T(8,128)(2,1)S(1)} %get-tuple-element.37.refs_2_.refs_1_.wo_ref.w_ref, bf16[1536,768]{1,0:T(8,128)(2,1)S(1)} %get-tuple-element.47.refs_2_, bf16[768,1536]{1,0:T(8,128)(2,1)S(1)} %get-tuple-element.40.refs_3_, ...), custom_call_target="tpu_custom_call" | custom-call | flops 1207959552 | bytes 11010048 | tf_op jit(solution)/shard_map/turn/pallas_call | solution.py:217
  45.9 3.3 %turn.9 = bf16[768,128]{1,0:T(8,128)(2,1)S(1)} custom-call(bf16[768,128]{1,0:T(8,128)(2,1)S(1)} %collective-permute-done.10.refs_0_, bf16[1536,768]{1,0:T(8,128)(2,1)S(1)} %get-tuple-element.37.refs_2_.refs_1_.wo_ref.w_ref, bf16[1536,768]{1,0:T(8,128)(2,1)S(1)} %get-tuple-element.47.refs_2_, bf16[768,1536]{1,0:T(8,128)(2,1)S(1)} %get-tuple-element.40.refs_3_, ...), custom_call_target="tpu_custom_call" | custom-call | flops 1207959552 | bytes 11010048 | tf_op jit(solution)/shard_map/turn/pallas_call | solution.py:217
  51.7 5.2 %collective-permute-done.11.refs_0_ = bf16[768,128]{1,0:T(8,128)(2,1)S(1)} collective-permute-done((bf16[768,128]{1,0:T(8,128)(2,1)S(1)}, bf16[768,128]{1,0:T(8,128)(2,1)S(1)}, u32[]{:S(2)}, u32[]{:S(2)}) %collective-permute-start.11) | collective-permute-done | bytes 196640 | tf_op jit(solution)/shard_map/ppermute | solution.py:396
  57.1 2.6 all_gather.3.c_ref
  59.7 3.7 %update_in.1 = bf16[1536,768]{1,0:T(8,128)(2,1)} custom-call(f32[1536,512]{1,0:T(8,128)S(1)} %get-tuple-element.41.refs_4_.s_ref, bf16[768,512]{1,0:T(8,128)(2,1)S(1)} %all_gather.3.c_ref, bf16[512,768]{1,0:T(8,128)(2,1)S(1)} %get-tuple-element.39.x_ref, bf16[1536,768]{1,0:T(8,128)(2,1)S(1)} %get-tuple-element.37.refs_2_.refs_1_.wo_ref.w_ref, ...), custom_call_target="tpu_custom_call" | custom-call | flops 2415919104 | bytes 10223616 | tf_op jit(solution)/shard_map/update_in/pallas_call | solution.py:293
  63.4 9.7 %all-to-all-start = ((bf16[32,48,768]{2,1,0:T(8,128)(2,1)}), bf16[32,48,768]{2,1,0:T(8,128)(2,1)}, u32[]{:S(2)}, u32[]{:S(2)}) async-start(bf16[32,48,768]{2,1,0:T(8,128)(2,1)} %bitcast.14), calls=%async_computation | async-start | bytes 4718592 | tf_op jit(solution)/shard_map/all_to_all | solution.py:404
  76.9 52.2 %all-to-all-done.u_ref = bf16[32,48,768]{2,1,0:T(8,128)(2,1)} async-done(((bf16[32,48,768]{2,1,0:T(8,128)(2,1)}), bf16[32,48,768]{2,1,0:T(8,128)(2,1)}, u32[]{:S(2)}, u32[]{:S(2)}) %all-to-all-start) | async-done | bytes 2359328 | tf_op jit(solution)/shard_map/all_to_all | solution.py:404
  129.1 5.6 %all-to-all-start.2 = ((bf16[32,48,768]{2,1,0:T(8,128)(2,1)}), bf16[32,48,768]{2,1,0:T(8,128)(2,1)}, u32[]{:S(2)}, u32[]{:S(2)}) async-start(bf16[32,48,768]{2,1,0:T(8,128)(2,1)} %bitcast.13), calls=%async_computation.2 | async-start | bytes 4718592 | tf_op jit(solution)/shard_map/all_to_all | solution.py:404
  135.3 5.4 %mix.2.after_ref = bf16[32,48,768]{2,1,0:T(8,128)(2,1)} custom-call(bf16[512,512]{1,0:T(8,128)(2,1)S(1)} %get-tuple-element.53.hi_ref, bf16[512,512]{1,0:T(8,128)(2,1)S(1)} %get-tuple-element.54.lo_ref, bf16[32,48,768]{2,1,0:T(8,128)(2,1)} %all-to-all-done.u_ref, f32[32,32]{1,0:T(8,128)S(1)} %copy-done.29), custom_call_target="tpu_custom_call" | custom-call | flops 2415919104 | bytes 5767168 | tf_op jit(solution)/shard_map/mix/pallas_call | solution.py:318
  141.6 48.8 %all-to-all-done.2.u_ref = bf16[32,48,768]{2,1,0:T(8,128)(2,1)} async-done(((bf16[32,48,768]{2,1,0:T(8,128)(2,1)}), bf16[32,48,768]{2,1,0:T(8,128)(2,1)}, u32[]{:S(2)}, u32[]{:S(2)}) %all-to-all-start.2) | async-done | bytes 2359328 | tf_op jit(solution)/shard_map/all_to_all | solution.py:404
  190.4 5.6 %all-to-all-start.1 = ((bf16[32,48,768]{2,1,0:T(8,128)(2,1)}), bf16[32,48,768]{2,1,0:T(8,128)(2,1)}, u32[]{:S(2)}, u32[]{:S(2)}) async-start(bf16[32,48,768]{2,1,0:T(8,128)(2,1)} %mix.2.after_ref), calls=%async_computation.1 | async-start | bytes 4718592 | tf_op jit(solution)/shard_map/all_to_all | solution.py:404
  198.7 5.4 %mix.3 = bf16[32,48,768]{2,1,0:T(8,128)(2,1)} custom-call(bf16[512,512]{1,0:T(8,128)(2,1)S(1)} %get-tuple-element.53.hi_ref, bf16[512,512]{1,0:T(8,128)(2,1)S(1)} %copy-done.33, bf16[32,48,768]{2,1,0:T(8,128)(2,1)} %all-to-all-done.2.u_ref, bf16[32,48,768]{2,1,0:T(8,128)(2,1)S(1)} %copy-done.11), custom_call_target="tpu_custom_call" | custom-call | flops 2415919104 | bytes 5767168 | tf_op jit(solution)/shard_map/mix/pallas_call | solution.py:318
  204.1 47.2 %all-to-all-done.1 = bf16[32,48,768]{2,1,0:T(8,128)(2,1)} async-done(((bf16[32,48,768]{2,1,0:T(8,128)(2,1)}), bf16[32,48,768]{2,1,0:T(8,128)(2,1)}, u32[]{:S(2)}, u32[]{:S(2)}) %all-to-all-start.1) | async-done | bytes 2359328 | tf_op jit(solution)/shard_map/all_to_all | solution.py:404
  251.4 6.1 %all-to-all-start.3 = ((bf16[32,48,768]{2,1,0:T(8,128)(2,1)}), bf16[32,48,768]{2,1,0:T(8,128)(2,1)}, u32[]{:S(2)}, u32[]{:S(2)}) async-start(bf16[32,48,768]{2,1,0:T(8,128)(2,1)} %mix.3), calls=%async_computation.3 | async-start | bytes 4718592 | tf_op jit(solution)/shard_map/all_to_all | solution.py:404
  257.5 2.6 landed.2.refs_7_
  267.6 3.3 %turn.10 = bf16[768,128]{1,0:T(8,128)(2,1)S(1)} custom-call(bf16[768,128]{1,0:T(8,128)(2,1)S(1)} %collective-permute-done.7.refs_0_, bf16[1536,768]{1,0:T(8,128)(2,1)S(1)} %get-tuple-element.37.refs_2_.refs_1_.wo_ref.w_ref, bf16[1536,768]{1,0:T(8,128)(2,1)S(1)} %copy-done.3, bf16[768,1536]{1,0:T(8,128)(2,1)S(1)} %copy-done.1, ...), custom_call_target="tpu_custom_call" | custom-call | flops 1207959552 | bytes 11010048 | tf_op jit(solution)/shard_map/turn/pallas_call | solution.py:217
  271.0 3.3 %turn.11 = bf16[768,128]{1,0:T(8,128)(2,1)S(1)} custom-call(bf16[768,128]{1,0:T(8,128)(2,1)S(1)} %collective-permute-done.11.refs_0_, bf16[1536,768]{1,0:T(8,128)(2,1)S(1)} %get-tuple-element.37.refs_2_.refs_1_.wo_ref.w_ref, bf16[1536,768]{1,0:T(8,128)(2,1)S(1)} %copy-done.3, bf16[768,1536]{1,0:T(8,128)(2,1)S(1)} %copy-done.1, ...), custom_call_target="tpu_custom_call" | custom-call | flops 1207959552 | bytes 11010048 | tf_op jit(solution)/shard_map/turn/pallas_call | solution.py:217
  277.7 34.3 %all-to-all-done.3 = bf16[32,48,768]{2,1,0:T(8,128)(2,1)} async-done(((bf16[32,48,768]{2,1,0:T(8,128)(2,1)}), bf16[32,48,768]{2,1,0:T(8,128)(2,1)}, u32[]{:S(2)}, u32[]{:S(2)}) %all-to-all-start.3) | async-done | bytes 2359328 | tf_op jit(solution)/shard_map/all_to_all | solution.py:404
  (109 shorter events, 45.5 us)
Async XLA Ops:
  0.6 5.4 %collective-permute-start = (bf16[512,384]{1,0:T(8,128)(2,1)}, bf16[512,384]{1,0:T(8,128)(2,1)S(1)}, u32[]{:S(2)}, u32[]{:S(2)}) collective-permute-start(bf16[512,384]{1,0:T(8,128)(2,1)} %bitcast.17), channel_id=1, source_target_pairs={{0,1},{1,0},{2,3},{3,2},{4,5},{5,4},{6,7},{7,6},{8,9},{9,8},{10,11... | collective-permute-start | bytes 1179656 | tf_op jit(solution)/shard_map/ppermute | solution.py:400
  0.7 5.3 %collective-permute-start.1 = (bf16[512,384]{1,0:T(8,128)(2,1)}, bf16[512,384]{1,0:T(8,128)(2,1)S(1)}, u32[]{:S(2)}, u32[]{:S(2)}) collective-permute-start(bf16[512,384]{1,0:T(8,128)(2,1)} %refs_1_.1), channel_id=1, source_target_pairs={{0,1},{1,0},{2,3},{3,2},{4,5},{5,4},{6,7},{7,6},{8,9},{9,8},{10,11... | collective-permute-start | bytes 1179656 | tf_op jit(solution)/shard_map/ppermute | solution.py:400
  6.1 18.4 %collective-permute-start.4 = (bf16[1536,768]{1,0:T(8,128)(2,1)}, bf16[1536,768]{1,0:T(8,128)(2,1)}, u32[]{:S(2)}, u32[]{:S(2)}) collective-permute-start(bf16[1536,768]{1,0:T(8,128)(2,1)} %bitcast.2.refs_2_), channel_id=1, source_target_pairs={{0,1},{1,0},{2,3},{3,2},{4,5},{5,4},{6,7},{7,6},{8,9},{9,8},{10,11... | collective-permute-start | bytes 7077896 | tf_op jit(solution)/shard_map/ppermute | solution.py:400
  6.2 18.3 %collective-permute-start.5 = (bf16[1536,768]{1,0:T(8,128)(2,1)}, bf16[1536,768]{1,0:T(8,128)(2,1)}, u32[]{:S(2)}, u32[]{:S(2)}) collective-permute-start(bf16[1536,768]{1,0:T(8,128)(2,1)} %bitcast.3.refs_3_), channel_id=1, source_target_pairs={{0,1},{1,0},{2,3},{3,2},{4,5},{5,4},{6,7},{7,6},{8,9},{9,8},{10,11... | collective-permute-start | bytes 7077896 | tf_op jit(solution)/shard_map/ppermute | solution.py:400
  12.8 33.0 %copy-start = (bf16[768,1536]{1,0:T(8,128)(2,1)}, bf16[768,1536]{1,0:T(8,128)(2,1)S(1)}, u32[]{:S(2)}) copy-start(bf16[768,1536]{1,0:T(8,128)(2,1)S(1)} %get-tuple-element.40.refs_3_) | copy-start | bytes 7077892
  12.9 33.0 %copy-start.6 = (f32[1536,256]{1,0:T(8,128)}, f32[1536,256]{1,0:T(8,128)S(1)}, u32[]{:S(2)}) copy-start(f32[1536,256]{1,0:T(8,128)S(1)} %get-tuple-element.51.refs_5_) | copy-start | bytes 4718596
  14.9 2.7 collective-permute-start.2
  17.2 3.0 collective-permute-start.8
  17.7 10.5 %collective-permute-start.3 = (bf16[768,128]{1,0:T(8,128)(2,1)S(1)}, bf16[768,128]{1,0:T(8,128)(2,1)S(1)}, u32[]{:S(2)}, u32[]{:S(2)}) collective-permute-start(bf16[768,128]{1,0:T(8,128)(2,1)S(1)} %both_parts.2), channel_id=1, source_target_pairs={{2,0},{4,2},{6,4},{3,1},{5,3},{7,5},{10,8},{12,10},{14,12},{11,9},... | collective-permute-start | bytes 589832 | tf_op jit(solution)/shard_map/ppermute | solution.py:396
  20.2 13.3 %collective-permute-start.9 = (bf16[768,128]{1,0:T(8,128)(2,1)S(1)}, bf16[768,128]{1,0:T(8,128)(2,1)S(1)}, u32[]{:S(2)}, u32[]{:S(2)}) collective-permute-start(bf16[768,128]{1,0:T(8,128)(2,1)S(1)} %both_parts.3), channel_id=1, source_target_pairs={{2,0},{4,2},{6,4},{3,1},{5,3},{7,5},{10,8},{12,10},{14,12},{11,9},... | collective-permute-start | bytes 589832 | tf_op jit(solution)/shard_map/ppermute | solution.py:396
  26.9 19.0 %copy-start.2 = (bf16[1536,768]{1,0:T(8,128)(2,1)}, bf16[1536,768]{1,0:T(8,128)(2,1)S(1)}, u32[]{:S(2)}) copy-start(bf16[1536,768]{1,0:T(8,128)(2,1)S(1)} %get-tuple-element.47.refs_2_) | copy-start | bytes 7077892
  28.2 17.7 %copy-start.4 = (bf16[768,1536]{1,0:T(8,128)(2,1)}, bf16[768,1536]{1,0:T(8,128)(2,1)S(1)}, u32[]{:S(2)}) copy-start(bf16[768,1536]{1,0:T(8,128)(2,1)S(1)} %get-tuple-element.50.refs_4_) | copy-start | bytes 7077892
  28.2 17.7 %copy-start.8 = (f32[1536,256]{1,0:T(8,128)}, f32[1536,256]{1,0:T(8,128)S(1)}, u32[]{:S(2)}) copy-start(f32[1536,256]{1,0:T(8,128)S(1)} %get-tuple-element.52.refs_6_) | copy-start | bytes 4718596
  31.6 9.0 %collective-permute-start.6 = (bf16[768,128]{1,0:T(8,128)(2,1)S(1)}, bf16[768,128]{1,0:T(8,128)(2,1)S(1)}, u32[]{:S(2)}, u32[]{:S(2)}) collective-permute-start(bf16[768,128]{1,0:T(8,128)(2,1)S(1)} %turn.6), channel_id=1, source_target_pairs={{2,0},{4,2},{6,4},{3,1},{5,3},{7,5},{10,8},{12,10},{14,12},{11,9},... | collective-permute-start | bytes 589832 | tf_op jit(solution)/shard_map/ppermute | solution.py:396
  36.9 9.0 %collective-permute-start.10 = (bf16[768,128]{1,0:T(8,128)(2,1)S(1)}, bf16[768,128]{1,0:T(8,128)(2,1)S(1)}, u32[]{:S(2)}, u32[]{:S(2)}) collective-permute-start(bf16[768,128]{1,0:T(8,128)(2,1)S(1)} %turn.8), channel_id=1, source_target_pairs={{2,0},{4,2},{6,4},{3,1},{5,3},{7,5},{10,8},{12,10},{14,12},{11,9},... | collective-permute-start | bytes 589832 | tf_op jit(solution)/shard_map/ppermute | solution.py:396
  43.9 7.8 %collective-permute-start.7 = (bf16[768,128]{1,0:T(8,128)(2,1)S(1)}, bf16[768,128]{1,0:T(8,128)(2,1)S(1)}, u32[]{:S(2)}, u32[]{:S(2)}) collective-permute-start(bf16[768,128]{1,0:T(8,128)(2,1)S(1)} %turn.7), channel_id=1, source_target_pairs={{2,0},{4,2},{6,4},{3,1},{5,3},{7,5},{10,8},{12,10},{14,12},{11,9},... | collective-permute-start | bytes 589832 | tf_op jit(solution)/shard_map/ppermute | solution.py:396
  49.3 14.1 %copy-start.27 = (bf16[768,128]{1,0:T(8,128)(2,1)}, bf16[768,128]{1,0:T(8,128)(2,1)S(1)}, u32[]{:S(2)}) copy-start(bf16[768,128]{1,0:T(8,128)(2,1)S(1)} %turn.9) | copy-start | bytes 589828
  49.3 10.4 %copy-start.14 = (bf16[1536,768]{1,0:T(8,128)(2,1)S(1)}, bf16[1536,768]{1,0:T(8,128)(2,1)}, u32[]{:S(2)}) copy-start(bf16[1536,768]{1,0:T(8,128)(2,1)} %copy-done.12) | copy-start | bytes 7077892
  49.3 7.7 %collective-permute-start.11 = (bf16[768,128]{1,0:T(8,128)(2,1)S(1)}, bf16[768,128]{1,0:T(8,128)(2,1)S(1)}, u32[]{:S(2)}, u32[]{:S(2)}) collective-permute-start(bf16[768,128]{1,0:T(8,128)(2,1)S(1)} %turn.9), channel_id=1, source_target_pairs={{2,0},{4,2},{6,4},{3,1},{5,3},{7,5},{10,8},{12,10},{14,12},{11,9},... | collective-permute-start | bytes 589832 | tf_op jit(solution)/shard_map/ppermute | solution.py:396
  63.4 65.7 %all-to-all-start = ((bf16[32,48,768]{2,1,0:T(8,128)(2,1)}), bf16[32,48,768]{2,1,0:T(8,128)(2,1)}, u32[]{:S(2)}, u32[]{:S(2)}) async-start(bf16[32,48,768]{2,1,0:T(8,128)(2,1)} %bitcast.14), calls=%async_computation | async-start | bytes 4718592 | tf_op jit(solution)/shard_map/all_to_all | solution.py:404
  129.1 61.3 %all-to-all-start.2 = ((bf16[32,48,768]{2,1,0:T(8,128)(2,1)}), bf16[32,48,768]{2,1,0:T(8,128)(2,1)}, u32[]{:S(2)}, u32[]{:S(2)}) async-start(bf16[32,48,768]{2,1,0:T(8,128)(2,1)} %bitcast.13), calls=%async_computation.2 | async-start | bytes 4718592 | tf_op jit(solution)/shard_map/all_to_all | solution.py:404
  190.4 61.0 %all-to-all-start.1 = ((bf16[32,48,768]{2,1,0:T(8,128)(2,1)}), bf16[32,48,768]{2,1,0:T(8,128)(2,1)}, u32[]{:S(2)}, u32[]{:S(2)}) async-start(bf16[32,48,768]{2,1,0:T(8,128)(2,1)} %mix.2.after_ref), calls=%async_computation.1 | async-start | bytes 4718592 | tf_op jit(solution)/shard_map/all_to_all | solution.py:404
  251.4 60.5 %all-to-all-start.3 = ((bf16[32,48,768]{2,1,0:T(8,128)(2,1)}), bf16[32,48,768]{2,1,0:T(8,128)(2,1)}, u32[]{:S(2)}, u32[]{:S(2)}) async-start(bf16[32,48,768]{2,1,0:T(8,128)(2,1)} %mix.3), calls=%async_computation.3 | async-start | bytes 4718592 | tf_op jit(solution)/shard_map/all_to_all | solution.py:404
  274.5 1.5 collective-permute-start.12
  (27 other events, 80.2 us)

commit v5 on v4

--- a/solution.py
+++ b/solution.py
@@ -55,27 +55,57 @@
     return jnp.where(core == 0, jnp.concatenate([mine, theirs], axis=1), jnp.concatenate([theirs, mine], axis=1))
 
 
-def entering_kernel(at, x_ref, other_x_ref, dy_ref, other_dy_ref, whole_ref, own_ref, cot_ref):
+def opening_kernel(at, x_hbm, other_x_hbm, dy_hbm, other_dy_hbm, w_hbm, *refs):
+    whole_ref, own_x_ref, cot_ref, a_ref, s_ref, own_s_ref, t_ref = refs[:7]
+    x_ref, other_x_ref, dy_ref, other_dy_ref, w_ref, sems = refs[7:]
     core = at[0]
-    own = own_ref.shape[0]
+    own = own_x_ref.shape[0]
+    parts = blocks(w_ref.shape[0])
+    pairs = [(x_hbm, x_ref), (other_x_hbm, other_x_ref)]
+    pairs += [(w_hbm.at[rows, :], w_ref.at[rows, :]) for rows in parts]
+    pairs += [(dy_hbm, dy_ref), (other_dy_hbm, other_dy_ref)]
+    copies = [pltpu.make_async_copy(*pair, sems.at[i]) for i, pair in enumerate(pairs)]
+    for copy in copies:
+        copy.start()
+    for copy in copies[:2]:
+        copy.wait()
     whole_ref[...] = joined(core, x_ref[...], other_x_ref[...])
-    own_ref[...] = whole_ref[pl.ds(pl.multiple_of(core * own, own), own), :]
+    own_x_ref[...] = whole_ref[pl.ds(pl.multiple_of(core * own, own), own), :]
+    x = whole_ref[...]
+    for i, rows in enumerate(parts):
+        copies[2 + i].wait()
+        weight = w_ref[rows, :]
+        values, slopes = gelu_parts(nt(weight, x) * in_scale)
+        a_ref[rows, :] = values.astype(BF)
+        s_ref[rows, :] = slopes
+        own_s_ref[rows, :] = jnp.where(core == 0, slopes[:, :own], slopes[:, own:])
+        t_ref[:, rows] = jnp.transpose(weight)
+    for copy in copies[-2:]:
+        copy.wait()
     dy = joined(core, dy_ref[...], other_dy_ref[...])
     cot_ref[...] = jnp.transpose(jnp.where(at[1] == 1, dy, jnp.zeros_like(dy)))
 
 
-def entering(at, x, other_x, dy, other_dy):
-    own = dy.shape[0] // 2
-    shapes = [(2 * own, D), (own, D), (D, 2 * own)]
-    return pl.pallas_call(
-        entering_kernel,
-        out_shape=[jax.ShapeDtypeStruct(s, BF) for s in shapes],
-        in_specs=[SMEM] + [VMEM] * 4,
+def opening(at, x, other_x, dy, other_dy, weight_in):
+    m, h = dy.shape[0], weight_in.shape[0]
+    own = m // 2
+    shapes = [
+        ((m, D), BF), ((own, D), BF), ((D, m), BF), ((h, m), BF), ((h, m), F32), ((h, own), F32), ((D, h), BF),
+    ]
+    return pl.pallas_call(
+        opening_kernel,
+        out_shape=[pltpu.VMEM(*s) for s in shapes],
+        in_specs=[SMEM] + [ANY] * 5,
         out_specs=[VMEM] * len(shapes),
-        compiler_params=params(),
-        cost_estimate=cost(0, 16 * own * D),
-        name="entering",
-    )(at, x, other_x, dy, other_dy)
+        scratch_shapes=[
+            *[pltpu.VMEM(dy.shape, BF)] * 4,
+            pltpu.VMEM((h, D), BF),
+            pltpu.SemaphoreType.DMA((4 + h // BLOCK,)),
+        ],
+        compiler_params=params(46),
+        cost_estimate=cost(2 * m * h * D, 6 * h * D + 8 * m * h, 2 * m * h),
+        name="opening",
+    )(at, x, other_x, dy, other_dy, weight_in)
 
 
 def first_turn_kernel(chunk, m, at, c_ref, wo_ref, wt_ref, s_ref, cot_ref, mine_ref, theirs_ref, delta):
@@ -168,36 +198,6 @@
     )(*arrays)
 
 
-def unit_parts_kernel(core, w_ref, x_ref, a_ref, s_ref, t_ref, own_ref):
-    own = own_ref.shape[1]
-    x = x_ref[...]
-    for at in blocks(w_ref.shape[0]):
-        weight = w_ref[at, :]
-        values, slopes = gelu_parts(nt(weight, x) * in_scale)
-        a_ref[at, :] = values.astype(BF)
-        s_ref[at, :] = slopes
-        own_ref[at, :] = jnp.where(core[0] == 0, slopes[:, :own], slopes[:, own:])
-        t_ref[:, at] = jnp.transpose(weight)
-
-
-def unit_parts(core, weight_in, x_rows):
-    m, h = x_rows.shape[0], weight_in.shape[0]
-    return pl.pallas_call(
-        unit_parts_kernel,
-        out_shape=[
-            jax.ShapeDtypeStruct((h, m), BF),
-            jax.ShapeDtypeStruct((h, m), F32),
-            jax.ShapeDtypeStruct((D, h), BF),
-            jax.ShapeDtypeStruct((h, m // 2), F32),
-        ],
-        in_specs=[SMEM, VMEM, VMEM],
-        out_specs=[VMEM] * 4,
-        compiler_params=params(),
-        cost_estimate=cost(2 * m * h * D, 2 * h * D + 6 * m * h, 2 * m * h),
-        name="unit_parts",
-    )(core, weight_in, x_rows)
-
-
 def turn_kernel(col0, c_ref, wo0_ref, wo1_ref, wt0_ref, wt1_ref, s0_ref, s1_ref, after_ref, o_ref, delta):
     cot = c_ref[...]
     m = cot.shape[1]
@@ -245,13 +245,20 @@
     )(core, mine, theirs)
 
 
+def all_tokens(core, refs):
+    mine, theirs = refs[:CHUNKS], refs[CHUNKS:]
+    beside = lambda first, second: jnp.concatenate([ref[...] for ref in first + second], axis=1)
+    return jnp.where(core == 0, beside(mine, theirs), beside(theirs, mine))
+
+
 def copies_out(scratch, o_ref, sems, i):
     at = pl.ds(i * BLOCK, BLOCK)
     return pltpu.make_async_copy(scratch.at[at, :], o_ref.at[at, :], sems.at[i])
 
 
-def update_out_kernel(a_ref, c_ref, w_ref, o_ref, scratch, sems):
-    cot = jnp.transpose(c_ref[...])
+def update_out_kernel(core, *refs):
+    a_ref, w_ref, o_ref, scratch, sems = refs[2 * CHUNKS :]
+    cot = jnp.transpose(all_tokens(core[0], refs[: 2 * CHUNKS]))
     parts = blocks(a_ref.shape[0])
     for i, at in enumerate(parts):
         grad = nn(a_ref[at, :], cot) * out_scale
@@ -261,22 +268,23 @@
         copies_out(scratch, o_ref, sems, i).wait()
 
 
-def update_out(act_t, cot, weight_out):
+def update_out(core, cots, act_t, weight_out):
     h, m = act_t.shape
     return pl.pallas_call(
         update_out_kernel,
         out_shape=pltpu.HBM((h, D), BF),
-        in_specs=[VMEM] * 3,
+        in_specs=[SMEM] + [VMEM] * (2 * CHUNKS + 2),
         out_specs=HBM,
         scratch_shapes=[pltpu.VMEM((h, D), BF), pltpu.SemaphoreType.DMA((h // BLOCK,))],
         compiler_params=params(),
         cost_estimate=cost(2 * m * h * D, 2 * m * h + 4 * h * D),
         name="update_out",
-    )(act_t, cot, weight_out)
-
-
-def update_in_kernel(s_ref, c_ref, x_ref, wo_ref, wi_ref, o_ref, scratch, sems):
-    cot, x = c_ref[...], x_ref[...]
+    )(core, *cots, act_t, weight_out)
+
+
+def update_in_kernel(core, *refs):
+    s_ref, x_ref, wo_ref, wi_ref, o_ref, scratch, sems = refs[2 * CHUNKS :]
+    cot, x = all_tokens(core[0], refs[: 2 * CHUNKS]), x_ref[...]
     parts = blocks(s_ref.shape[0])
     for i, at in enumerate(parts):
         backward = nn(wo_ref[at, :], cot) * out_scale
@@ -288,18 +296,18 @@
         copies_out(scratch, o_ref, sems, i).wait()
 
 
-def update_in(slopes_t, cot, x_rows, weight_out, weight_in):
+def update_in(core, cots, slopes_t, x_rows, weight_out, weight_in):
     h, m = slopes_t.shape
     return pl.pallas_call(
         update_in_kernel,
         out_shape=pltpu.HBM((h, D), BF),
-        in_specs=[VMEM] * 5,
+        in_specs=[SMEM] + [VMEM] * (2 * CHUNKS + 4),
         out_specs=HBM,
         scratch_shapes=[pltpu.VMEM((h, D), BF), pltpu.SemaphoreType.DMA((h // BLOCK,))],
         compiler_params=params(),
         cost_estimate=cost(4 * m * h * D, 4 * m * h + 6 * h * D),
         name="update_in",
-    )(slopes_t, cot, x_rows, weight_out, weight_in)
+    )(core, *cots, slopes_t, x_rows, weight_out, weight_in)
 
 
 def mix_kernel(hi_ref, lo_ref, u_ref, after_ref, o_ref):
@@ -419,26 +427,24 @@
     last = (segment_index == segments - 1).astype(jnp.int32)
     other_x = other_core(inputs[0])
     other_dy = other_core(loss_grad)
-    own_x, own_dy, own_in, own_out = kept(inputs[0], loss_grad, weight_in, weight_out, mib=54)
-    late_in, late_out, other_x, other_dy, own_x = lax.optimization_barrier(
-        (weight_in, weight_out, other_x, other_dy, own_x)
-    )
+    late_in, late_out, other_x, other_dy = lax.optimization_barrier((weight_in, weight_out, other_x, other_dy))
     other_in = other_core(late_in)
     other_out = other_core(late_out)
     at = jnp.stack([core.astype(jnp.int32), last])
-    x_rows, x_own, cot = entering(at, own_x, other_x, own_dy, other_dy)
-    act_t, slopes_t, own_in_t, own_slopes = unit_parts(core_at, own_in, x_rows)
+    x_rows, x_own, cot, act_t, slopes_t, own_slopes, own_in_t = opening(
+        at, inputs[0], other_x, loss_grad, other_dy, weight_in
+    )
     hi, lo = spread_matrix(mixing)
 
     columns = own // CHUNKS
-    halves = [first_turn(at, c, cot, own_out, own_in_t, slopes_t) for c in range(CHUNKS)]
+    halves = [first_turn(at, c, cot, weight_out, own_in_t, slopes_t) for c in range(CHUNKS)]
     kept_cot = [[half[0] for half in halves]]
     kept_result = [[both_parts(half[0], half[1], other_core(half[2])) for half in halves]]
     cots = [passed_along(r) for r in kept_result[0]]
 
     other_in, other_out = kept(other_in, other_out)
     other_slopes, other_in_t = token_slopes(x_own, other_in)
-    slopes, wouts, wins_t = (own_slopes, other_slopes), (own_out, other_out), (own_in_t, other_in_t)
+    slopes, wouts, wins_t = (own_slopes, other_slopes), (weight_out, other_out), (own_in_t, other_in_t)
     for turn_index in range(1, segments - 1):
         results = [turn(cots[c], wouts, wins_t, slopes, c * columns, mixing) for c in range(CHUNKS)]
         kept_cot.append(cots)
@@ -453,12 +459,13 @@
             for t in range(1, segments):
                 total = total + kept[t][c]
             parts.append(total)
-        return jnp.concatenate(parts, axis=1)
-
-    cot_t = lax.all_gather(summed(kept_cot), "tp", axis=1, tiled=True)
-    updated_in = update_in(slopes_t, cot_t, x_rows, own_out, own_in)
+        return parts
+
+    mine = summed(kept_cot)
+    all_cots = mine + [other_core(part) for part in mine]
+    updated_in = update_in(core_at, all_cots, slopes_t, x_rows, weight_out, weight_in)
     pieces_in = sent_out(updated_in.reshape(replicas, units // replicas, D))
-    updated_out = update_out(act_t, cot_t, own_out)
+    updated_out = update_out(core_at, all_cots, act_t, weight_out)
     pieces_out = sent_out(updated_out.reshape(replicas, units // replicas, D))
     mixture_in = mix(hi, lo, pieces_in, mixing)
     back_in = sent_out(mixture_in)
@@ -466,7 +473,7 @@
     mixed_in = landed(back_in.reshape(units, D), mixing)
 
     kept_result.append([turn(cots[c], wouts, wins_t, slopes, c * columns, mixed_in) for c in range(CHUNKS)])
-    result = summed(kept_result)
+    result = jnp.concatenate(summed(kept_result), axis=1)
     width = D // 2
     mine = lax.dynamic_slice_in_dim(result, core * width, width, 0)
     theirs = other_core(lax.dynamic_slice_in_dim(result, (1 - core) * width, width, 0))

time: 316 us -> 312 us (0.987)
    ppermute x7 -> x9, waiting for transfers between devices: 1.44 us -> 4.84 us  [other_core(): return lax.ppermute(shard, 'tp', [(0, 1), (1, 0)])]
    unnamed x68 -> x72, local copies, waits for them, and re-layouts: 17.3 us -> 14.3 us
  transfers between devices with their start and end apart: 17 -> 19, of which waited for: 6 -> 9; matrix products, arithmetic and copies ran while one was open for 0% -> 0% of each run, Pallas kernels for 16% -> 16%
where the time goes in v5:
time: 312 us; the launch traced here: 311 us
  waiting for transfers between devices  191 us (61%)
  Pallas kernels  57.1 us (18%)
  starting transfers between devices  45.7 us (15%)
  local copies, waits for them, and re-layouts  15 us (5%)
    all_to_all x4, waiting for transfers between devices, sent_out(): return lax.all_to_all(block, 'rep', split_axis=0, concat_axis=0, tiled=True)  181 us
    all_to_all x4, starting transfers between devices, sent_out(): return lax.all_to_all(block, 'rep', split_axis=0, concat_axis=0, tiled=True)  27 us
    pallas_call x6, Pallas kernels, turn(): pl.pallas_call(lambda *refs: turn_kernel(col0, *refs), out_shape=jax.Shap...  20 us
    ppermute x6, starting transfers between devices, passed_along(): lax.ppermute(shard, 'section', [(i, i - 1) for i in range(1, length)])  16.4 us
    unnamed x72, local copies, waits for them, and re-layouts  14.3 us
    pallas_call x2, Pallas kernels, mix(): pl.pallas_call(mix_kernel, grid=(rows // block,), out_shape=pltpu.HBM(pie...  10.9 us
  transfers between devices with their start and end apart: 19, of which 9 were waited for; matrix products, arithmetic and copies ran while one was open for 0% of the time, Pallas kernels for 16%

profile of v5, /device:TPU:16, one launch (start us, length us, event | category | flops | bytes accessed | tf_op | source)
XLA Modules:
  0.0 310.7 jit_solution(11665125635887658496)
XLA Ops:
  4.3 5.6 %opening.1 = (bf16[512,768]{1,0:T(8,128)(2,1)S(1)}, bf16[256,768]{1,0:T(8,128)(2,1)S(1)}, bf16[768,512]{1,0:T(8,128)(2,1)S(1)}, bf16[1536,512]{1,0:T(8,128)(2,1)...) custom-call(s32[2]{0:T(128)} %pad_add_fusion.at.refs_0_, ...), custom_call_target="tpu_custom_call" | custom-call | flops 1207959552 | bytes 13369344 | tf_op jit(solution)/shard_map/opening/pallas_call | solution.py:95
  17.3 4.3 %collective-permute-start.3 = (bf16[768,128]{1,0:T(8,128)(2,1)S(1)}, bf16[768,128]{1,0:T(8,128)(2,1)S(1)}, u32[]{:S(2)}, u32[]{:S(2)}) collective-permute-start(bf16[768,128]{1,0:T(8,128)(2,1)S(1)} %both_parts.2), channel_id=1, source_target_pairs={{2,0},{4,2},{6,4},{3,1},{5,3},{7,5},{10,8},{12,10},{14,12},{11,9},... | collective-permute-start | bytes 589832 | tf_op jit(solution)/shard_map/ppermute | solution.py:404
  25.4 3.3 %turn.8 = bf16[768,128]{1,0:T(8,128)(2,1)S(1)} custom-call(bf16[768,128]{1,0:T(8,128)(2,1)S(1)} %collective-permute-done.9.refs_0_, bf16[1536,768]{1,0:T(8,128)(2,1)S(1)} %bitcast.15, bf16[1536,768]{1,0:T(8,128)(2,1)S(1)} %get-tuple-element.36.refs_2_, bf16[768,1536]{1,0:T(8,128)(2,1)S(1)} %get-tuple-element.29.refs_3_, ...), custom_call_target="tpu_custom_call" | custom-call | flops 1207959552 | bytes 11010048 | tf_op jit(solution)/shard_map/turn/pallas_call | solution.py:217
  30.7 3.3 %turn.6 = bf16[768,128]{1,0:T(8,128)(2,1)S(1)} custom-call(bf16[768,128]{1,0:T(8,128)(2,1)S(1)} %collective-permute-done.3.refs_0_, bf16[1536,768]{1,0:T(8,128)(2,1)S(1)} %bitcast.16, bf16[1536,768]{1,0:T(8,128)(2,1)S(1)} %get-tuple-element.36.refs_2_, bf16[768,1536]{1,0:T(8,128)(2,1)S(1)} %get-tuple-element.29.refs_3_, ...), custom_call_target="tpu_custom_call" | custom-call | flops 1207959552 | bytes 11010048 | tf_op jit(solution)/shard_map/turn/pallas_call | solution.py:217
  34.0 3.6 %collective-permute-start.6 = (bf16[768,128]{1,0:T(8,128)(2,1)S(1)}, bf16[768,128]{1,0:T(8,128)(2,1)S(1)}, u32[]{:S(2)}, u32[]{:S(2)}) collective-permute-start(bf16[768,128]{1,0:T(8,128)(2,1)S(1)} %turn.6), channel_id=1, source_target_pairs={{2,0},{4,2},{6,4},{3,1},{5,3},{7,5},{10,8},{12,10},{14,12},{11,9},... | collective-permute-start | bytes 589832 | tf_op jit(solution)/shard_map/ppermute | solution.py:404
  37.7 3.3 %turn.9 = bf16[768,128]{1,0:T(8,128)(2,1)S(1)} custom-call(bf16[768,128]{1,0:T(8,128)(2,1)S(1)} %collective-permute-done.10.refs_0_, bf16[1536,768]{1,0:T(8,128)(2,1)S(1)} %bitcast.17, bf16[1536,768]{1,0:T(8,128)(2,1)S(1)} %get-tuple-element.36.refs_2_, bf16[768,1536]{1,0:T(8,128)(2,1)S(1)} %get-tuple-element.29.refs_3_, ...), custom_call_target="tpu_custom_call" | custom-call | flops 1207959552 | bytes 11010048 | tf_op jit(solution)/shard_map/turn/pallas_call | solution.py:217
  43.0 3.3 %turn.7 = bf16[768,128]{1,0:T(8,128)(2,1)S(1)} custom-call(bf16[768,128]{1,0:T(8,128)(2,1)S(1)} %collective-permute-done.6.refs_0_, bf16[1536,768]{1,0:T(8,128)(2,1)S(1)} %bitcast.18, bf16[1536,768]{1,0:T(8,128)(2,1)S(1)} %get-tuple-element.36.refs_2_, bf16[768,1536]{1,0:T(8,128)(2,1)S(1)} %get-tuple-element.29.refs_3_, ...), custom_call_target="tpu_custom_call" | custom-call | flops 1207959552 | bytes 11010048 | tf_op jit(solution)/shard_map/turn/pallas_call | solution.py:217
  48.8 5.2 %collective-permute-done.7.refs_0_ = bf16[768,128]{1,0:T(8,128)(2,1)S(1)} collective-permute-done((bf16[768,128]{1,0:T(8,128)(2,1)S(1)}, bf16[768,128]{1,0:T(8,128)(2,1)S(1)}, u32[]{:S(2)}, u32[]{:S(2)}) %collective-permute-start.7) | collective-permute-done | bytes 196640 | tf_op jit(solution)/shard_map/ppermute | solution.py:404
  55.8 3.7 %update_in.1 = bf16[1536,768]{1,0:T(8,128)(2,1)} custom-call(s32[1]{0:T(128)} %bitcast.core, bf16[768,128]{1,0:T(8,128)(2,1)S(1)} %add_add_fusion.2.refs_0_, bf16[768,128]{1,0:T(8,128)(2,1)S(1)} %add_add_fusion.1.refs_1_, bf16[768,128]{1,0:T(8,128)(2,1)S(1)} %collective-permute-done.12.refs_2_, bf16[768,128]{1,0:T(8,128)(2,1)S(1)} %collective-permute-done.13.refs_3_, ...), custom_call_target="tpu_custom_call" | custom-call | flops 2415919104 | bytes 10223616 | tf_op jit(solution)/shard_map/update_in/pallas_call | solution.py:301
  59.4 9.7 %all-to-all-start = ((bf16[32,48,768]{2,1,0:T(8,128)(2,1)}), bf16[32,48,768]{2,1,0:T(8,128)(2,1)}, u32[]{:S(2)}, u32[]{:S(2)}) async-start(bf16[32,48,768]{2,1,0:T(8,128)(2,1)} %bitcast.28), calls=%async_computation | async-start | bytes 4718592 | tf_op jit(solution)/shard_map/all_to_all | solution.py:412
  70.6 2.4 update_out.1
  73.0 52.1 %all-to-all-done.u_ref = bf16[32,48,768]{2,1,0:T(8,128)(2,1)} async-done(((bf16[32,48,768]{2,1,0:T(8,128)(2,1)}), bf16[32,48,768]{2,1,0:T(8,128)(2,1)}, u32[]{:S(2)}, u32[]{:S(2)}) %all-to-all-start) | async-done | bytes 2359328 | tf_op jit(solution)/shard_map/all_to_all | solution.py:412
  125.1 5.6 %all-to-all-start.2 = ((bf16[32,48,768]{2,1,0:T(8,128)(2,1)}), bf16[32,48,768]{2,1,0:T(8,128)(2,1)}, u32[]{:S(2)}, u32[]{:S(2)}) async-start(bf16[32,48,768]{2,1,0:T(8,128)(2,1)} %bitcast.27), calls=%async_computation.2 | async-start | bytes 4718592 | tf_op jit(solution)/shard_map/all_to_all | solution.py:412
  131.4 5.4 %mix.2.after_ref = bf16[32,48,768]{2,1,0:T(8,128)(2,1)} custom-call(bf16[512,512]{1,0:T(8,128)(2,1)S(1)} %get-tuple-element.42.hi_ref, bf16[512,512]{1,0:T(8,128)(2,1)S(1)} %get-tuple-element.43.lo_ref, bf16[32,48,768]{2,1,0:T(8,128)(2,1)} %all-to-all-done.u_ref, f32[32,32]{1,0:T(8,128)S(1)} %copy-done.28), custom_call_target="tpu_custom_call" | custom-call | flops 2415919104 | bytes 5767168 | tf_op jit(solution)/shard_map/mix/pallas_call | solution.py:326
  138.5 48.0 %all-to-all-done.2.u_ref = bf16[32,48,768]{2,1,0:T(8,128)(2,1)} async-done(((bf16[32,48,768]{2,1,0:T(8,128)(2,1)}), bf16[32,48,768]{2,1,0:T(8,128)(2,1)}, u32[]{:S(2)}, u32[]{:S(2)}) %all-to-all-start.2) | async-done | bytes 2359328 | tf_op jit(solution)/shard_map/all_to_all | solution.py:412
  186.5 5.6 %all-to-all-start.1 = ((bf16[32,48,768]{2,1,0:T(8,128)(2,1)}), bf16[32,48,768]{2,1,0:T(8,128)(2,1)}, u32[]{:S(2)}, u32[]{:S(2)}) async-start(bf16[32,48,768]{2,1,0:T(8,128)(2,1)} %mix.2.after_ref), calls=%async_computation.1 | async-start | bytes 4718592 | tf_op jit(solution)/shard_map/all_to_all | solution.py:412
  195.8 5.5 %mix.3 = bf16[32,48,768]{2,1,0:T(8,128)(2,1)} custom-call(bf16[512,512]{1,0:T(8,128)(2,1)S(1)} %copy-done.31, bf16[512,512]{1,0:T(8,128)(2,1)S(1)} %copy-done.33, bf16[32,48,768]{2,1,0:T(8,128)(2,1)} %all-to-all-done.2.u_ref, bf16[32,48,768]{2,1,0:T(8,128)(2,1)S(1)} %copy-done.12), custom_call_target="tpu_custom_call" | custom-call | flops 2415919104 | bytes 5767168 | tf_op jit(solution)/shard_map/mix/pallas_call | solution.py:326
  201.3 46.2 %all-to-all-done.1 = bf16[32,48,768]{2,1,0:T(8,128)(2,1)} async-done(((bf16[32,48,768]{2,1,0:T(8,128)(2,1)}), bf16[32,48,768]{2,1,0:T(8,128)(2,1)}, u32[]{:S(2)}, u32[]{:S(2)}) %all-to-all-start.1) | async-done | bytes 2359328 | tf_op jit(solution)/shard_map/all_to_all | solution.py:412
  247.4 6.1 %all-to-all-start.3 = ((bf16[32,48,768]{2,1,0:T(8,128)(2,1)}), bf16[32,48,768]{2,1,0:T(8,128)(2,1)}, u32[]{:S(2)}, u32[]{:S(2)}) async-start(bf16[32,48,768]{2,1,0:T(8,128)(2,1)} %mix.3), calls=%async_computation.3 | async-start | bytes 4718592 | tf_op jit(solution)/shard_map/all_to_all | solution.py:412
  253.6 2.6 landed.2.refs_7_
  263.7 3.3 %turn.10 = bf16[768,128]{1,0:T(8,128)(2,1)S(1)} custom-call(bf16[768,128]{1,0:T(8,128)(2,1)S(1)} %collective-permute-done.7.refs_0_, bf16[1536,768]{1,0:T(8,128)(2,1)S(1)} %bitcast.21, bf16[1536,768]{1,0:T(8,128)(2,1)S(1)} %copy-done.4, bf16[768,1536]{1,0:T(8,128)(2,1)S(1)} %copy-done.2, bf16[768,1536]{1,0:T(8,128)(2,1)S(1)} %copy-done.6, ...), custom_call_target="tpu_custom_call" | custom-call | flops 1207959552 | bytes 11010048 | tf_op jit(solution)/shard_map/turn/pallas_call | solution.py:217
  267.1 3.3 %turn.11 = bf16[768,128]{1,0:T(8,128)(2,1)S(1)} custom-call(bf16[768,128]{1,0:T(8,128)(2,1)S(1)} %collective-permute-done.11.refs_0_, bf16[1536,768]{1,0:T(8,128)(2,1)S(1)} %bitcast.22, bf16[1536,768]{1,0:T(8,128)(2,1)S(1)} %copy-done.4, bf16[768,1536]{1,0:T(8,128)(2,1)S(1)} %copy-done.2, bf16[768,1536]{1,0:T(8,128)(2,1)S(1)} %copy-done.6, ...), custom_call_target="tpu_custom_call" | custom-call | flops 1207959552 | bytes 11010048 | tf_op jit(solution)/shard_map/turn/pallas_call | solution.py:217
  273.7 34.3 %all-to-all-done.3 = bf16[32,48,768]{2,1,0:T(8,128)(2,1)} async-done(((bf16[32,48,768]{2,1,0:T(8,128)(2,1)}), bf16[32,48,768]{2,1,0:T(8,128)(2,1)}, u32[]{:S(2)}, u32[]{:S(2)}) %all-to-all-start.3) | async-done | bytes 2359328 | tf_op jit(solution)/shard_map/all_to_all | solution.py:412
  308.0 2.5 landed.3
  (113 shorter events, 40.8 us)
Async XLA Ops:
  0.6 2.0 collective-permute-start
  0.7 2.5 collective-permute-start.1
  3.2 18.4 %collective-permute-start.4 = (bf16[1536,768]{1,0:T(8,128)(2,1)}, bf16[1536,768]{1,0:T(8,128)(2,1)}, u32[]{:S(2)}, u32[]{:S(2)}) collective-permute-start(bf16[1536,768]{1,0:T(8,128)(2,1)} %bitcast.24), channel_id=1, source_target_pairs={{0,1},{1,0},{2,3},{3,2},{4,5},{5,4},{6,7},{7,6},{8,9},{9,8},{10,11... | collective-permute-start | bytes 7077896 | tf_op jit(solution)/shard_map/ppermute | solution.py:408
  3.4 18.2 %collective-permute-start.5 = (bf16[1536,768]{1,0:T(8,128)(2,1)}, bf16[1536,768]{1,0:T(8,128)(2,1)}, u32[]{:S(2)}, u32[]{:S(2)}) collective-permute-start(bf16[1536,768]{1,0:T(8,128)(2,1)} %bitcast.12), channel_id=1, source_target_pairs={{0,1},{1,0},{2,3},{3,2},{4,5},{5,4},{6,7},{7,6},{8,9},{9,8},{10,11... | collective-permute-start | bytes 7077896 | tf_op jit(solution)/shard_map/ppermute | solution.py:408
  9.9 33.1 %copy-start.1 = (bf16[768,1536]{1,0:T(8,128)(2,1)}, bf16[768,1536]{1,0:T(8,128)(2,1)S(1)}, u32[]{:S(2)}) copy-start(bf16[768,1536]{1,0:T(8,128)(2,1)S(1)} %get-tuple-element.29.refs_3_) | copy-start | bytes 7077892
  9.9 33.1 %copy-start.7 = (f32[1536,256]{1,0:T(8,128)}, f32[1536,256]{1,0:T(8,128)S(1)}, u32[]{:S(2)}) copy-start(f32[1536,256]{1,0:T(8,128)S(1)} %get-tuple-element.40.refs_5_) | copy-start | bytes 4718596
  12.0 2.7 collective-permute-start.8
  14.3 2.9 collective-permute-start.2
  14.8 10.5 %collective-permute-start.9 = (bf16[768,128]{1,0:T(8,128)(2,1)S(1)}, bf16[768,128]{1,0:T(8,128)(2,1)S(1)}, u32[]{:S(2)}, u32[]{:S(2)}) collective-permute-start(bf16[768,128]{1,0:T(8,128)(2,1)S(1)} %both_parts.3), channel_id=1, source_target_pairs={{2,0},{4,2},{6,4},{3,1},{5,3},{7,5},{10,8},{12,10},{14,12},{11,9},... | collective-permute-start | bytes 589832 | tf_op jit(solution)/shard_map/ppermute | solution.py:404
  17.3 13.3 %collective-permute-start.3 = (bf16[768,128]{1,0:T(8,128)(2,1)S(1)}, bf16[768,128]{1,0:T(8,128)(2,1)S(1)}, u32[]{:S(2)}, u32[]{:S(2)}) collective-permute-start(bf16[768,128]{1,0:T(8,128)(2,1)S(1)} %both_parts.2), channel_id=1, source_target_pairs={{2,0},{4,2},{6,4},{3,1},{5,3},{7,5},{10,8},{12,10},{14,12},{11,9},... | collective-permute-start | bytes 589832 | tf_op jit(solution)/shard_map/ppermute | solution.py:404
  24.0 19.0 %copy-start.3 = (bf16[1536,768]{1,0:T(8,128)(2,1)}, bf16[1536,768]{1,0:T(8,128)(2,1)S(1)}, u32[]{:S(2)}) copy-start(bf16[1536,768]{1,0:T(8,128)(2,1)S(1)} %get-tuple-element.36.refs_2_) | copy-start | bytes 7077892
  25.3 17.7 %copy-start.5 = (bf16[768,1536]{1,0:T(8,128)(2,1)}, bf16[768,1536]{1,0:T(8,128)(2,1)S(1)}, u32[]{:S(2)}) copy-start(bf16[768,1536]{1,0:T(8,128)(2,1)S(1)} %get-tuple-element.39.refs_4_) | copy-start | bytes 7077892
  25.3 17.7 %copy-start.9 = (f32[1536,256]{1,0:T(8,128)}, f32[1536,256]{1,0:T(8,128)S(1)}, u32[]{:S(2)}) copy-start(f32[1536,256]{1,0:T(8,128)S(1)} %get-tuple-element.41.refs_6_) | copy-start | bytes 4718596
  28.7 9.0 %collective-permute-start.10 = (bf16[768,128]{1,0:T(8,128)(2,1)S(1)}, bf16[768,128]{1,0:T(8,128)(2,1)S(1)}, u32[]{:S(2)}, u32[]{:S(2)}) collective-permute-start(bf16[768,128]{1,0:T(8,128)(2,1)S(1)} %turn.8), channel_id=1, source_target_pairs={{2,0},{4,2},{6,4},{3,1},{5,3},{7,5},{10,8},{12,10},{14,12},{11,9},... | collective-permute-start | bytes 589832 | tf_op jit(solution)/shard_map/ppermute | solution.py:404
  34.0 9.0 %collective-permute-start.6 = (bf16[768,128]{1,0:T(8,128)(2,1)S(1)}, bf16[768,128]{1,0:T(8,128)(2,1)S(1)}, u32[]{:S(2)}, u32[]{:S(2)}) collective-permute-start(bf16[768,128]{1,0:T(8,128)(2,1)S(1)} %turn.6), channel_id=1, source_target_pairs={{2,0},{4,2},{6,4},{3,1},{5,3},{7,5},{10,8},{12,10},{14,12},{11,9},... | collective-permute-start | bytes 589832 | tf_op jit(solution)/shard_map/ppermute | solution.py:404
  41.0 7.6 %collective-permute-start.11 = (bf16[768,128]{1,0:T(8,128)(2,1)S(1)}, bf16[768,128]{1,0:T(8,128)(2,1)S(1)}, u32[]{:S(2)}, u32[]{:S(2)}) collective-permute-start(bf16[768,128]{1,0:T(8,128)(2,1)S(1)} %turn.9), channel_id=1, source_target_pairs={{2,0},{4,2},{6,4},{3,1},{5,3},{7,5},{10,8},{12,10},{14,12},{11,9},... | collective-permute-start | bytes 589832 | tf_op jit(solution)/shard_map/ppermute | solution.py:404
  46.4 7.6 %collective-permute-start.7 = (bf16[768,128]{1,0:T(8,128)(2,1)S(1)}, bf16[768,128]{1,0:T(8,128)(2,1)S(1)}, u32[]{:S(2)}, u32[]{:S(2)}) collective-permute-start(bf16[768,128]{1,0:T(8,128)(2,1)S(1)} %turn.7), channel_id=1, source_target_pairs={{2,0},{4,2},{6,4},{3,1},{5,3},{7,5},{10,8},{12,10},{14,12},{11,9},... | collective-permute-start | bytes 589832 | tf_op jit(solution)/shard_map/ppermute | solution.py:404
  48.7 5.6 %collective-permute-start.13 = (bf16[768,128]{1,0:T(8,128)(2,1)S(1)}, bf16[768,128]{1,0:T(8,128)(2,1)S(1)}, u32[]{:S(2)}, u32[]{:S(2)}) collective-permute-start(bf16[768,128]{1,0:T(8,128)(2,1)S(1)} %add_add_fusion.1.refs_1_), channel_id=1, source_target_pairs={{0,1},{1,0},{2,3},{3,2},{4,5},{5,4},{6,7},{7,6},{8,9},{9,8},{10,11... | collective-permute-start | bytes 589832 | tf_op jit(solution)/shard_map/ppermute | solution.py:408
  54.0 1.7 collective-permute-start.12
  59.4 65.7 %all-to-all-start = ((bf16[32,48,768]{2,1,0:T(8,128)(2,1)}), bf16[32,48,768]{2,1,0:T(8,128)(2,1)}, u32[]{:S(2)}, u32[]{:S(2)}) async-start(bf16[32,48,768]{2,1,0:T(8,128)(2,1)} %bitcast.28), calls=%async_computation | async-start | bytes 4718592 | tf_op jit(solution)/shard_map/all_to_all | solution.py:412
  125.1 61.3 %all-to-all-start.2 = ((bf16[32,48,768]{2,1,0:T(8,128)(2,1)}), bf16[32,48,768]{2,1,0:T(8,128)(2,1)}, u32[]{:S(2)}, u32[]{:S(2)}) async-start(bf16[32,48,768]{2,1,0:T(8,128)(2,1)} %bitcast.27), calls=%async_computation.2 | async-start | bytes 4718592 | tf_op jit(solution)/shard_map/all_to_all | solution.py:412
  186.5 61.0 %all-to-all-start.1 = ((bf16[32,48,768]{2,1,0:T(8,128)(2,1)}), bf16[32,48,768]{2,1,0:T(8,128)(2,1)}, u32[]{:S(2)}, u32[]{:S(2)}) async-start(bf16[32,48,768]{2,1,0:T(8,128)(2,1)} %mix.2.after_ref), calls=%async_computation.1 | async-start | bytes 4718592 | tf_op jit(solution)/shard_map/all_to_all | solution.py:412
  247.4 60.6 %all-to-all-start.3 = ((bf16[32,48,768]{2,1,0:T(8,128)(2,1)}), bf16[32,48,768]{2,1,0:T(8,128)(2,1)}, u32[]{:S(2)}, u32[]{:S(2)}) async-start(bf16[32,48,768]{2,1,0:T(8,128)(2,1)} %mix.3), calls=%async_computation.3 | async-start | bytes 4718592 | tf_op jit(solution)/shard_map/all_to_all | solution.py:412
  270.6 1.5 collective-permute-start.14
  (31 other events, 120.8 us)

commit v6 on v5

--- a/solution.py
+++ b/solution.py
@@ -17,6 +17,10 @@
 out_scale = FF ** (-0.5)
 
 CHUNKS = 2
+Z = 8
+X = 4
+WAY = -1
+MAIN = 640
 BLOCK = 512
 MIB = 1024 * 1024
 VMEM = pl.BlockSpec(memory_space=pltpu.VMEM)
@@ -282,32 +286,38 @@
     )(core, *cots, act_t, weight_out)
 
 
-def update_in_kernel(core, *refs):
-    s_ref, x_ref, wo_ref, wi_ref, o_ref, scratch, sems = refs[2 * CHUNKS :]
+def update_in_kernel(core, place, *refs):
+    s_ref, x_ref, wo_ref, wi_ref, o_ref, v_ref, scratch, sems = refs[2 * CHUNKS :]
     cot, x = all_tokens(core[0], refs[: 2 * CHUNKS]), x_ref[...]
-    parts = blocks(s_ref.shape[0])
-    for i, at in enumerate(parts):
+    rows = v_ref.shape[1]
+    copies = []
+    for i in range(Z // 2):
+        at = pl.ds(2 * i * rows, 2 * rows)
         backward = nn(wo_ref[at, :], cot) * out_scale
         delta = (s_ref[at, :] * backward).astype(BF)
         grad = nn(delta, x) * in_scale
-        scratch[at, :] = (wi_ref[at, :].astype(F32) - step_size * grad).astype(BF)
-        copies_out(scratch, o_ref, sems, i).start()
-    for i in range(len(parts)):
-        copies_out(scratch, o_ref, sems, i).wait()
-
-
-def update_in(core, cots, slopes_t, x_rows, weight_out, weight_in):
+        new = (wi_ref[at, :].astype(F32) - step_size * grad).astype(BF)
+        scratch[at, :] = new[:, :MAIN]
+        for half in range(2):
+            v_ref[lax.rem(WAY * (2 * i + half - place[0]) + 2 * Z, Z)] = new[half * rows : (half + 1) * rows, MAIN:]
+        copies.append(pltpu.make_async_copy(scratch.at[at, :], o_ref.at[at, :], sems.at[i]))
+        copies[-1].start()
+    for copy in copies:
+        copy.wait()
+
+
+def update_in(core, place, cots, slopes_t, x_rows, weight_out, weight_in):
     h, m = slopes_t.shape
     return pl.pallas_call(
         update_in_kernel,
-        out_shape=pltpu.HBM((h, D), BF),
-        in_specs=[SMEM] + [VMEM] * (2 * CHUNKS + 4),
-        out_specs=HBM,
-        scratch_shapes=[pltpu.VMEM((h, D), BF), pltpu.SemaphoreType.DMA((h // BLOCK,))],
+        out_shape=[pltpu.HBM((h, MAIN), BF), jax.ShapeDtypeStruct((Z, h // Z, D - MAIN), BF)],
+        in_specs=[SMEM, SMEM] + [VMEM] * (2 * CHUNKS + 4),
+        out_specs=[HBM, VMEM],
+        scratch_shapes=[pltpu.VMEM((h, MAIN), BF), pltpu.SemaphoreType.DMA((Z // 2,))],
         compiler_params=params(),
         cost_estimate=cost(4 * m * h * D, 4 * m * h + 6 * h * D),
         name="update_in",
-    )(core, *cots, slopes_t, x_rows, weight_out, weight_in)
+    )(core, place, *cots, slopes_t, x_rows, weight_out, weight_in)
 
 
 def mix_kernel(hi_ref, lo_ref, u_ref, after_ref, o_ref):
@@ -363,6 +373,68 @@
         cost_estimate=cost(2 * n * n * matrix.shape[0], 4 * n * n),
         name="spread",
     )(matrix)
+
+
+def side_mix_kernel(place, m_ref, own, one, two, three, o_ref):
+    groups, rows, width = own.shape
+    replicas = Z * X
+    z, x = place[0], place[1]
+    n, k = 16 * groups, 16 * replicas
+
+    def replica_of(group, sign):
+        j, step = group // Z, group % Z
+        return (z + 2 * Z + sign * WAY * step) % Z * X + (x + X - j) % X
+
+    def chosen(shape, along, sign):
+        group = lax.broadcasted_iota(jnp.int32, shape, along) // 16
+        return jnp.where(lax.broadcasted_iota(jnp.int32, shape, 1 - along) == replica_of(group, sign), 1.0, 0.0).astype(BF)
+
+    to, come = chosen((n, replicas), 0, 1), chosen((replicas, k), 1, -1)
+    same = lax.broadcasted_iota(jnp.int32, (n, k), 0) % 16 == lax.broadcasted_iota(jnp.int32, (n, k), 1) % 16
+    left = m_ref[...]
+    spread = []
+    for _ in range(2):
+        part = left.astype(BF)
+        left = left - part.astype(F32)
+        spread.append(jnp.where(same, nn(nn(to, part).astype(BF), come), 0.0).astype(BF))
+    for i in range(rows // 16):
+        at = pl.ds(i * 16, 16)
+        u = jnp.concatenate([ref[:, at, :].reshape(groups * 16, width) for ref in (own, one, two, three)], axis=0)
+        mixed = nn(spread[0], u) + nn(spread[1], u)
+        o_ref[:, at, :] = mixed.astype(BF).reshape(groups, 16, width)
+
+
+def side_mix(place, matrix, pieces):
+    shape = pieces[0].shape
+    return pl.pallas_call(
+        side_mix_kernel,
+        out_shape=jax.ShapeDtypeStruct(shape, BF),
+        in_specs=[SMEM] + [VMEM] * 5,
+        out_specs=VMEM,
+        compiler_params=params(),
+        cost_estimate=cost(8 * Z * 512 * 16 * shape[1] * shape[2] // 16, 10 * pieces[0].size),
+        name="side_mix",
+    )(place, matrix, *pieces)
+
+
+def shifted(shard, along_z, along_x):
+    pairs = []
+    for z in range(Z):
+        for x in range(X):
+            pairs.append((z * X + x, (z + along_z) % Z * X + (x + along_x) % X))
+    return lax.ppermute(shard, "rep", pairs)
+
+
+def first_round(v):
+    return shifted(v[3:], 3 * WAY, 0), shifted(v[2], 2 * WAY, 0), shifted(v[1], WAY, 0)
+
+
+def later_rounds(v, first):
+    third, second, next_one = first
+    fourth, fifth = shifted(third[1], WAY, 0), shifted(third[2], 2 * WAY, 0)
+    sixth = shifted(third[3:], 3 * WAY, 0)
+    seventh = shifted(sixth[1], WAY, 0)
+    return jnp.stack([v[0], next_one, second, third[0], fourth, fifth, sixth[0], seventh])
 
 
 LANDINGS = 6
@@ -399,6 +471,34 @@
     )(array, after)
 
 
+def landed_both_kernel(place, u_ref, v_ref, o_ref, main, held, sems):
+    rows = v_ref.shape[1]
+    load = pltpu.make_async_copy(u_ref, main, sems.at[0])
+    load.start()
+    for step in range(Z):
+        chunk = lax.rem(place[0] - WAY * step + Z, Z)
+        held[pl.ds(pl.multiple_of(chunk * rows, 16), rows), MAIN:] = v_ref[step]
+    load.wait()
+    held[:, :MAIN] = main[...]
+    store = pltpu.make_async_copy(held, o_ref, sems.at[1])
+    store.start()
+    store.wait()
+
+
+def landed_both(place, array, side):
+    h = array.shape[0]
+    return pl.pallas_call(
+        landed_both_kernel,
+        out_shape=pltpu.HBM((h, D), BF),
+        in_specs=[SMEM, ANY, VMEM],
+        out_specs=HBM,
+        scratch_shapes=[pltpu.VMEM(array.shape, BF), pltpu.VMEM((h, D), BF), pltpu.SemaphoreType.DMA((2,))],
+        compiler_params=params(),
+        cost_estimate=cost(0, 4 * h * D),
+        name="landed_both",
+    )(place, array, side)
+
+
 def passed_along(shard):
     length = lax.axis_size("section")
     return lax.ppermute(shard, "section", [(i, i - 1) for i in range(1, length)])
@@ -463,16 +563,27 @@
 
     mine = summed(kept_cot)
     all_cots = mine + [other_core(part) for part in mine]
-    updated_in = update_in(core_at, all_cots, slopes_t, x_rows, weight_out, weight_in)
-    pieces_in = sent_out(updated_in.reshape(replicas, units // replicas, D))
+    place_in_rep = lax.axis_index("rep")
+    place = jnp.stack([place_in_rep // X, place_in_rep % X]).astype(jnp.int32)
+    updated_in, side = update_in(core_at, place, all_cots, slopes_t, x_rows, weight_out, weight_in)
+    pieces_in = sent_out(updated_in.reshape(replicas, units // replicas, MAIN))
     updated_out = update_out(core_at, all_cots, act_t, weight_out)
+    side, updated_out = lax.optimization_barrier((side, updated_out))
+    side_first = first_round(side)
     pieces_out = sent_out(updated_out.reshape(replicas, units // replicas, D))
     mixture_in = mix(hi, lo, pieces_in, mixing)
+    *side_first, mixture_in = lax.optimization_barrier((*side_first, mixture_in))
+    side = later_rounds(side, side_first)
+    side = side_mix(place, mixing, [side] + [shifted(side, 0, j) for j in range(1, X)])
     back_in = sent_out(mixture_in)
-    back_out = sent_out(mix(hi, lo, pieces_out, mixture_in))
-    mixed_in = landed(back_in.reshape(units, D), mixing)
-
-    kept_result.append([turn(cots[c], wouts, wins_t, slopes, c * columns, mixed_in) for c in range(CHUNKS)])
+    mixture_out = mix(hi, lo, pieces_out, mixture_in)
+    side, mixture_out = lax.optimization_barrier((side, mixture_out))
+    side_first = first_round(side)
+    back_out = sent_out(mixture_out)
+    kept_result.append([turn(cots[c], wouts, wins_t, slopes, c * columns, back_in) for c in range(CHUNKS)])
+    *side_first, kept_result[-1][1] = lax.optimization_barrier((*side_first, kept_result[-1][1]))
+    mixed_in = landed_both(place, back_in.reshape(units, MAIN), later_rounds(side, side_first))
+
     result = jnp.concatenate(summed(kept_result), axis=1)
     width = D // 2
     mine = lax.dynamic_slice_in_dim(result, core * width, width, 0)

time: 312 us -> 406 us (1.30); the launches traced: 311 us -> 398 us
  starting transfers between devices: 45.7 us -> 91.9 us
  waiting for transfers between devices: 191 us -> 224 us
  local copies, waits for them, and re-layouts: 15 us -> 19.1 us
    ppermute x0 -> x17, waiting for transfers between devices: none -> 172 us  [shifted(): return lax.ppermute(shard, 'rep', pairs)]
    all_to_all x4, waiting for transfers between devices: 181 us -> 43.9 us  [sent_out(): return lax.all_to_all(block, 'rep', split_axis=0, concat_axis=0, tiled=True)]
    ppermute x0 -> x17, starting transfers between devices: none -> 41.3 us  [shifted(): return lax.ppermute(shard, 'rep', pairs)]
    pallas_call x1 -> x3, Pallas kernels: 3.66 us -> 9.97 us  [the longest x1 4.3 us: update_in(): pl.pallas_call(update_in_kernel, out_shape=[pltpu.HBM((h, MAIN), BF), jax...]
    all_to_all x4, starting transfers between devices: 27 us -> 31.7 us  [sent_out(): return lax.all_to_all(block, 'rep', split_axis=0, concat_axis=0, tiled=True)]
    unnamed x72 -> x98, local copies, waits for them, and re-layouts: 14.3 us -> 16.4 us
  transfers between devices with their start and end apart: 19 -> 36, of which waited for: 9 -> 16; matrix products, arithmetic and copies ran while one was open for 0% -> 1% of each run, Pallas kernels for 16% -> 14%
where the time goes in v6:
time: 406 us; the launch traced here: 398 us
  waiting for transfers between devices  224 us (55%)
  starting transfers between devices  91.9 us (23%)
  Pallas kernels  60.6 us (15%)
  local copies, waits for them, and re-layouts  19.1 us (5%)
    ppermute x17, waiting for transfers between devices, shifted(): return lax.ppermute(shard, 'rep', pairs)  172 us
    all_to_all x4, waiting for transfers between devices, sent_out(): return lax.all_to_all(block, 'rep', split_axis=0, concat_axis=0, tiled=True)  43.9 us
    ppermute x17, starting transfers between devices, shifted(): return lax.ppermute(shard, 'rep', pairs)  41.3 us
    all_to_all x4, starting transfers between devices, sent_out(): return lax.all_to_all(block, 'rep', split_axis=0, concat_axis=0, tiled=True)  31.7 us
    pallas_call x6, Pallas kernels, turn(): pl.pallas_call(lambda *refs: turn_kernel(col0, *refs), out_shape=jax.Shap...  20 us
    ppermute x6, starting transfers between devices, passed_along(): lax.ppermute(shard, 'section', [(i, i - 1) for i in range(1, length)])  16.4 us
    unnamed x98, local copies, waits for them, and re-layouts  16.4 us
    pallas_call x2, Pallas kernels, mix(): pl.pallas_call(mix_kernel, grid=(rows // block,), out_shape=pltpu.HBM(pie...  10.7 us
  transfers between devices with their start and end apart: 36, of which 16 were waited for; matrix products, arithmetic and copies ran while one was open for 1% of the time, Pallas kernels for 14%

profile of v6, /device:TPU:16, one launch (start us, length us, event | category | flops | bytes accessed | tf_op | source)
XLA Modules:
  0.0 398.1 jit_solution(6629491013355709486)
XLA Ops:
  4.3 5.6 %opening.1 = (bf16[512,768]{1,0:T(8,128)(2,1)S(1)}, bf16[256,768]{1,0:T(8,128)(2,1)S(1)}, bf16[768,512]{1,0:T(8,128)(2,1)S(1)}, bf16[1536,512]{1,0:T(8,128)(2,1)...) custom-call(s32[2]{0:T(128)} %pad_add_fusion.at.refs_0_, ...), custom_call_target="tpu_custom_call" | custom-call | flops 1207959552 | bytes 13369344 | tf_op jit(solution)/shard_map/opening/pallas_call | solution.py:99
  18.1 4.3 %collective-permute-start.9 = (bf16[768,128]{1,0:T(8,128)(2,1)S(1)}, bf16[768,128]{1,0:T(8,128)(2,1)S(1)}, u32[]{:S(2)}, u32[]{:S(2)}) collective-permute-start(bf16[768,128]{1,0:T(8,128)(2,1)S(1)} %both_parts.3), channel_id=1, source_target_pairs={{2,0},{4,2},{6,4},{3,1},{5,3},{7,5},{10,8},{12,10},{14,12},{11,9},... | collective-permute-start | bytes 589832 | tf_op jit(solution)/shard_map/ppermute | solution.py:504
  31.5 3.3 turn.8
  34.9 3.7 collective-permute-start.10
  38.5 3.3 turn.7
  49.7 5.1 %collective-permute-done.11.refs_0_ = bf16[768,128]{1,0:T(8,128)(2,1)S(1)} collective-permute-done((bf16[768,128]{1,0:T(8,128)(2,1)S(1)}, bf16[768,128]{1,0:T(8,128)(2,1)S(1)}, u32[]{:S(2)}, u32[]{:S(2)}) %collective-permute-start.11) | collective-permute-done | bytes 196640 | tf_op jit(solution)/shard_map/ppermute | solution.py:504
  61.5 4.3 %update_in.1 = (bf16[1536,640]{1,0:T(8,128)(2,1)}, bf16[8,192,128]{2,1,0:T(8,128)(2,1)S(1)}) custom-call(s32[1]{0:T(128)} %bitcast.core, s32[2]{0:T(128)S(1)} %pad_add_fusion.1.place, bf16[768,128]{1,0:T(8,128)(2,1)S(1)} %add_add_fusion.2.refs_0_, bf16[768,128]{1,0:T(8,128)(2,1)S(1)} %add_add_fusion.1.refs_1_, ...), custom_call_target="tpu_custom_call" | custom-call | flops 2415919104 | bytes 10223616 | tf_op jit(solution)/shard_map/update_in/pallas_call | solution.py:311
  66.5 9.7 %all-to-all-start = ((bf16[32,48,640]{2,1,0:T(8,128)(2,1)}), bf16[32,48,640]{2,1,0:T(8,128)(2,1)}, u32[]{:S(2)}, u32[]{:S(2)}) async-start(bf16[32,48,640]{2,1,0:T(8,128)(2,1)} %bitcast.71), calls=%async_computation | async-start | bytes 3932160 | tf_op jit(solution)/shard_map/all_to_all | solution.py:512
  80.1 43.9 %all-to-all-done.u_ref = bf16[32,48,640]{2,1,0:T(8,128)(2,1)} async-done(((bf16[32,48,640]{2,1,0:T(8,128)(2,1)}), bf16[32,48,640]{2,1,0:T(8,128)(2,1)}, u32[]{:S(2)}, u32[]{:S(2)}) %all-to-all-start) | async-done | bytes 1966112 | tf_op jit(solution)/shard_map/all_to_all | solution.py:512
  123.9 6.1 %all-to-all-start.2 = ((bf16[32,48,768]{2,1,0:T(8,128)(2,1)}), bf16[32,48,768]{2,1,0:T(8,128)(2,1)}, u32[]{:S(2)}, u32[]{:S(2)}) async-start(bf16[32,48,768]{2,1,0:T(8,128)(2,1)} %bitcast.68), calls=%async_computation.2 | async-start | bytes 4718592 | tf_op jit(solution)/shard_map/all_to_all | solution.py:512
  130.8 4.8 %collective-permute-start.14 = (bf16[5,192,128]{2,1,0:T(8,128)(2,1)S(1)}, bf16[5,192,128]{2,1,0:T(8,128)(2,1)}, u32[]{:S(2)}, u32[]{:S(2)}) collective-permute-start(bf16[5,192,128]{2,1,0:T(8,128)(2,1)S(1)} %slice.63), channel_id=1, source_target_pairs={{0,160},{8,168},{16,176},{24,184},{32,192},{40,200},{48,208},{56,2... | collective-permute-start | bytes 737288 | tf_op jit(solution)/shard_map/ppermute | solution.py:425
  137.8 5.3 %mix.2.after_ref = bf16[32,48,640]{2,1,0:T(8,128)(2,1)} custom-call(bf16[512,512]{1,0:T(8,128)(2,1)S(1)} %get-tuple-element.63.hi_ref, bf16[512,512]{1,0:T(8,128)(2,1)S(1)} %get-tuple-element.64.lo_ref, bf16[32,48,640]{2,1,0:T(8,128)(2,1)} %all-to-all-done.u_ref, f32[32,32]{1,0:T(8,128)S(1)} %copy-done.33), custom_call_target="tpu_custom_call" | custom-call | flops 2013265920 | bytes 4980736 | tf_op jit(solution)/shard_map/mix/pallas_call | solution.py:336
  143.0 57.1 %collective-permute-done.15 = bf16[192,128]{1,0:T(8,128)(2,1)S(1)} collective-permute-done((bf16[192,128]{1,0:T(8,128)(2,1)S(1)}, bf16[192,128]{1,0:T(8,128)(2,1)S(1)}, u32[]{:S(2)}, u32[]{:S(2)}) %collective-permute-start.15) | collective-permute-done | bytes 49184 | tf_op jit(solution)/shard_map/ppermute | solution.py:425
  200.8 8.7 %all-to-all-start.1 = ((bf16[32,48,640]{2,1,0:T(8,128)(2,1)}), bf16[32,48,640]{2,1,0:T(8,128)(2,1)}, u32[]{:S(2)}, u32[]{:S(2)}) async-start(bf16[32,48,640]{2,1,0:T(8,128)(2,1)} %mix.2.after_ref), calls=%async_computation.1 | async-start | bytes 3932160 | tf_op jit(solution)/shard_map/all_to_all | solution.py:512
  218.3 39.6 %collective-permute-done.17 = bf16[192,128]{1,0:T(8,128)(2,1)S(1)} collective-permute-done((bf16[192,128]{1,0:T(8,128)(2,1)S(1)}, bf16[192,128]{1,0:T(8,128)(2,1)S(1)}, u32[]{:S(2)}, u32[]{:S(2)}) %collective-permute-start.17) | collective-permute-done | bytes 49184 | tf_op jit(solution)/shard_map/ppermute | solution.py:425
  257.9 3.5 collective-permute-done.18
  261.4 3.5 collective-permute-start.20
  273.1 7.5 %collective-permute-done.21.one = bf16[8,192,128]{2,1,0:T(8,128)(2,1)S(1)} collective-permute-done((bf16[8,192,128]{2,1,0:T(8,128)(2,1)S(1)}, bf16[8,192,128]{2,1,0:T(8,128)(2,1)S(1)}, u32[]{:S(2)}, u32[]{:S(2)}) %collective-permute-start.21) | collective-permute-done | bytes 393248 | tf_op jit(solution)/shard_map/ppermute | solution.py:425
  280.7 4.4 %collective-permute-done.22.two = bf16[8,192,128]{2,1,0:T(8,128)(2,1)S(1)} collective-permute-done((bf16[8,192,128]{2,1,0:T(8,128)(2,1)S(1)}, bf16[8,192,128]{2,1,0:T(8,128)(2,1)S(1)}, u32[]{:S(2)}, u32[]{:S(2)}) %collective-permute-start.22) | collective-permute-done | bytes 393248 | tf_op jit(solution)/shard_map/ppermute | solution.py:425
  287.6 5.5 %mix.3 = bf16[32,48,768]{2,1,0:T(8,128)(2,1)} custom-call(bf16[512,512]{1,0:T(8,128)(2,1)S(1)} %copy-done.39, bf16[512,512]{1,0:T(8,128)(2,1)S(1)} %copy-done.41, bf16[32,48,768]{2,1,0:T(8,128)(2,1)} %all-to-all-done.2.u_ref, bf16[32,48,640]{2,1,0:T(8,128)(2,1)S(1)} %copy-done.14), custom_call_target="tpu_custom_call" | custom-call | flops 2415919104 | bytes 5767168 | tf_op jit(solution)/shard_map/mix/pallas_call | solution.py:336
  293.1 7.2 %all-to-all-start.3 = ((bf16[32,48,768]{2,1,0:T(8,128)(2,1)}), bf16[32,48,768]{2,1,0:T(8,128)(2,1)}, u32[]{:S(2)}, u32[]{:S(2)}) async-start(bf16[32,48,768]{2,1,0:T(8,128)(2,1)} %mix.3), calls=%async_computation.3 | async-start | bytes 4718592 | tf_op jit(solution)/shard_map/all_to_all | solution.py:512
  300.4 4.8 %collective-permute-start.24 = (bf16[5,192,128]{2,1,0:T(8,128)(2,1)S(1)}, bf16[5,192,128]{2,1,0:T(8,128)(2,1)S(1)}, u32[]{:S(2)}, u32[]{:S(2)}) collective-permute-start(bf16[5,192,128]{2,1,0:T(8,128)(2,1)S(1)} %slice.73), channel_id=1, source_target_pairs={{0,160},{8,168},{16,176},{24,184},{32,192},{40,200},{48,208},{56,2... | collective-permute-start | bytes 737288 | tf_op jit(solution)/shard_map/ppermute | solution.py:425
  318.5 51.3 %collective-permute-done.25 = bf16[192,128]{1,0:T(8,128)(2,1)S(1)} collective-permute-done((bf16[192,128]{1,0:T(8,128)(2,1)S(1)}, bf16[192,128]{1,0:T(8,128)(2,1)S(1)}, u32[]{:S(2)}, u32[]{:S(2)}) %collective-permute-start.25) | collective-permute-done | bytes 49184 | tf_op jit(solution)/shard_map/ppermute | solution.py:425
  390.1 3.7 landed_both.1
  (186 shorter events, 100.2 us)
Async XLA Ops:
  3.2 19.2 %collective-permute-start.4 = (bf16[1536,768]{1,0:T(8,128)(2,1)}, bf16[1536,768]{1,0:T(8,128)(2,1)}, u32[]{:S(2)}, u32[]{:S(2)}) collective-permute-start(bf16[1536,768]{1,0:T(8,128)(2,1)} %bitcast.65), channel_id=1, source_target_pairs={{0,1},{1,0},{2,3},{3,2},{4,5},{5,4},{6,7},{7,6},{8,9},{9,8},{10,11... | collective-permute-start | bytes 7077896 | tf_op jit(solution)/shard_map/ppermute | solution.py:508
  3.4 19.1 %collective-permute-start.5 = (bf16[1536,768]{1,0:T(8,128)(2,1)}, bf16[1536,768]{1,0:T(8,128)(2,1)}, u32[]{:S(2)}, u32[]{:S(2)}) collective-permute-start(bf16[1536,768]{1,0:T(8,128)(2,1)} %bitcast.54), channel_id=1, source_target_pairs={{0,1},{1,0},{2,3},{3,2},{4,5},{5,4},{6,7},{7,6},{8,9},{9,8},{10,11... | collective-permute-start | bytes 7077896 | tf_op jit(solution)/shard_map/ppermute | solution.py:508
  15.7 10.5 %collective-permute-start.3 = (bf16[768,128]{1,0:T(8,128)(2,1)S(1)}, bf16[768,128]{1,0:T(8,128)(2,1)S(1)}, u32[]{:S(2)}, u32[]{:S(2)}) collective-permute-start(bf16[768,128]{1,0:T(8,128)(2,1)S(1)} %both_parts.2), channel_id=1, source_target_pairs={{2,0},{4,2},{6,4},{3,1},{5,3},{7,5},{10,8},{12,10},{14,12},{11,9},... | collective-permute-start | bytes 589832 | tf_op jit(solution)/shard_map/ppermute | solution.py:504
  18.1 13.3 %collective-permute-start.9 = (bf16[768,128]{1,0:T(8,128)(2,1)S(1)}, bf16[768,128]{1,0:T(8,128)(2,1)S(1)}, u32[]{:S(2)}, u32[]{:S(2)}) collective-permute-start(bf16[768,128]{1,0:T(8,128)(2,1)S(1)} %both_parts.3), channel_id=1, source_target_pairs={{2,0},{4,2},{6,4},{3,1},{5,3},{7,5},{10,8},{12,10},{14,12},{11,9},... | collective-permute-start | bytes 589832 | tf_op jit(solution)/shard_map/ppermute | solution.py:504
  29.6 9.0 %collective-permute-start.6 = (bf16[768,128]{1,0:T(8,128)(2,1)S(1)}, bf16[768,128]{1,0:T(8,128)(2,1)S(1)}, u32[]{:S(2)}, u32[]{:S(2)}) collective-permute-start(bf16[768,128]{1,0:T(8,128)(2,1)S(1)} %turn.6), channel_id=1, source_target_pairs={{2,0},{4,2},{6,4},{3,1},{5,3},{7,5},{10,8},{12,10},{14,12},{11,9},... | collective-permute-start | bytes 589832 | tf_op jit(solution)/shard_map/ppermute | solution.py:504
  34.9 9.0 %collective-permute-start.10 = (bf16[768,128]{1,0:T(8,128)(2,1)S(1)}, bf16[768,128]{1,0:T(8,128)(2,1)S(1)}, u32[]{:S(2)}, u32[]{:S(2)}) collective-permute-start(bf16[768,128]{1,0:T(8,128)(2,1)S(1)} %turn.8), channel_id=1, source_target_pairs={{2,0},{4,2},{6,4},{3,1},{5,3},{7,5},{10,8},{12,10},{14,12},{11,9},... | collective-permute-start | bytes 589832 | tf_op jit(solution)/shard_map/ppermute | solution.py:504
  66.5 57.4 %all-to-all-start = ((bf16[32,48,640]{2,1,0:T(8,128)(2,1)}), bf16[32,48,640]{2,1,0:T(8,128)(2,1)}, u32[]{:S(2)}, u32[]{:S(2)}) async-start(bf16[32,48,640]{2,1,0:T(8,128)(2,1)} %bitcast.71), calls=%async_computation | async-start | bytes 3932160 | tf_op jit(solution)/shard_map/all_to_all | solution.py:512
  123.9 76.9 %all-to-all-start.2 = ((bf16[32,48,768]{2,1,0:T(8,128)(2,1)}), bf16[32,48,768]{2,1,0:T(8,128)(2,1)}, u32[]{:S(2)}, u32[]{:S(2)}) async-start(bf16[32,48,768]{2,1,0:T(8,128)(2,1)} %bitcast.68), calls=%async_computation.2 | async-start | bytes 4718592 | tf_op jit(solution)/shard_map/all_to_all | solution.py:512
  130.8 70.0 %collective-permute-start.14 = (bf16[5,192,128]{2,1,0:T(8,128)(2,1)S(1)}, bf16[5,192,128]{2,1,0:T(8,128)(2,1)}, u32[]{:S(2)}, u32[]{:S(2)}) collective-permute-start(bf16[5,192,128]{2,1,0:T(8,128)(2,1)S(1)} %slice.63), channel_id=1, source_target_pairs={{0,160},{8,168},{16,176},{24,184},{32,192},{40,200},{48,208},{56,2... | collective-permute-start | bytes 737288 | tf_op jit(solution)/shard_map/ppermute | solution.py:425
  135.7 64.4 %collective-permute-start.15 = (bf16[192,128]{1,0:T(8,128)(2,1)S(1)}, bf16[192,128]{1,0:T(8,128)(2,1)S(1)}, u32[]{:S(2)}, u32[]{:S(2)}) collective-permute-start(bf16[192,128]{1,0:T(8,128)(2,1)S(1)} %get-tuple-element.84), channel_id=1, source_target_pairs={{0,192},{8,200},{16,208},{24,216},{32,224},{40,232},{48,240},{56,2... | collective-permute-start | bytes 147464 | tf_op jit(solution)/shard_map/ppermute | solution.py:425
  137.2 63.6 %collective-permute-start.16 = (bf16[192,128]{1,0:T(8,128)(2,1)S(1)}, bf16[192,128]{1,0:T(8,128)(2,1)S(1)}, u32[]{:S(2)}, u32[]{:S(2)}) collective-permute-start(bf16[192,128]{1,0:T(8,128)(2,1)S(1)} %get-tuple-element.83), channel_id=1, source_target_pairs={{0,224},{8,232},{16,240},{24,248},{32,0},{40,8},{48,16},{56,24},{6... | collective-permute-start | bytes 147464 | tf_op jit(solution)/shard_map/ppermute | solution.py:425
  200.8 92.3 %all-to-all-start.1 = ((bf16[32,48,640]{2,1,0:T(8,128)(2,1)}), bf16[32,48,640]{2,1,0:T(8,128)(2,1)}, u32[]{:S(2)}, u32[]{:S(2)}) async-start(bf16[32,48,640]{2,1,0:T(8,128)(2,1)} %mix.2.after_ref), calls=%async_computation.1 | async-start | bytes 3932160 | tf_op jit(solution)/shard_map/all_to_all | solution.py:512
  210.6 47.3 %collective-permute-start.17 = (bf16[192,128]{1,0:T(8,128)(2,1)S(1)}, bf16[192,128]{1,0:T(8,128)(2,1)S(1)}, u32[]{:S(2)}, u32[]{:S(2)}) collective-permute-start(bf16[192,128]{1,0:T(8,128)(2,1)S(1)} %get-tuple-element.89), channel_id=1, source_target_pairs={{0,224},{8,232},{16,240},{24,248},{32,0},{40,8},{48,16},{56,24},{6... | collective-permute-start | bytes 147464 | tf_op jit(solution)/shard_map/ppermute | solution.py:425
  214.5 46.8 %collective-permute-start.19 = (bf16[2,192,128]{2,1,0:T(8,128)(2,1)S(1)}, bf16[2,192,128]{2,1,0:T(8,128)(2,1)S(1)}, u32[]{:S(2)}, u32[]{:S(2)}) collective-permute-start(bf16[2,192,128]{2,1,0:T(8,128)(2,1)S(1)} %slice.70), channel_id=1, source_target_pairs={{0,160},{8,168},{16,176},{24,184},{32,192},{40,200},{48,208},{56,2... | collective-permute-start | bytes 294920 | tf_op jit(solution)/shard_map/ppermute | solution.py:425
  217.7 43.6 %collective-permute-start.18 = (bf16[192,128]{1,0:T(8,128)(2,1)S(1)}, bf16[192,128]{1,0:T(8,128)(2,1)S(1)}, u32[]{:S(2)}, u32[]{:S(2)}) collective-permute-start(bf16[192,128]{1,0:T(8,128)(2,1)S(1)} %get-tuple-element.88), channel_id=1, source_target_pairs={{0,192},{8,200},{16,208},{24,216},{32,224},{40,232},{48,240},{56,2... | collective-permute-start | bytes 147464 | tf_op jit(solution)/shard_map/ppermute | solution.py:425
  267.2 13.4 %collective-permute-start.21 = (bf16[8,192,128]{2,1,0:T(8,128)(2,1)S(1)}, bf16[8,192,128]{2,1,0:T(8,128)(2,1)S(1)}, u32[]{:S(2)}, u32[]{:S(2)}) collective-permute-start(bf16[8,192,128]{2,1,0:T(8,128)(2,1)S(1)} %bitcast_dynamic-update-slice_fusion.5.own), channel_id=1, source_target_pairs={{0,8},{8,16},{16,24},{24,0},{32,40},{40,48},{48,56},{56,32},{64,72... | collective-permute-start | bytes 1179656 | tf_op jit(solution)/shard_map/ppermute | solution.py:425
  269.0 16.1 %collective-permute-start.22 = (bf16[8,192,128]{2,1,0:T(8,128)(2,1)S(1)}, bf16[8,192,128]{2,1,0:T(8,128)(2,1)S(1)}, u32[]{:S(2)}, u32[]{:S(2)}) collective-permute-start(bf16[8,192,128]{2,1,0:T(8,128)(2,1)S(1)} %bitcast_dynamic-update-slice_fusion.5.own), channel_id=1, source_target_pairs={{0,16},{8,24},{16,0},{24,8},{32,48},{40,56},{48,32},{56,40},{64,80... | collective-permute-start | bytes 1179656 | tf_op jit(solution)/shard_map/ppermute | solution.py:425
  271.5 13.5 %collective-permute-start.23 = (bf16[8,192,128]{2,1,0:T(8,128)(2,1)S(1)}, bf16[8,192,128]{2,1,0:T(8,128)(2,1)S(1)}, u32[]{:S(2)}, u32[]{:S(2)}) collective-permute-start(bf16[8,192,128]{2,1,0:T(8,128)(2,1)S(1)} %bitcast_dynamic-update-slice_fusion.5.own), channel_id=1, source_target_pairs={{0,24},{8,0},{16,8},{24,16},{32,56},{40,32},{48,40},{56,48},{64,88... | collective-permute-start | bytes 1179656 | tf_op jit(solution)/shard_map/ppermute | solution.py:425
  293.1 102.3 %all-to-all-start.3 = ((bf16[32,48,768]{2,1,0:T(8,128)(2,1)}), bf16[32,48,768]{2,1,0:T(8,128)(2,1)}, u32[]{:S(2)}, u32[]{:S(2)}) async-start(bf16[32,48,768]{2,1,0:T(8,128)(2,1)} %mix.3), calls=%async_computation.3 | async-start | bytes 4718592 | tf_op jit(solution)/shard_map/all_to_all | solution.py:512
  300.4 69.9 %collective-permute-start.24 = (bf16[5,192,128]{2,1,0:T(8,128)(2,1)S(1)}, bf16[5,192,128]{2,1,0:T(8,128)(2,1)S(1)}, u32[]{:S(2)}, u32[]{:S(2)}) collective-permute-start(bf16[5,192,128]{2,1,0:T(8,128)(2,1)S(1)} %slice.73), channel_id=1, source_target_pairs={{0,160},{8,168},{16,176},{24,184},{32,192},{40,200},{48,208},{56,2... | collective-permute-start | bytes 737288 | tf_op jit(solution)/shard_map/ppermute | solution.py:425
  305.2 64.5 %collective-permute-start.25 = (bf16[192,128]{1,0:T(8,128)(2,1)S(1)}, bf16[192,128]{1,0:T(8,128)(2,1)S(1)}, u32[]{:S(2)}, u32[]{:S(2)}) collective-permute-start(bf16[192,128]{1,0:T(8,128)(2,1)S(1)} %get-tuple-element.79), channel_id=1, source_target_pairs={{0,192},{8,200},{16,208},{24,216},{32,224},{40,232},{48,240},{56,2... | collective-permute-start | bytes 147464 | tf_op jit(solution)/shard_map/ppermute | solution.py:425
  306.7 63.6 %collective-permute-start.26 = (bf16[192,128]{1,0:T(8,128)(2,1)S(1)}, bf16[192,128]{1,0:T(8,128)(2,1)S(1)}, u32[]{:S(2)}, u32[]{:S(2)}) collective-permute-start(bf16[192,128]{1,0:T(8,128)(2,1)S(1)} %get-tuple-element.78), channel_id=1, source_target_pairs={{0,224},{8,232},{16,240},{24,248},{32,0},{40,8},{48,16},{56,24},{6... | collective-permute-start | bytes 147464 | tf_op jit(solution)/shard_map/ppermute | solution.py:425
  370.4 11.7 %collective-permute-start.28 = (bf16[192,128]{1,0:T(8,128)(2,1)S(1)}, bf16[192,128]{1,0:T(8,128)(2,1)S(1)}, u32[]{:S(2)}, u32[]{:S(2)}) collective-permute-start(bf16[192,128]{1,0:T(8,128)(2,1)S(1)} %get-tuple-element.86), channel_id=1, source_target_pairs={{0,224},{8,232},{16,240},{24,248},{32,0},{40,8},{48,16},{56,24},{6... | collective-permute-start | bytes 147464 | tf_op jit(solution)/shard_map/ppermute | solution.py:425
  376.2 9.1 %collective-permute-start.30 = (bf16[2,192,128]{2,1,0:T(8,128)(2,1)S(1)}, bf16[2,192,128]{2,1,0:T(8,128)(2,1)S(1)}, u32[]{:S(2)}, u32[]{:S(2)}) collective-permute-start(bf16[2,192,128]{2,1,0:T(8,128)(2,1)S(1)} %slice.80), channel_id=1, source_target_pairs={{0,160},{8,168},{16,176},{24,184},{32,192},{40,200},{48,208},{56,2... | collective-permute-start | bytes 294920 | tf_op jit(solution)/shard_map/ppermute | solution.py:425
  (56 other events, 430.0 us)

commit v7 on v5

--- a/solution.py
+++ b/solution.py
@@ -251,92 +251,74 @@
     return jnp.where(core == 0, beside(mine, theirs), beside(theirs, mine))
 
 
-def copies_out(scratch, o_ref, sems, i):
-    at = pl.ds(i * BLOCK, BLOCK)
-    return pltpu.make_async_copy(scratch.at[at, :], o_ref.at[at, :], sems.at[i])
-
-
-def update_out_kernel(core, *refs):
-    a_ref, w_ref, o_ref, scratch, sems = refs[2 * CHUNKS :]
-    cot = jnp.transpose(all_tokens(core[0], refs[: 2 * CHUNKS]))
-    parts = blocks(a_ref.shape[0])
-    for i, at in enumerate(parts):
-        grad = nn(a_ref[at, :], cot) * out_scale
-        scratch[at, :] = (w_ref[at, :].astype(F32) - step_size * grad).astype(BF)
-        copies_out(scratch, o_ref, sems, i).start()
-    for i in range(len(parts)):
-        copies_out(scratch, o_ref, sems, i).wait()
-
-
-def update_out(core, cots, act_t, weight_out):
-    h, m = act_t.shape
-    return pl.pallas_call(
-        update_out_kernel,
-        out_shape=pltpu.HBM((h, D), BF),
-        in_specs=[SMEM] + [VMEM] * (2 * CHUNKS + 2),
+PARTS = 4
+
+
+def update_kernel(core, *refs):
+    a_ref, s_ref, x_ref, wo_ref, wi_ref, o_ref, scratch, sems = refs[2 * CHUNKS :]
+    cot_t, x = all_tokens(core[0], refs[: 2 * CHUNKS]), x_ref[...]
+    cot = jnp.transpose(cot_t)
+    _, replicas, rows, _ = scratch.shape
+    group = replicas // PARTS
+    copies = []
+
+    def finish(which, i, weight, grad):
+        new = (weight.astype(F32) - step_size * grad).astype(BF)
+        at = pl.ds(i * group, group)
+        scratch[which, at] = new.reshape(group, rows, D)
+        copies.append(pltpu.make_async_copy(scratch.at[which, at], o_ref.at[at, which], sems.at[which, i]))
+        copies[-1].start()
+
+    for i in range(PARTS):
+        at = pl.ds(i * group * rows, group * rows)
+        finish(1, i, wo_ref[at, :], nn(a_ref[at, :], cot) * out_scale)
+        backward = nn(wo_ref[at, :], cot_t) * out_scale
+        delta = (s_ref[at, :] * backward).astype(BF)
+        finish(0, i, wi_ref[at, :], nn(delta, x) * in_scale)
+    for copy in copies:
+        copy.wait()
+
+
+def update(replicas, core, cots, act_t, slopes_t, x_rows, weight_out, weight_in):
+    h, m = slopes_t.shape
+    rows = h // replicas
+    return pl.pallas_call(
+        update_kernel,
+        out_shape=pltpu.HBM((replicas, 2, rows, D), BF),
+        in_specs=[SMEM] + [VMEM] * (2 * CHUNKS + 5),
         out_specs=HBM,
-        scratch_shapes=[pltpu.VMEM((h, D), BF), pltpu.SemaphoreType.DMA((h // BLOCK,))],
-        compiler_params=params(),
-        cost_estimate=cost(2 * m * h * D, 2 * m * h + 4 * h * D),
-        name="update_out",
-    )(core, *cots, act_t, weight_out)
-
-
-def update_in_kernel(core, *refs):
-    s_ref, x_ref, wo_ref, wi_ref, o_ref, scratch, sems = refs[2 * CHUNKS :]
-    cot, x = all_tokens(core[0], refs[: 2 * CHUNKS]), x_ref[...]
-    parts = blocks(s_ref.shape[0])
-    for i, at in enumerate(parts):
-        backward = nn(wo_ref[at, :], cot) * out_scale
-        delta = (s_ref[at, :] * backward).astype(BF)
-        grad = nn(delta, x) * in_scale
-        scratch[at, :] = (wi_ref[at, :].astype(F32) - step_size * grad).astype(BF)
-        copies_out(scratch, o_ref, sems, i).start()
-    for i in range(len(parts)):
-        copies_out(scratch, o_ref, sems, i).wait()
-
-
-def update_in(core, cots, slopes_t, x_rows, weight_out, weight_in):
-    h, m = slopes_t.shape
-    return pl.pallas_call(
-        update_in_kernel,
-        out_shape=pltpu.HBM((h, D), BF),
-        in_specs=[SMEM] + [VMEM] * (2 * CHUNKS + 4),
-        out_specs=HBM,
-        scratch_shapes=[pltpu.VMEM((h, D), BF), pltpu.SemaphoreType.DMA((h // BLOCK,))],
-        compiler_params=params(),
-        cost_estimate=cost(4 * m * h * D, 4 * m * h + 6 * h * D),
-        name="update_in",
-    )(core, *cots, slopes_t, x_rows, weight_out, weight_in)
-
-
-def mix_kernel(hi_ref, lo_ref, u_ref, after_ref, o_ref):
-    replicas, rows, width = u_ref.shape
-    u = u_ref[...].reshape(replicas * rows, width)
-    mixed = nn(hi_ref[...], u) + nn(lo_ref[...], u)
-    o_ref[...] = mixed.astype(BF).reshape(replicas, rows, width)
-
-
-def mix(hi, lo, pieces, after):
-    replicas, rows, width = pieces.shape
+        scratch_shapes=[pltpu.VMEM((2, replicas, rows, D), BF), pltpu.SemaphoreType.DMA((2, PARTS))],
+        compiler_params=params(24),
+        cost_estimate=cost(6 * m * h * D, 6 * m * h + 8 * h * D),
+        name="update",
+    )(core, *cots, act_t, slopes_t, x_rows, weight_out, weight_in)
+
+
+def mix_kernel(m_ref, u_ref, o_ref):
+    replicas, _, rows, width = u_ref.shape
+    mixed = nn(m_ref[...], u_ref[...].reshape(replicas * rows, width))
+    o_ref[...] = mixed.astype(BF).reshape(replicas, 1, rows, width)
+
+
+def mix(spread, pieces):
+    replicas, both, rows, width = pieces.shape
     block = 16
-    n = hi.shape[0]
-    matrix = pl.BlockSpec((n, n), lambda i: (0, 0))
-    piece = pl.BlockSpec((replicas, block, width), lambda i: (0, i, 0))
+    n = spread.shape[0]
+    piece = pl.BlockSpec((replicas, 1, block, width), lambda w, i: (0, w, i, 0))
     return pl.pallas_call(
         mix_kernel,
-        grid=(rows // block,),
+        grid=(both, rows // block),
         out_shape=pltpu.HBM(pieces.shape, BF),
-        in_specs=[matrix, matrix, piece, ANY],
+        in_specs=[pl.BlockSpec((n, n), lambda w, i: (0, 0)), piece],
         out_specs=piece,
         compiler_params=params(),
-        cost_estimate=cost(4 * n * n * width * rows // block, 4 * pieces.size + 4 * n * n),
+        cost_estimate=cost(2 * n * n * width * both * rows // block, 4 * pieces.size + 2 * n * n),
         name="mix",
-    )(hi, lo, pieces, after)
-
-
-def spread_kernel(m_ref, hi_ref, lo_ref):
-    n, replicas = hi_ref.shape[0], m_ref.shape[0]
+    )(spread, pieces)
+
+
+def spread_kernel(m_ref, o_ref):
+    n, replicas = o_ref.shape[0], m_ref.shape[0]
     narrow = n // replicas
 
     def chosen(shape, along):
@@ -345,34 +327,31 @@
 
     rows, columns = chosen((n, replicas), 0), chosen((replicas, n), 1)
     same = lax.broadcasted_iota(jnp.int32, (n, n), 0) % narrow == lax.broadcasted_iota(jnp.int32, (n, n), 1) % narrow
-    left = m_ref[...]
-    for ref in (hi_ref, lo_ref):
-        part = left.astype(BF)
-        left = left - part.astype(F32)
-        ref[...] = jnp.where(same, nn(nn(rows, part).astype(BF), columns), 0.0).astype(BF)
+    spread = nn(nn(rows, m_ref[...].astype(BF)).astype(BF), columns)
+    o_ref[...] = jnp.where(same, spread, 0.0).astype(BF)
 
 
 def spread_matrix(matrix):
     n = 16 * matrix.shape[0]
     return pl.pallas_call(
         spread_kernel,
-        out_shape=[jax.ShapeDtypeStruct((n, n), BF)] * 2,
+        out_shape=jax.ShapeDtypeStruct((n, n), BF),
         in_specs=[VMEM],
-        out_specs=[VMEM, VMEM],
+        out_specs=VMEM,
         compiler_params=params(),
         cost_estimate=cost(2 * n * n * matrix.shape[0], 4 * n * n),
         name="spread",
     )(matrix)
 
 
-LANDINGS = 6
-
-
-def landed_kernel(u_ref, after_ref, o_ref, held, into, out_of):
-    rows = u_ref.shape[0] // LANDINGS
-    at = [pl.ds(i * rows, rows) for i in range(LANDINGS)]
-    loads = [pltpu.make_async_copy(u_ref.at[at[i], :], held.at[at[i], :], into.at[i]) for i in range(LANDINGS)]
-    stores = [pltpu.make_async_copy(held.at[at[i], :], o_ref.at[at[i], :], out_of.at[i]) for i in range(LANDINGS)]
+def landed_kernel(u_ref, after_ref, in_ref, out_ref, held, into, out_of):
+    group = u_ref.shape[0] // PARTS
+    loads, stores = [], []
+    for which, o_ref in enumerate((in_ref, out_ref)):
+        for i in range(PARTS):
+            at = pl.ds(i * group, group)
+            loads.append(pltpu.make_async_copy(u_ref.at[at, which], held.at[which, at], into.at[which, i]))
+            stores.append(pltpu.make_async_copy(held.at[which, at], o_ref.at[at], out_of.at[which, i]))
     for load in loads:
         load.start()
     for load, store in zip(loads, stores):
@@ -383,15 +362,16 @@
 
 
 def landed(array, after):
+    replicas, both, rows, width = array.shape
     return pl.pallas_call(
         landed_kernel,
-        out_shape=pltpu.HBM(array.shape, BF),
+        out_shape=[pltpu.HBM((replicas, rows, width), BF)] * both,
         in_specs=[ANY, ANY],
-        out_specs=HBM,
+        out_specs=[HBM] * both,
         scratch_shapes=[
-            pltpu.VMEM(array.shape, BF),
-            pltpu.SemaphoreType.DMA((LANDINGS,)),
-            pltpu.SemaphoreType.DMA((LANDINGS,)),
+            pltpu.VMEM((both, replicas, rows, width), BF),
+            pltpu.SemaphoreType.DMA((both, PARTS)),
+            pltpu.SemaphoreType.DMA((both, PARTS)),
         ],
         compiler_params=params(),
         cost_estimate=cost(0, 4 * array.size),
@@ -425,16 +405,18 @@
 
     core_at = jnp.reshape(core, (1,)).astype(jnp.int32)
     last = (segment_index == segments - 1).astype(jnp.int32)
+    at = jnp.stack([core.astype(jnp.int32), last])
     other_x = other_core(inputs[0])
     other_dy = other_core(loss_grad)
-    late_in, late_out, other_x, other_dy = lax.optimization_barrier((weight_in, weight_out, other_x, other_dy))
+    late_in, late_out, other_x, other_dy, at = lax.optimization_barrier(
+        (weight_in, weight_out, other_x, other_dy, at)
+    )
     other_in = other_core(late_in)
     other_out = other_core(late_out)
-    at = jnp.stack([core.astype(jnp.int32), last])
     x_rows, x_own, cot, act_t, slopes_t, own_slopes, own_in_t = opening(
         at, inputs[0], other_x, loss_grad, other_dy, weight_in
     )
-    hi, lo = spread_matrix(mixing)
+    spread = spread_matrix(mixing)
 
     columns = own // CHUNKS
     halves = [first_turn(at, c, cot, weight_out, own_in_t, slopes_t) for c in range(CHUNKS)]
@@ -463,23 +445,19 @@
 
     mine = summed(kept_cot)
     all_cots = mine + [other_core(part) for part in mine]
-    updated_in = update_in(core_at, all_cots, slopes_t, x_rows, weight_out, weight_in)
-    pieces_in = sent_out(updated_in.reshape(replicas, units // replicas, D))
-    updated_out = update_out(core_at, all_cots, act_t, weight_out)
-    pieces_out = sent_out(updated_out.reshape(replicas, units // replicas, D))
-    mixture_in = mix(hi, lo, pieces_in, mixing)
-    back_in = sent_out(mixture_in)
-    back_out = sent_out(mix(hi, lo, pieces_out, mixture_in))
-    mixed_in = landed(back_in.reshape(units, D), mixing)
-
-    kept_result.append([turn(cots[c], wouts, wins_t, slopes, c * columns, mixed_in) for c in range(CHUNKS)])
+    updated = update(replicas, core_at, all_cots, act_t, slopes_t, x_rows, weight_out, weight_in)
+    back = sent_out(mix(spread, sent_out(updated)))
+
+    after = updated[0, 0, :16, :128]
+    kept_result.append([turn(cots[c], wouts, wins_t, slopes, c * columns, after) for c in range(CHUNKS)])
     result = jnp.concatenate(summed(kept_result), axis=1)
     width = D // 2
     mine = lax.dynamic_slice_in_dim(result, core * width, width, 0)
     theirs = other_core(lax.dynamic_slice_in_dim(result, (1 - core) * width, width, 0))
     dx = leaving(core_at, mine, theirs)
-    mixed_out = landed(back_out.reshape(units, D), dx[:16, :128])
-    return dx[None], mixed_in[None, None], mixed_out[None, None]
+    mixed_in, mixed_out = landed(back, dx[:16, :128])
+    whole = (1, 1, units, D)
+    return dx[None], mixed_in.reshape(whole), mixed_out.reshape(whole)
 
 
 def solution(mesh):

time: 312 us -> 306 us (0.981)
  waiting for transfers between devices: 191 us -> 202 us
  Pallas kernels: 57.1 us -> 49.1 us
  starting transfers between devices: 45.7 us -> 38.5 us
  local copies, waits for them, and re-layouts: 15 us -> 10 us
    all_to_all x4 -> x2, waiting for transfers between devices: 181 us -> 192 us  [sent_out(): return lax.all_to_all(block, 'rep', split_axis=0, concat_axis=0, tiled=True)]
    all_to_all x4 -> x2, starting transfers between devices: 27 us -> 18.9 us  [sent_out(): return lax.all_to_all(block, 'rep', split_axis=0, concat_axis=0, tiled=True)]
    pallas_call x7 -> x4, Pallas kernels: 22.8 us -> 17 us  [the longest x1 7.39 us: mix(): pl.pallas_call(mix_kernel, grid=(both, rows // block), out_shape=pltpu.HB...]
    unnamed x72 -> x52, local copies, waits for them, and re-layouts: 14.3 us -> 8.65 us
  transfers between devices with their start and end apart: 19 -> 17, of which waited for: 9 -> 8; matrix products, arithmetic and copies ran while one was open for 0% -> 1% of each run, Pallas kernels for 16% -> 11%
where the time goes in v7:
time: 306 us; the launch traced here: 302 us
  waiting for transfers between devices  202 us (66%)
  Pallas kernels  49.1 us (16%)
  starting transfers between devices  38.5 us (13%)
  local copies, waits for them, and re-layouts  10 us (3%)
    all_to_all x2, waiting for transfers between devices, sent_out(): return lax.all_to_all(block, 'rep', split_axis=0, concat_axis=0, tiled=True)  192 us
    pallas_call x6, Pallas kernels, turn(): pl.pallas_call(lambda *refs: turn_kernel(col0, *refs), out_shape=jax.Shap...  20 us
    all_to_all x2, starting transfers between devices, sent_out(): return lax.all_to_all(block, 'rep', split_axis=0, concat_axis=0, tiled=True)  18.9 us
    ppermute x6, starting transfers between devices, passed_along(): lax.ppermute(shard, 'section', [(i, i - 1) for i in range(1, length)])  17.2 us
    unnamed x52, local copies, waits for them, and re-layouts  8.65 us
    pallas_call x1, Pallas kernels, mix(): pl.pallas_call(mix_kernel, grid=(both, rows // block), out_shape=pltpu.HB...  7.39 us
    ppermute x6, waiting for transfers between devices, passed_along(): lax.ppermute(shard, 'section', [(i, i - 1) for i in range(1, length)])  6.39 us
  transfers between devices with their start and end apart: 17, of which 8 were waited for; matrix products, arithmetic and copies ran while one was open for 1% of the time, Pallas kernels for 11%

profile of v7, /device:TPU:16, one launch (start us, length us, event | category | flops | bytes accessed | tf_op | source)
XLA Modules:
  0.0 302.1 jit_solution(15811434845340878416)
XLA Ops:
  4.5 5.4 %opening.1 = (bf16[512,768]{1,0:T(8,128)(2,1)S(1)}, bf16[256,768]{1,0:T(8,128)(2,1)S(1)}, bf16[768,512]{1,0:T(8,128)(2,1)S(1)}, bf16[1536,512]{1,0:T(8,128)(2,1)...) custom-call(s32[2]{0:T(128)} %pad_add_fusion.at.refs_0_, ...), custom_call_target="tpu_custom_call" | custom-call | flops 1207959552 | bytes 13369344 | tf_op jit(solution)/shard_map/opening/pallas_call | solution.py:95
  10.0 2.0 first_turn.2
  12.2 2.0 first_turn.3
  14.8 2.4 collective-permute-start.3
  17.3 4.3 %collective-permute-start.9 = (bf16[768,128]{1,0:T(8,128)(2,1)S(1)}, bf16[768,128]{1,0:T(8,128)(2,1)S(1)}, u32[]{:S(2)}, u32[]{:S(2)}) collective-permute-start(bf16[768,128]{1,0:T(8,128)(2,1)S(1)} %both_parts.3), channel_id=1, source_target_pairs={{2,0},{4,2},{6,4},{3,1},{5,3},{7,5},{10,8},{12,10},{14,12},{11,9},... | collective-permute-start | bytes 589832 | tf_op jit(solution)/shard_map/ppermute | solution.py:384
  24.5 3.3 %turn.6 = bf16[768,128]{1,0:T(8,128)(2,1)S(1)} custom-call(bf16[768,128]{1,0:T(8,128)(2,1)S(1)} %collective-permute-done.3.refs_0_, bf16[1536,768]{1,0:T(8,128)(2,1)S(1)} %bitcast.13, bf16[1536,768]{1,0:T(8,128)(2,1)S(1)} %get-tuple-element.38.refs_2_, bf16[768,1536]{1,0:T(8,128)(2,1)S(1)} %get-tuple-element.31.refs_3_, ...), custom_call_target="tpu_custom_call" | custom-call | flops 1207959552 | bytes 11010048 | tf_op jit(solution)/shard_map/turn/pallas_call | solution.py:217
  27.8 2.1 collective-permute-start.6
  29.9 3.3 %turn.8 = bf16[768,128]{1,0:T(8,128)(2,1)S(1)} custom-call(bf16[768,128]{1,0:T(8,128)(2,1)S(1)} %collective-permute-done.9.refs_0_, bf16[1536,768]{1,0:T(8,128)(2,1)S(1)} %bitcast.14, bf16[1536,768]{1,0:T(8,128)(2,1)S(1)} %get-tuple-element.38.refs_2_, bf16[768,1536]{1,0:T(8,128)(2,1)S(1)} %get-tuple-element.31.refs_3_, ...), custom_call_target="tpu_custom_call" | custom-call | flops 1207959552 | bytes 11010048 | tf_op jit(solution)/shard_map/turn/pallas_call | solution.py:217
  33.2 4.4 %collective-permute-start.10 = (bf16[768,128]{1,0:T(8,128)(2,1)S(1)}, bf16[768,128]{1,0:T(8,128)(2,1)S(1)}, u32[]{:S(2)}, u32[]{:S(2)}) collective-permute-start(bf16[768,128]{1,0:T(8,128)(2,1)S(1)} %turn.8), channel_id=1, source_target_pairs={{2,0},{4,2},{6,4},{3,1},{5,3},{7,5},{10,8},{12,10},{14,12},{11,9},... | collective-permute-start | bytes 589832 | tf_op jit(solution)/shard_map/ppermute | solution.py:384
  37.7 3.3 %turn.7 = bf16[768,128]{1,0:T(8,128)(2,1)S(1)} custom-call(bf16[768,128]{1,0:T(8,128)(2,1)S(1)} %collective-permute-done.6.refs_0_, bf16[1536,768]{1,0:T(8,128)(2,1)S(1)} %bitcast.15, bf16[1536,768]{1,0:T(8,128)(2,1)S(1)} %get-tuple-element.38.refs_2_, bf16[768,1536]{1,0:T(8,128)(2,1)S(1)} %get-tuple-element.31.refs_3_, ...), custom_call_target="tpu_custom_call" | custom-call | flops 1207959552 | bytes 11010048 | tf_op jit(solution)/shard_map/turn/pallas_call | solution.py:217
  41.0 1.9 collective-permute-start.7
  43.0 3.3 %turn.9 = bf16[768,128]{1,0:T(8,128)(2,1)S(1)} custom-call(bf16[768,128]{1,0:T(8,128)(2,1)S(1)} %collective-permute-done.10.refs_0_, bf16[1536,768]{1,0:T(8,128)(2,1)S(1)} %bitcast.16, bf16[1536,768]{1,0:T(8,128)(2,1)S(1)} %get-tuple-element.38.refs_2_, bf16[768,1536]{1,0:T(8,128)(2,1)S(1)} %get-tuple-element.31.refs_3_, ...), custom_call_target="tpu_custom_call" | custom-call | flops 1207959552 | bytes 11010048 | tf_op jit(solution)/shard_map/turn/pallas_call | solution.py:217
  46.4 2.2 collective-permute-start.11
  48.8 5.1 %collective-permute-done.11.refs_0_ = bf16[768,128]{1,0:T(8,128)(2,1)S(1)} collective-permute-done((bf16[768,128]{1,0:T(8,128)(2,1)S(1)}, bf16[768,128]{1,0:T(8,128)(2,1)S(1)}, u32[]{:S(2)}, u32[]{:S(2)}) %collective-permute-start.11) | collective-permute-done | bytes 196640 | tf_op jit(solution)/shard_map/ppermute | solution.py:384
  55.7 5.1 %update.1 = bf16[32,2,48,768]{3,2,1,0:T(8,128)(2,1)} custom-call(s32[1]{0:T(128)} %bitcast.core, bf16[768,128]{1,0:T(8,128)(2,1)S(1)} %add_add_fusion.2.refs_0_, bf16[768,128]{1,0:T(8,128)(2,1)S(1)} %add_add_fusion.1.refs_1_, bf16[768,128]{1,0:T(8,128)(2,1)S(1)} %collective-permute-done.12.refs_2_, bf16[768,128]{1,0:T(8,128)(2,1)S(1)} %collective-permute-done.13.refs_3_, ...), custom_call_target="tpu_custom_call" | custom-call | flops 3623878656 | bytes 14155776 | tf_op jit(solution)/shard_map/update/pallas_call | solution.py:285
  60.8 9.7 %all-to-all-start = ((bf16[32,2,48,768]{3,2,1,0:T(8,128)(2,1)}), bf16[32,2,48,768]{3,2,1,0:T(8,128)(2,1)}, u32[]{:S(2)}, u32[]{:S(2)}) async-start(bf16[32,2,48,768]{3,2,1,0:T(8,128)(2,1)} %update.1), calls=%async_computation | async-start | bytes 9437184 | tf_op jit(solution)/shard_map/all_to_all | solution.py:392
  71.0 105.0 %all-to-all-done.u_ref = bf16[32,2,48,768]{3,2,1,0:T(8,128)(2,1)} async-done(((bf16[32,2,48,768]{3,2,1,0:T(8,128)(2,1)}), bf16[32,2,48,768]{3,2,1,0:T(8,128)(2,1)}, u32[]{:S(2)}, u32[]{:S(2)}) %all-to-all-start) | async-done | bytes 4718624 | tf_op jit(solution)/shard_map/all_to_all | solution.py:392
  175.9 7.4 %mix.1 = bf16[32,2,48,768]{3,2,1,0:T(8,128)(2,1)} custom-call(bf16[512,512]{1,0:T(8,128)(2,1)S(1)} %spread.1.m_ref, bf16[32,2,48,768]{3,2,1,0:T(8,128)(2,1)} %all-to-all-done.u_ref), custom_call_target="tpu_custom_call" | custom-call | flops 2415919104 | bytes 9961472 | tf_op jit(solution)/shard_map/mix/pallas_call | solution.py:308
  183.3 9.2 %all-to-all-start.1 = ((bf16[32,2,48,768]{3,2,1,0:T(8,128)(2,1)}), bf16[32,2,48,768]{3,2,1,0:T(8,128)(2,1)}, u32[]{:S(2)}, u32[]{:S(2)}) async-start(bf16[32,2,48,768]{3,2,1,0:T(8,128)(2,1)} %mix.1), calls=%async_computation.1 | async-start | bytes 9437184 | tf_op jit(solution)/shard_map/all_to_all | solution.py:392
  193.3 1.7 copy-done.2
  201.1 3.3 %turn.11 = bf16[768,128]{1,0:T(8,128)(2,1)S(1)} custom-call(bf16[768,128]{1,0:T(8,128)(2,1)S(1)} %copy-done.13, bf16[1536,768]{1,0:T(8,128)(2,1)S(1)} %bitcast.18, bf16[1536,768]{1,0:T(8,128)(2,1)S(1)} %copy-done.4, bf16[768,1536]{1,0:T(8,128)(2,1)S(1)} %copy-done.2, bf16[768,1536]{1,0:T(8,128)(2,1)S(1)} %copy-done.6, f32[1536,256]{1,0:T(8,128)S(1)} %copy-done.8, ...), custom_call_target="tpu_custom_call" | custom-call | flops 1207959552 | bytes 11010048 | tf_op jit(solution)/shard_map/turn/pallas_call | solution.py:217
  204.4 3.3 %turn.10 = bf16[768,128]{1,0:T(8,128)(2,1)S(1)} custom-call(bf16[768,128]{1,0:T(8,128)(2,1)S(1)} %collective-permute-done.7.refs_0_, bf16[1536,768]{1,0:T(8,128)(2,1)S(1)} %bitcast.19, bf16[1536,768]{1,0:T(8,128)(2,1)S(1)} %copy-done.4, bf16[768,1536]{1,0:T(8,128)(2,1)S(1)} %copy-done.2, bf16[768,1536]{1,0:T(8,128)(2,1)S(1)} %copy-done.6, ...), custom_call_target="tpu_custom_call" | custom-call | flops 1207959552 | bytes 11010048 | tf_op jit(solution)/shard_map/turn/pallas_call | solution.py:217
  211.1 86.7 %all-to-all-done.1.u_ref = bf16[32,2,48,768]{3,2,1,0:T(8,128)(2,1)} async-done(((bf16[32,2,48,768]{3,2,1,0:T(8,128)(2,1)}), bf16[32,2,48,768]{3,2,1,0:T(8,128)(2,1)}, u32[]{:S(2)}, u32[]{:S(2)}) %all-to-all-start.1) | async-done | bytes 4718624 | tf_op jit(solution)/shard_map/all_to_all | solution.py:392
  297.8 4.1 %landed.1 = (bf16[32,48,768]{2,1,0:T(8,128)(2,1)}, bf16[32,48,768]{2,1,0:T(8,128)(2,1)}) custom-call(bf16[32,2,48,768]{3,2,1,0:T(8,128)(2,1)} %all-to-all-done.1.u_ref, bf16[16,128]{1,0:T(8,128)(2,1)S(1)} %slice.9.after_ref), custom_call_target="tpu_custom_call" | custom-call | bytes 9437184 | tf_op jit(solution)/shard_map/landed/pallas_call | solution.py:366
  (87 shorter events, 20.0 us)
Async XLA Ops:
  0.6 2.0 collective-permute-start
  0.7 2.5 collective-permute-start.1
  4.0 17.6 %collective-permute-start.4 = (bf16[1536,768]{1,0:T(8,128)(2,1)}, bf16[1536,768]{1,0:T(8,128)(2,1)S(1)}, u32[]{:S(2)}, u32[]{:S(2)}) collective-permute-start(bf16[1536,768]{1,0:T(8,128)(2,1)} %bitcast.20), channel_id=1, source_target_pairs={{0,1},{1,0},{2,3},{3,2},{4,5},{5,4},{6,7},{7,6},{8,9},{9,8},{10,11... | collective-permute-start | bytes 7077896 | tf_op jit(solution)/shard_map/ppermute | solution.py:388
  4.1 17.5 %collective-permute-start.5 = (bf16[1536,768]{1,0:T(8,128)(2,1)}, bf16[1536,768]{1,0:T(8,128)(2,1)S(1)}, u32[]{:S(2)}, u32[]{:S(2)}) collective-permute-start(bf16[1536,768]{1,0:T(8,128)(2,1)} %bitcast.10), channel_id=1, source_target_pairs={{0,1},{1,0},{2,3},{3,2},{4,5},{5,4},{6,7},{7,6},{8,9},{9,8},{10,11... | collective-permute-start | bytes 7077896 | tf_op jit(solution)/shard_map/ppermute | solution.py:388
  9.9 33.0 %copy-start.1 = (bf16[768,1536]{1,0:T(8,128)(2,1)}, bf16[768,1536]{1,0:T(8,128)(2,1)S(1)}, u32[]{:S(2)}) copy-start(bf16[768,1536]{1,0:T(8,128)(2,1)S(1)} %get-tuple-element.31.refs_3_) | copy-start | bytes 7077892
  9.9 33.0 %copy-start.7 = (f32[1536,256]{1,0:T(8,128)}, f32[1536,256]{1,0:T(8,128)S(1)}, u32[]{:S(2)}) copy-start(f32[1536,256]{1,0:T(8,128)S(1)} %get-tuple-element.42.refs_5_) | copy-start | bytes 4718596
  12.0 2.7 collective-permute-start.2
  14.3 2.9 collective-permute-start.8
  14.8 9.6 %collective-permute-start.3 = (bf16[768,128]{1,0:T(8,128)(2,1)S(1)}, bf16[768,128]{1,0:T(8,128)(2,1)S(1)}, u32[]{:S(2)}, u32[]{:S(2)}) collective-permute-start(bf16[768,128]{1,0:T(8,128)(2,1)S(1)} %both_parts.2), channel_id=1, source_target_pairs={{2,0},{4,2},{6,4},{3,1},{5,3},{7,5},{10,8},{12,10},{14,12},{11,9},... | collective-permute-start | bytes 589832 | tf_op jit(solution)/shard_map/ppermute | solution.py:384
  17.3 12.6 %collective-permute-start.9 = (bf16[768,128]{1,0:T(8,128)(2,1)S(1)}, bf16[768,128]{1,0:T(8,128)(2,1)S(1)}, u32[]{:S(2)}, u32[]{:S(2)}) collective-permute-start(bf16[768,128]{1,0:T(8,128)(2,1)S(1)} %both_parts.3), channel_id=1, source_target_pairs={{2,0},{4,2},{6,4},{3,1},{5,3},{7,5},{10,8},{12,10},{14,12},{11,9},... | collective-permute-start | bytes 589832 | tf_op jit(solution)/shard_map/ppermute | solution.py:384
  21.9 21.1 %copy-start.3 = (bf16[1536,768]{1,0:T(8,128)(2,1)}, bf16[1536,768]{1,0:T(8,128)(2,1)S(1)}, u32[]{:S(2)}) copy-start(bf16[1536,768]{1,0:T(8,128)(2,1)S(1)} %get-tuple-element.38.refs_2_) | copy-start | bytes 7077892
  23.2 19.8 %copy-start.5 = (bf16[768,1536]{1,0:T(8,128)(2,1)}, bf16[768,1536]{1,0:T(8,128)(2,1)S(1)}, u32[]{:S(2)}) copy-start(bf16[768,1536]{1,0:T(8,128)(2,1)S(1)} %get-tuple-element.41.refs_4_) | copy-start | bytes 7077892
  23.2 19.8 %copy-start.9 = (f32[1536,256]{1,0:T(8,128)}, f32[1536,256]{1,0:T(8,128)S(1)}, u32[]{:S(2)}) copy-start(f32[1536,256]{1,0:T(8,128)S(1)} %get-tuple-element.43.refs_6_) | copy-start | bytes 4718596
  27.8 9.8 %collective-permute-start.6 = (bf16[768,128]{1,0:T(8,128)(2,1)S(1)}, bf16[768,128]{1,0:T(8,128)(2,1)S(1)}, u32[]{:S(2)}, u32[]{:S(2)}) collective-permute-start(bf16[768,128]{1,0:T(8,128)(2,1)S(1)} %turn.6), channel_id=1, source_target_pairs={{2,0},{4,2},{6,4},{3,1},{5,3},{7,5},{10,8},{12,10},{14,12},{11,9},... | collective-permute-start | bytes 589832 | tf_op jit(solution)/shard_map/ppermute | solution.py:384
  33.2 9.7 %collective-permute-start.10 = (bf16[768,128]{1,0:T(8,128)(2,1)S(1)}, bf16[768,128]{1,0:T(8,128)(2,1)S(1)}, u32[]{:S(2)}, u32[]{:S(2)}) collective-permute-start(bf16[768,128]{1,0:T(8,128)(2,1)S(1)} %turn.8), channel_id=1, source_target_pairs={{2,0},{4,2},{6,4},{3,1},{5,3},{7,5},{10,8},{12,10},{14,12},{11,9},... | collective-permute-start | bytes 589832 | tf_op jit(solution)/shard_map/ppermute | solution.py:384
  41.0 7.6 %collective-permute-start.7 = (bf16[768,128]{1,0:T(8,128)(2,1)S(1)}, bf16[768,128]{1,0:T(8,128)(2,1)S(1)}, u32[]{:S(2)}, u32[]{:S(2)}) collective-permute-start(bf16[768,128]{1,0:T(8,128)(2,1)S(1)} %turn.7), channel_id=1, source_target_pairs={{2,0},{4,2},{6,4},{3,1},{5,3},{7,5},{10,8},{12,10},{14,12},{11,9},... | collective-permute-start | bytes 589832 | tf_op jit(solution)/shard_map/ppermute | solution.py:384
  43.0 12.7 %copy-start.11 = (bf16[1,1,1536,768]{3,2,1,0:T(8,128)(2,1)S(1)}, bf16[1,1,1536,768]{3,2,1,0:T(8,128)(2,1)}, u32[]{:S(2)}) copy-start(bf16[1,1,1536,768]{3,2,1,0:T(8,128)(2,1)} %param.7) | copy-start | bytes 7077892
  46.4 7.6 %collective-permute-start.11 = (bf16[768,128]{1,0:T(8,128)(2,1)S(1)}, bf16[768,128]{1,0:T(8,128)(2,1)S(1)}, u32[]{:S(2)}, u32[]{:S(2)}) collective-permute-start(bf16[768,128]{1,0:T(8,128)(2,1)S(1)} %turn.9), channel_id=1, source_target_pairs={{2,0},{4,2},{6,4},{3,1},{5,3},{7,5},{10,8},{12,10},{14,12},{11,9},... | collective-permute-start | bytes 589832 | tf_op jit(solution)/shard_map/ppermute | solution.py:384
  48.7 5.6 %collective-permute-start.12 = (bf16[768,128]{1,0:T(8,128)(2,1)S(1)}, bf16[768,128]{1,0:T(8,128)(2,1)S(1)}, u32[]{:S(2)}, u32[]{:S(2)}) collective-permute-start(bf16[768,128]{1,0:T(8,128)(2,1)S(1)} %add_add_fusion.2.refs_0_), channel_id=1, source_target_pairs={{0,1},{1,0},{2,3},{3,2},{4,5},{5,4},{6,7},{7,6},{8,9},{9,8},{10,11... | collective-permute-start | bytes 589832 | tf_op jit(solution)/shard_map/ppermute | solution.py:388
  54.0 1.7 collective-permute-start.13
  60.8 115.1 %all-to-all-start = ((bf16[32,2,48,768]{3,2,1,0:T(8,128)(2,1)}), bf16[32,2,48,768]{3,2,1,0:T(8,128)(2,1)}, u32[]{:S(2)}, u32[]{:S(2)}) async-start(bf16[32,2,48,768]{3,2,1,0:T(8,128)(2,1)} %update.1), calls=%async_computation | async-start | bytes 9437184 | tf_op jit(solution)/shard_map/all_to_all | solution.py:392
  183.3 9.9 %copy-start.13 = (bf16[768,128]{1,0:T(8,128)(2,1)S(1)}, bf16[768,128]{1,0:T(8,128)(2,1)}, u32[]{:S(2)}) copy-start(bf16[768,128]{1,0:T(8,128)(2,1)} %copy-done.12) | copy-start | bytes 589828
  183.3 114.5 %all-to-all-start.1 = ((bf16[32,2,48,768]{3,2,1,0:T(8,128)(2,1)}), bf16[32,2,48,768]{3,2,1,0:T(8,128)(2,1)}, u32[]{:S(2)}, u32[]{:S(2)}) async-start(bf16[32,2,48,768]{3,2,1,0:T(8,128)(2,1)} %mix.1), calls=%async_computation.1 | async-start | bytes 9437184 | tf_op jit(solution)/shard_map/all_to_all | solution.py:392
  208.0 1.5 collective-permute-start.14
  (19 other events, 73.6 us)

commit v8 on v7

--- a/solution.py
+++ b/solution.py
@@ -22,7 +22,6 @@
 VMEM = pl.BlockSpec(memory_space=pltpu.VMEM)
 HBM = pl.BlockSpec(memory_space=pltpu.HBM)
 ANY = pl.BlockSpec(memory_space=pl.ANY)
-SMEM = pl.BlockSpec(memory_space=pltpu.SMEM)
 
 
 def params(mib=20):
@@ -55,10 +54,10 @@
     return jnp.where(core == 0, jnp.concatenate([mine, theirs], axis=1), jnp.concatenate([theirs, mine], axis=1))
 
 
-def opening_kernel(at, x_hbm, other_x_hbm, dy_hbm, other_dy_hbm, w_hbm, *refs):
+def opening_kernel(x_hbm, other_x_hbm, dy_hbm, other_dy_hbm, w_hbm, *refs):
     whole_ref, own_x_ref, cot_ref, a_ref, s_ref, own_s_ref, t_ref = refs[:7]
     x_ref, other_x_ref, dy_ref, other_dy_ref, w_ref, sems = refs[7:]
-    core = at[0]
+    core = lax.axis_index("tp")
     own = own_x_ref.shape[0]
     parts = blocks(w_ref.shape[0])
     pairs = [(x_hbm, x_ref), (other_x_hbm, other_x_ref)]
@@ -83,10 +82,11 @@
     for copy in copies[-2:]:
         copy.wait()
     dy = joined(core, dy_ref[...], other_dy_ref[...])
-    cot_ref[...] = jnp.transpose(jnp.where(at[1] == 1, dy, jnp.zeros_like(dy)))
-
-
-def opening(at, x, other_x, dy, other_dy, weight_in):
+    last = lax.axis_index("section") == lax.axis_size("section") - 1
+    cot_ref[...] = jnp.transpose(jnp.where(last, dy, jnp.zeros_like(dy)))
+
+
+def opening(x, other_x, dy, other_dy, weight_in):
     m, h = dy.shape[0], weight_in.shape[0]
     own = m // 2
     shapes = [
@@ -95,7 +95,7 @@
     return pl.pallas_call(
         opening_kernel,
         out_shape=[pltpu.VMEM(*s) for s in shapes],
-        in_specs=[SMEM] + [ANY] * 5,
+        in_specs=[ANY] * 5,
         out_specs=[VMEM] * len(shapes),
         scratch_shapes=[
             *[pltpu.VMEM(dy.shape, BF)] * 4,
@@ -105,12 +105,13 @@
         compiler_params=params(46),
         cost_estimate=cost(2 * m * h * D, 6 * h * D + 8 * m * h, 2 * m * h),
         name="opening",
-    )(at, x, other_x, dy, other_dy, weight_in)
-
-
-def first_turn_kernel(chunk, m, at, c_ref, wo_ref, wt_ref, s_ref, cot_ref, mine_ref, theirs_ref, delta):
+    )(x, other_x, dy, other_dy, weight_in)
+
+
+def first_turn_kernel(chunk, m, c_ref, wo_ref, wt_ref, s_ref, cot_ref, mine_ref, theirs_ref, delta):
     own = c_ref.shape[1] // 2
-    lanes = [pl.ds(pl.multiple_of(side * own + chunk * m, m), m) for side in (at[0], 1 - at[0])]
+    core = lax.axis_index("tp")
+    lanes = [pl.ds(pl.multiple_of(side * own + chunk * m, m), m) for side in (core, 1 - core)]
     cot = jnp.concatenate([c_ref[:, lane] for lane in lanes], axis=1)
     for at_rows in blocks(wo_ref.shape[0]):
         backward = nn(wo_ref[at_rows, :], cot) * out_scale
@@ -122,19 +123,19 @@
     theirs_ref[...] = partial[:, m:]
 
 
-def first_turn(at, chunk, cot, weight_out, weight_in_t, slopes):
+def first_turn(chunk, cot, weight_out, weight_in_t, slopes):
     h, tokens = slopes.shape
     m = tokens // 2 // CHUNKS
     return pl.pallas_call(
         lambda *refs: first_turn_kernel(chunk, m, *refs),
         out_shape=[jax.ShapeDtypeStruct((D, m), BF)] * 3,
-        in_specs=[SMEM] + [VMEM] * 4,
+        in_specs=[VMEM] * 4,
         out_specs=[VMEM] * 3,
         scratch_shapes=[pltpu.VMEM((h, 2 * m), BF)],
         compiler_params=params(),
         cost_estimate=cost(8 * m * h * D, 4 * h * D + 8 * m * h),
         name="first_turn",
-    )(at, cot, weight_out, weight_in_t, slopes)
+    )(cot, weight_out, weight_in_t, slopes)
 
 
 def both_parts_kernel(c_ref, mine_ref, theirs_ref, o_ref):
@@ -226,23 +227,24 @@
     )(cot, wouts[0], wouts[1], wins_t[0], wins_t[1], slopes[0], slopes[1], after)
 
 
-def leaving_kernel(core, mine_ref, theirs_ref, o_ref):
+def leaving_kernel(mine_ref, theirs_ref, o_ref):
+    core = lax.axis_index("tp")
     own = mine_ref.shape[1]
-    o_ref[pl.ds(pl.multiple_of(core[0] * own, own), own), :] = jnp.transpose(mine_ref[...])
-    o_ref[pl.ds(pl.multiple_of((1 - core[0]) * own, own), own), :] = jnp.transpose(theirs_ref[...])
-
-
-def leaving(core, mine, theirs):
+    o_ref[pl.ds(pl.multiple_of(core * own, own), own), :] = jnp.transpose(mine_ref[...])
+    o_ref[pl.ds(pl.multiple_of((1 - core) * own, own), own), :] = jnp.transpose(theirs_ref[...])
+
+
+def leaving(mine, theirs):
     width, own = mine.shape
     return pl.pallas_call(
         leaving_kernel,
         out_shape=jax.ShapeDtypeStruct((2 * own, width), BF),
-        in_specs=[SMEM, VMEM, VMEM],
+        in_specs=[VMEM, VMEM],
         out_specs=VMEM,
         compiler_params=params(),
         cost_estimate=cost(0, 8 * own * width),
         name="leaving",
-    )(core, mine, theirs)
+    )(mine, theirs)
 
 
 def all_tokens(core, refs):
@@ -254,9 +256,9 @@
 PARTS = 4
 
 
-def update_kernel(core, *refs):
+def update_kernel(*refs):
     a_ref, s_ref, x_ref, wo_ref, wi_ref, o_ref, scratch, sems = refs[2 * CHUNKS :]
-    cot_t, x = all_tokens(core[0], refs[: 2 * CHUNKS]), x_ref[...]
+    cot_t, x = all_tokens(lax.axis_index("tp"), refs[: 2 * CHUNKS]), x_ref[...]
     cot = jnp.transpose(cot_t)
     _, replicas, rows, _ = scratch.shape
     group = replicas // PARTS
@@ -279,40 +281,52 @@
         copy.wait()
 
 
-def update(replicas, core, cots, act_t, slopes_t, x_rows, weight_out, weight_in):
+def update(replicas, cots, act_t, slopes_t, x_rows, weight_out, weight_in):
     h, m = slopes_t.shape
     rows = h // replicas
     return pl.pallas_call(
         update_kernel,
         out_shape=pltpu.HBM((replicas, 2, rows, D), BF),
-        in_specs=[SMEM] + [VMEM] * (2 * CHUNKS + 5),
+        in_specs=[VMEM] * (2 * CHUNKS + 5),
         out_specs=HBM,
         scratch_shapes=[pltpu.VMEM((2, replicas, rows, D), BF), pltpu.SemaphoreType.DMA((2, PARTS))],
         compiler_params=params(24),
         cost_estimate=cost(6 * m * h * D, 6 * m * h + 8 * h * D),
         name="update",
-    )(core, *cots, act_t, slopes_t, x_rows, weight_out, weight_in)
-
-
-def mix_kernel(m_ref, u_ref, o_ref):
-    replicas, _, rows, width = u_ref.shape
-    mixed = nn(m_ref[...], u_ref[...].reshape(replicas * rows, width))
-    o_ref[...] = mixed.astype(BF).reshape(replicas, 1, rows, width)
+    )(*cots, act_t, slopes_t, x_rows, weight_out, weight_in)
+
+
+def mix_kernel(m_ref, u_ref, o_ref, loaded, stored, into, out_of):
+    both, parts, replicas, rows, width = loaded.shape
+    order = [(which, i) for which in range(both) for i in range(parts)]
+    piece = lambda ref, which, i: ref.at[:, which, pl.ds(i * rows, rows), :]
+    loads = [pltpu.make_async_copy(piece(u_ref, *at), loaded.at[at], into.at[at]) for at in order]
+    stores = [pltpu.make_async_copy(stored.at[at], piece(o_ref, *at), out_of.at[at]) for at in order]
+    for load in loads:
+        load.start()
+    for at, load, store in zip(order, loads, stores):
+        load.wait()
+        mixed = nn(m_ref[...], loaded[at].reshape(replicas * rows, width))
+        stored[at] = mixed.astype(BF).reshape(replicas, rows, width)
+        store.start()
+    for store in stores:
+        store.wait()
 
 
 def mix(spread, pieces):
     replicas, both, rows, width = pieces.shape
     block = 16
+    parts = rows // block
     n = spread.shape[0]
-    piece = pl.BlockSpec((replicas, 1, block, width), lambda w, i: (0, w, i, 0))
     return pl.pallas_call(
         mix_kernel,
-        grid=(both, rows // block),
         out_shape=pltpu.HBM(pieces.shape, BF),
-        in_specs=[pl.BlockSpec((n, n), lambda w, i: (0, 0)), piece],
-        out_specs=piece,
-        compiler_params=params(),
-        cost_estimate=cost(2 * n * n * width * both * rows // block, 4 * pieces.size + 2 * n * n),
+        in_specs=[VMEM, ANY],
+        out_specs=HBM,
+        scratch_shapes=[pltpu.VMEM((both, parts, replicas, block, width), BF)] * 2
+        + [pltpu.SemaphoreType.DMA((both, parts))] * 2,
+        compiler_params=params(),
+        cost_estimate=cost(2 * n * n * width * both * parts, 4 * pieces.size + 2 * n * n),
         name="mix",
     )(spread, pieces)
 
@@ -394,7 +408,6 @@
 
 def shards(inputs, loss_grad, w_in, w_out, mixing):
     segments = lax.axis_size("section")
-    segment_index = lax.axis_index("section")
     core = lax.axis_index("tp")
     replicas = lax.axis_size("rep")
     weight_in = w_in[0, 0]
@@ -403,23 +416,18 @@
     tokens = loss_grad.shape[0]
     own = tokens // 2
 
-    core_at = jnp.reshape(core, (1,)).astype(jnp.int32)
-    last = (segment_index == segments - 1).astype(jnp.int32)
-    at = jnp.stack([core.astype(jnp.int32), last])
     other_x = other_core(inputs[0])
     other_dy = other_core(loss_grad)
-    late_in, late_out, other_x, other_dy, at = lax.optimization_barrier(
-        (weight_in, weight_out, other_x, other_dy, at)
-    )
+    late_in, late_out, other_x, other_dy = lax.optimization_barrier((weight_in, weight_out, other_x, other_dy))
     other_in = other_core(late_in)
     other_out = other_core(late_out)
     x_rows, x_own, cot, act_t, slopes_t, own_slopes, own_in_t = opening(
-        at, inputs[0], other_x, loss_grad, other_dy, weight_in
+        inputs[0], other_x, loss_grad, other_dy, weight_in
     )
     spread = spread_matrix(mixing)
 
     columns = own // CHUNKS
-    halves = [first_turn(at, c, cot, weight_out, own_in_t, slopes_t) for c in range(CHUNKS)]
+    halves = [first_turn(c, cot, weight_out, own_in_t, slopes_t) for c in range(CHUNKS)]
     kept_cot = [[half[0] for half in halves]]
     kept_result = [[both_parts(half[0], half[1], other_core(half[2])) for half in halves]]
     cots = [passed_along(r) for r in kept_result[0]]
@@ -445,7 +453,7 @@
 
     mine = summed(kept_cot)
     all_cots = mine + [other_core(part) for part in mine]
-    updated = update(replicas, core_at, all_cots, act_t, slopes_t, x_rows, weight_out, weight_in)
+    updated = update(replicas, all_cots, act_t, slopes_t, x_rows, weight_out, weight_in)
     back = sent_out(mix(spread, sent_out(updated)))
 
     after = updated[0, 0, :16, :128]
@@ -454,7 +462,7 @@
     width = D // 2
     mine = lax.dynamic_slice_in_dim(result, core * width, width, 0)
     theirs = other_core(lax.dynamic_slice_in_dim(result, (1 - core) * width, width, 0))
-    dx = leaving(core_at, mine, theirs)
+    dx = leaving(mine, theirs)
     mixed_in, mixed_out = landed(back, dx[:16, :128])
     whole = (1, 1, units, D)
     return dx[None], mixed_in.reshape(whole), mixed_out.reshape(whole)

time: 306 us -> 305 us (level)
    unnamed x52 -> x54, local copies, waits for them, and re-layouts: 8.65 us -> 11.2 us
where the time goes in v8:
time: 305 us; the launch traced here: 301 us
  waiting for transfers between devices  203 us (67%)
  Pallas kernels  47.9 us (16%)
  starting transfers between devices  36.1 us (12%)
  local copies, waits for them, and re-layouts  12.6 us (4%)
    all_to_all x2, waiting for transfers between devices, sent_out(): return lax.all_to_all(block, 'rep', split_axis=0, concat_axis=0, tiled=True)  192 us
    pallas_call x6, Pallas kernels, turn(): pl.pallas_call(lambda *refs: turn_kernel(col0, *refs), out_shape=jax.Shap...  20 us
    all_to_all x2, starting transfers between devices, sent_out(): return lax.all_to_all(block, 'rep', split_axis=0, concat_axis=0, tiled=True)  19 us
    ppermute x6, starting transfers between devices, passed_along(): lax.ppermute(shard, 'section', [(i, i - 1) for i in range(1, length)])  14.9 us
    unnamed x54, local copies, waits for them, and re-layouts  11.2 us
    pallas_call x1, Pallas kernels, mix(): pl.pallas_call(mix_kernel, out_shape=pltpu.HBM(pieces.shape, BF), in_spec...  6.42 us
    ppermute x6, waiting for transfers between devices, passed_along(): lax.ppermute(shard, 'section', [(i, i - 1) for i in range(1, length)])  6.28 us
  transfers between devices with their start and end apart: 17, of which 8 were waited for; matrix products, arithmetic and copies ran while one was open for 1% of the time, Pallas kernels for 11%

profile of v8, /device:TPU:16, one launch (start us, length us, event | category | flops | bytes accessed | tf_op | source)
XLA Modules:
  0.0 300.9 jit_solution(14233528425899085339)
XLA Ops:
  4.0 4.8 %opening.1 = (bf16[512,768]{1,0:T(8,128)(2,1)S(1)}, bf16[256,768]{1,0:T(8,128)(2,1)S(1)}, bf16[768,512]{1,0:T(8,128)(2,1)S(1)}, bf16[1536,512]{1,0:T(8,128)(2,1)...) custom-call(bf16[512,384]{1,0:T(8,128)(2,1)} %bitcast.25, ...), custom_call_target="tpu_custom_call" | custom-call | flops 1207959552 | bytes 13369344 | tf_op jit(solution)/shard_map/opening/pallas_call | solution.py:95
  12.6 2.4 collective-permute-start.3
  15.0 4.3 %collective-permute-start.9 = (bf16[768,128]{1,0:T(8,128)(2,1)S(1)}, bf16[768,128]{1,0:T(8,128)(2,1)S(1)}, u32[]{:S(2)}, u32[]{:S(2)}) collective-permute-start(bf16[768,128]{1,0:T(8,128)(2,1)S(1)} %both_parts.3), channel_id=1, source_target_pairs={{2,0},{4,2},{6,4},{3,1},{5,3},{7,5},{10,8},{12,10},{14,12},{11,9},... | collective-permute-start | bytes 589832 | tf_op jit(solution)/shard_map/ppermute | solution.py:398
  20.7 1.7 copy-done.12
  22.4 1.8 kept.1
  25.6 3.3 %turn.6 = bf16[768,128]{1,0:T(8,128)(2,1)S(1)} custom-call(bf16[768,128]{1,0:T(8,128)(2,1)S(1)} %collective-permute-done.3.refs_0_, bf16[1536,768]{1,0:T(8,128)(2,1)S(1)} %bitcast.11, bf16[1536,768]{1,0:T(8,128)(2,1)S(1)} %get-tuple-element.36.refs_2_, bf16[768,1536]{1,0:T(8,128)(2,1)S(1)} %get-tuple-element.29.refs_2_.refs_3_, ...), custom_call_target="tpu_custom_call" | custom-call | flops 1207959552 | bytes 11010048 | tf_op jit(solution)/shard_map/turn/pallas_call | solution.py:218
  28.9 1.9 collective-permute-start.6
  30.8 3.3 %turn.8 = bf16[768,128]{1,0:T(8,128)(2,1)S(1)} custom-call(bf16[768,128]{1,0:T(8,128)(2,1)S(1)} %collective-permute-done.9.refs_0_, bf16[1536,768]{1,0:T(8,128)(2,1)S(1)} %bitcast.12, bf16[1536,768]{1,0:T(8,128)(2,1)S(1)} %get-tuple-element.36.refs_2_, bf16[768,1536]{1,0:T(8,128)(2,1)S(1)} %get-tuple-element.29.refs_2_.refs_3_, ...), custom_call_target="tpu_custom_call" | custom-call | flops 1207959552 | bytes 11010048 | tf_op jit(solution)/shard_map/turn/pallas_call | solution.py:218
  34.2 1.9 collective-permute-start.10
  37.2 3.3 %turn.7 = bf16[768,128]{1,0:T(8,128)(2,1)S(1)} custom-call(bf16[768,128]{1,0:T(8,128)(2,1)S(1)} %collective-permute-done.6.refs_0_, bf16[1536,768]{1,0:T(8,128)(2,1)S(1)} %bitcast.13, bf16[1536,768]{1,0:T(8,128)(2,1)S(1)} %get-tuple-element.36.refs_2_, bf16[768,1536]{1,0:T(8,128)(2,1)S(1)} %get-tuple-element.29.refs_2_.refs_3_, ...), custom_call_target="tpu_custom_call" | custom-call | flops 1207959552 | bytes 11010048 | tf_op jit(solution)/shard_map/turn/pallas_call | solution.py:218
  40.6 2.2 collective-permute-start.7
  42.8 3.3 %turn.9 = bf16[768,128]{1,0:T(8,128)(2,1)S(1)} custom-call(bf16[768,128]{1,0:T(8,128)(2,1)S(1)} %collective-permute-done.10.refs_0_, bf16[1536,768]{1,0:T(8,128)(2,1)S(1)} %bitcast.14, bf16[1536,768]{1,0:T(8,128)(2,1)S(1)} %get-tuple-element.36.refs_2_, bf16[768,1536]{1,0:T(8,128)(2,1)S(1)} %get-tuple-element.29.refs_2_.refs_3_, ...), custom_call_target="tpu_custom_call" | custom-call | flops 1207959552 | bytes 11010048 | tf_op jit(solution)/shard_map/turn/pallas_call | solution.py:218
  46.2 2.2 collective-permute-start.11
  48.6 5.2 %collective-permute-done.11.refs_0_ = bf16[768,128]{1,0:T(8,128)(2,1)S(1)} collective-permute-done((bf16[768,128]{1,0:T(8,128)(2,1)S(1)}, bf16[768,128]{1,0:T(8,128)(2,1)S(1)}, u32[]{:S(2)}, u32[]{:S(2)}) %collective-permute-start.11) | collective-permute-done | bytes 196640 | tf_op jit(solution)/shard_map/ppermute | solution.py:398
  55.6 5.1 %update.1 = bf16[32,2,48,768]{3,2,1,0:T(8,128)(2,1)} custom-call(bf16[768,128]{1,0:T(8,128)(2,1)S(1)} %add_add_fusion.2.refs_0_, bf16[768,128]{1,0:T(8,128)(2,1)S(1)} %add_add_fusion.1.refs_1_, bf16[768,128]{1,0:T(8,128)(2,1)S(1)} %collective-permute-done.12.refs_2_, bf16[768,128]{1,0:T(8,128)(2,1)S(1)} %collective-permute-done.13.refs_3_, ...), custom_call_target="tpu_custom_call" | custom-call | flops 3623878656 | bytes 14155776 | tf_op jit(solution)/shard_map/update/pallas_call | solution.py:287
  60.7 9.7 %all-to-all-start = ((bf16[32,2,48,768]{3,2,1,0:T(8,128)(2,1)}), bf16[32,2,48,768]{3,2,1,0:T(8,128)(2,1)}, u32[]{:S(2)}, u32[]{:S(2)}) async-start(bf16[32,2,48,768]{3,2,1,0:T(8,128)(2,1)} %update.1), calls=%async_computation | async-start | bytes 9437184 | tf_op jit(solution)/shard_map/all_to_all | solution.py:406
  70.8 105.0 %all-to-all-done.u_ref = bf16[32,2,48,768]{3,2,1,0:T(8,128)(2,1)} async-done(((bf16[32,2,48,768]{3,2,1,0:T(8,128)(2,1)}), bf16[32,2,48,768]{3,2,1,0:T(8,128)(2,1)}, u32[]{:S(2)}, u32[]{:S(2)}) %all-to-all-start) | async-done | bytes 4718624 | tf_op jit(solution)/shard_map/all_to_all | solution.py:406
  175.8 6.4 %mix.1 = bf16[32,2,48,768]{3,2,1,0:T(8,128)(2,1)} custom-call(bf16[512,512]{1,0:T(8,128)(2,1)S(1)} %spread.1.m_ref, bf16[32,2,48,768]{3,2,1,0:T(8,128)(2,1)} %all-to-all-done.u_ref), custom_call_target="tpu_custom_call" | custom-call | flops 2415919104 | bytes 9961472 | tf_op jit(solution)/shard_map/mix/pallas_call | solution.py:321
  182.2 9.3 %all-to-all-start.1 = ((bf16[32,2,48,768]{3,2,1,0:T(8,128)(2,1)}), bf16[32,2,48,768]{3,2,1,0:T(8,128)(2,1)}, u32[]{:S(2)}, u32[]{:S(2)}) async-start(bf16[32,2,48,768]{3,2,1,0:T(8,128)(2,1)} %mix.1), calls=%async_computation.1 | async-start | bytes 9437184 | tf_op jit(solution)/shard_map/all_to_all | solution.py:406
  192.2 1.7 copy-done.2
  200.0 3.3 %turn.11 = bf16[768,128]{1,0:T(8,128)(2,1)S(1)} custom-call(bf16[768,128]{1,0:T(8,128)(2,1)S(1)} %copy-done.15, bf16[1536,768]{1,0:T(8,128)(2,1)S(1)} %bitcast.16, bf16[1536,768]{1,0:T(8,128)(2,1)S(1)} %copy-done.4, bf16[768,1536]{1,0:T(8,128)(2,1)S(1)} %copy-done.2, bf16[768,1536]{1,0:T(8,128)(2,1)S(1)} %copy-done.6, f32[1536,256]{1,0:T(8,128)S(1)} %copy-done.8, ...), custom_call_target="tpu_custom_call" | custom-call | flops 1207959552 | bytes 11010048 | tf_op jit(solution)/shard_map/turn/pallas_call | solution.py:218
  203.4 3.3 %turn.10 = bf16[768,128]{1,0:T(8,128)(2,1)S(1)} custom-call(bf16[768,128]{1,0:T(8,128)(2,1)S(1)} %collective-permute-done.7.refs_0_, bf16[1536,768]{1,0:T(8,128)(2,1)S(1)} %bitcast.17, bf16[1536,768]{1,0:T(8,128)(2,1)S(1)} %copy-done.4, bf16[768,1536]{1,0:T(8,128)(2,1)S(1)} %copy-done.2, bf16[768,1536]{1,0:T(8,128)(2,1)S(1)} %copy-done.6, ...), custom_call_target="tpu_custom_call" | custom-call | flops 1207959552 | bytes 11010048 | tf_op jit(solution)/shard_map/turn/pallas_call | solution.py:218
  210.0 86.5 %all-to-all-done.1.u_ref = bf16[32,2,48,768]{3,2,1,0:T(8,128)(2,1)} async-done(((bf16[32,2,48,768]{3,2,1,0:T(8,128)(2,1)}), bf16[32,2,48,768]{3,2,1,0:T(8,128)(2,1)}, u32[]{:S(2)}, u32[]{:S(2)}) %all-to-all-start.1) | async-done | bytes 4718624 | tf_op jit(solution)/shard_map/all_to_all | solution.py:406
  296.5 4.1 %landed.1 = (bf16[32,48,768]{2,1,0:T(8,128)(2,1)}, bf16[32,48,768]{2,1,0:T(8,128)(2,1)}) custom-call(bf16[32,2,48,768]{3,2,1,0:T(8,128)(2,1)} %all-to-all-done.1.u_ref, bf16[16,128]{1,0:T(8,128)(2,1)S(1)} %slice.9.after_ref), custom_call_target="tpu_custom_call" | custom-call | bytes 9437184 | tf_op jit(solution)/shard_map/landed/pallas_call | solution.py:380
  (88 shorter events, 23.4 us)
Async XLA Ops:
  0.6 2.0 collective-permute-start
  0.7 2.5 collective-permute-start.1
  3.2 16.1 %collective-permute-start.4 = (bf16[1536,768]{1,0:T(8,128)(2,1)}, bf16[1536,768]{1,0:T(8,128)(2,1)S(1)}, u32[]{:S(2)}, u32[]{:S(2)}) collective-permute-start(bf16[1536,768]{1,0:T(8,128)(2,1)} %bitcast.18), channel_id=1, source_target_pairs={{0,1},{1,0},{2,3},{3,2},{4,5},{5,4},{6,7},{7,6},{8,9},{9,8},{10,11... | collective-permute-start | bytes 7077896 | tf_op jit(solution)/shard_map/ppermute | solution.py:402
  3.4 17.3 %collective-permute-start.5 = (bf16[1536,768]{1,0:T(8,128)(2,1)}, bf16[1536,768]{1,0:T(8,128)(2,1)}, u32[]{:S(2)}, u32[]{:S(2)}) collective-permute-start(bf16[1536,768]{1,0:T(8,128)(2,1)} %bitcast.8), channel_id=1, source_target_pairs={{0,1},{1,0},{2,3},{3,2},{4,5},{5,4},{6,7},{7,6},{8,9},{9,8},{10,11... | collective-permute-start | bytes 7077896 | tf_op jit(solution)/shard_map/ppermute | solution.py:402
  8.8 34.0 %copy-start.1 = (bf16[768,1536]{1,0:T(8,128)(2,1)}, bf16[768,1536]{1,0:T(8,128)(2,1)S(1)}, u32[]{:S(2)}) copy-start(bf16[768,1536]{1,0:T(8,128)(2,1)S(1)} %get-tuple-element.29.refs_2_.refs_3_) | copy-start | bytes 7077892
  8.8 34.0 %copy-start.7 = (f32[1536,256]{1,0:T(8,128)}, f32[1536,256]{1,0:T(8,128)S(1)}, u32[]{:S(2)}) copy-start(f32[1536,256]{1,0:T(8,128)S(1)} %get-tuple-element.40.refs_5_) | copy-start | bytes 4718596
  10.3 2.2 collective-permute-start.2
  12.0 2.9 collective-permute-start.8
  12.6 13.0 %collective-permute-start.3 = (bf16[768,128]{1,0:T(8,128)(2,1)S(1)}, bf16[768,128]{1,0:T(8,128)(2,1)S(1)}, u32[]{:S(2)}, u32[]{:S(2)}) collective-permute-start(bf16[768,128]{1,0:T(8,128)(2,1)S(1)} %both_parts.2), channel_id=1, source_target_pairs={{2,0},{4,2},{6,4},{3,1},{5,3},{7,5},{10,8},{12,10},{14,12},{11,9},... | collective-permute-start | bytes 589832 | tf_op jit(solution)/shard_map/ppermute | solution.py:398
  15.0 15.8 %collective-permute-start.9 = (bf16[768,128]{1,0:T(8,128)(2,1)S(1)}, bf16[768,128]{1,0:T(8,128)(2,1)S(1)}, u32[]{:S(2)}, u32[]{:S(2)}) collective-permute-start(bf16[768,128]{1,0:T(8,128)(2,1)S(1)} %both_parts.3), channel_id=1, source_target_pairs={{2,0},{4,2},{6,4},{3,1},{5,3},{7,5},{10,8},{12,10},{14,12},{11,9},... | collective-permute-start | bytes 589832 | tf_op jit(solution)/shard_map/ppermute | solution.py:398
  24.2 18.6 %copy-start.3 = (bf16[1536,768]{1,0:T(8,128)(2,1)}, bf16[1536,768]{1,0:T(8,128)(2,1)S(1)}, u32[]{:S(2)}) copy-start(bf16[1536,768]{1,0:T(8,128)(2,1)S(1)} %get-tuple-element.36.refs_2_) | copy-start | bytes 7077892
  25.5 17.3 %copy-start.5 = (bf16[768,1536]{1,0:T(8,128)(2,1)}, bf16[768,1536]{1,0:T(8,128)(2,1)S(1)}, u32[]{:S(2)}) copy-start(bf16[768,1536]{1,0:T(8,128)(2,1)S(1)} %get-tuple-element.39.refs_4_) | copy-start | bytes 7077892
  25.5 17.3 %copy-start.9 = (f32[1536,256]{1,0:T(8,128)}, f32[1536,256]{1,0:T(8,128)S(1)}, u32[]{:S(2)}) copy-start(f32[1536,256]{1,0:T(8,128)S(1)} %get-tuple-element.41.refs_6_) | copy-start | bytes 4718596
  28.9 8.3 %collective-permute-start.6 = (bf16[768,128]{1,0:T(8,128)(2,1)S(1)}, bf16[768,128]{1,0:T(8,128)(2,1)S(1)}, u32[]{:S(2)}, u32[]{:S(2)}) collective-permute-start(bf16[768,128]{1,0:T(8,128)(2,1)S(1)} %turn.6), channel_id=1, source_target_pairs={{2,0},{4,2},{6,4},{3,1},{5,3},{7,5},{10,8},{12,10},{14,12},{11,9},... | collective-permute-start | bytes 589832 | tf_op jit(solution)/shard_map/ppermute | solution.py:398
  34.2 8.6 %collective-permute-start.10 = (bf16[768,128]{1,0:T(8,128)(2,1)S(1)}, bf16[768,128]{1,0:T(8,128)(2,1)S(1)}, u32[]{:S(2)}, u32[]{:S(2)}) collective-permute-start(bf16[768,128]{1,0:T(8,128)(2,1)S(1)} %turn.8), channel_id=1, source_target_pairs={{2,0},{4,2},{6,4},{3,1},{5,3},{7,5},{10,8},{12,10},{14,12},{11,9},... | collective-permute-start | bytes 589832 | tf_op jit(solution)/shard_map/ppermute | solution.py:398
  40.6 7.8 %collective-permute-start.7 = (bf16[768,128]{1,0:T(8,128)(2,1)S(1)}, bf16[768,128]{1,0:T(8,128)(2,1)S(1)}, u32[]{:S(2)}, u32[]{:S(2)}) collective-permute-start(bf16[768,128]{1,0:T(8,128)(2,1)S(1)} %turn.7), channel_id=1, source_target_pairs={{2,0},{4,2},{6,4},{3,1},{5,3},{7,5},{10,8},{12,10},{14,12},{11,9},... | collective-permute-start | bytes 589832 | tf_op jit(solution)/shard_map/ppermute | solution.py:398
  42.8 12.7 %copy-start.13 = (bf16[1,1,1536,768]{3,2,1,0:T(8,128)(2,1)S(1)}, bf16[1,1,1536,768]{3,2,1,0:T(8,128)(2,1)}, u32[]{:S(2)}) copy-start(bf16[1,1,1536,768]{3,2,1,0:T(8,128)(2,1)} %param.7) | copy-start | bytes 7077892
  46.2 7.6 %collective-permute-start.11 = (bf16[768,128]{1,0:T(8,128)(2,1)S(1)}, bf16[768,128]{1,0:T(8,128)(2,1)S(1)}, u32[]{:S(2)}, u32[]{:S(2)}) collective-permute-start(bf16[768,128]{1,0:T(8,128)(2,1)S(1)} %turn.9), channel_id=1, source_target_pairs={{2,0},{4,2},{6,4},{3,1},{5,3},{7,5},{10,8},{12,10},{14,12},{11,9},... | collective-permute-start | bytes 589832 | tf_op jit(solution)/shard_map/ppermute | solution.py:398
  48.5 5.7 %collective-permute-start.12 = (bf16[768,128]{1,0:T(8,128)(2,1)S(1)}, bf16[768,128]{1,0:T(8,128)(2,1)S(1)}, u32[]{:S(2)}, u32[]{:S(2)}) collective-permute-start(bf16[768,128]{1,0:T(8,128)(2,1)S(1)} %add_add_fusion.2.refs_0_), channel_id=1, source_target_pairs={{0,1},{1,0},{2,3},{3,2},{4,5},{5,4},{6,7},{7,6},{8,9},{9,8},{10,11... | collective-permute-start | bytes 589832 | tf_op jit(solution)/shard_map/ppermute | solution.py:402
  53.8 1.7 collective-permute-start.13
  60.7 115.1 %all-to-all-start = ((bf16[32,2,48,768]{3,2,1,0:T(8,128)(2,1)}), bf16[32,2,48,768]{3,2,1,0:T(8,128)(2,1)}, u32[]{:S(2)}, u32[]{:S(2)}) async-start(bf16[32,2,48,768]{3,2,1,0:T(8,128)(2,1)} %update.1), calls=%async_computation | async-start | bytes 9437184 | tf_op jit(solution)/shard_map/all_to_all | solution.py:406
  182.2 10.0 %copy-start.15 = (bf16[768,128]{1,0:T(8,128)(2,1)S(1)}, bf16[768,128]{1,0:T(8,128)(2,1)}, u32[]{:S(2)}) copy-start(bf16[768,128]{1,0:T(8,128)(2,1)} %copy-done.14) | copy-start | bytes 589828
  182.2 114.3 %all-to-all-start.1 = ((bf16[32,2,48,768]{3,2,1,0:T(8,128)(2,1)}), bf16[32,2,48,768]{3,2,1,0:T(8,128)(2,1)}, u32[]{:S(2)}, u32[]{:S(2)}) async-start(bf16[32,2,48,768]{3,2,1,0:T(8,128)(2,1)} %mix.1), calls=%async_computation.1 | async-start | bytes 9437184 | tf_op jit(solution)/shard_map/all_to_all | solution.py:406
  206.9 1.5 collective-permute-start.14
  (20 other events, 69.2 us)

commit v9 on v8

--- a/solution.py
+++ b/solution.py
@@ -432,7 +432,7 @@
     kept_result = [[both_parts(half[0], half[1], other_core(half[2])) for half in halves]]
     cots = [passed_along(r) for r in kept_result[0]]
 
-    other_in, other_out = kept(other_in, other_out)
+    (other_out,) = kept(other_out)
     other_slopes, other_in_t = token_slopes(x_own, other_in)
     slopes, wouts, wins_t = (own_slopes, other_slopes), (weight_out, other_out), (own_in_t, other_in_t)
     for turn_index in range(1, segments - 1):

time: 305 us -> 306 us (level)
  no operation moved by 1% of the time
where the time goes in v9:
time: 306 us; the launch traced here: 302 us
  waiting for transfers between devices  203 us (66%)
  Pallas kernels  48.7 us (16%)
  starting transfers between devices  36.3 us (12%)
  local copies, waits for them, and re-layouts  12.6 us (4%)
    all_to_all x2, waiting for transfers between devices, sent_out(): return lax.all_to_all(block, 'rep', split_axis=0, concat_axis=0, tiled=True)  191 us
    pallas_call x6, Pallas kernels, turn(): pl.pallas_call(lambda *refs: turn_kernel(col0, *refs), out_shape=jax.Shap...  20 us
    all_to_all x2, starting transfers between devices, sent_out(): return lax.all_to_all(block, 'rep', split_axis=0, concat_axis=0, tiled=True)  19.2 us
    ppermute x6, starting transfers between devices, passed_along(): lax.ppermute(shard, 'section', [(i, i - 1) for i in range(1, length)])  14.9 us
    unnamed x54, local copies, waits for them, and re-layouts  11.2 us
    pallas_call x1, Pallas kernels, mix(): pl.pallas_call(mix_kernel, out_shape=pltpu.HBM(pieces.shape, BF), in_spec...  6.35 us
    ppermute x6, waiting for transfers between devices, passed_along(): lax.ppermute(shard, 'section', [(i, i - 1) for i in range(1, length)])  6.28 us
  transfers between devices with their start and end apart: 17, of which 8 were waited for; matrix products, arithmetic and copies ran while one was open for 1% of the time, Pallas kernels for 11%

profile of v9, /device:TPU:16, one launch (start us, length us, event | category | flops | bytes accessed | tf_op | source)
XLA Modules:
  0.0 301.7 jit_solution(2984518833723844275)
XLA Ops:
  4.0 4.8 %opening.1 = (bf16[512,768]{1,0:T(8,128)(2,1)S(1)}, bf16[256,768]{1,0:T(8,128)(2,1)S(1)}, bf16[768,512]{1,0:T(8,128)(2,1)S(1)}, bf16[1536,512]{1,0:T(8,128)(2,1)...) custom-call(bf16[512,384]{1,0:T(8,128)(2,1)} %bitcast.25, ...), custom_call_target="tpu_custom_call" | custom-call | flops 1207959552 | bytes 13369344 | tf_op jit(solution)/shard_map/opening/pallas_call | solution.py:95
  12.6 2.4 collective-permute-start.3
  15.0 4.3 %collective-permute-start.9 = (bf16[768,128]{1,0:T(8,128)(2,1)S(1)}, bf16[768,128]{1,0:T(8,128)(2,1)S(1)}, u32[]{:S(2)}, u32[]{:S(2)}) collective-permute-start(bf16[768,128]{1,0:T(8,128)(2,1)S(1)} %both_parts.3), channel_id=1, source_target_pairs={{2,0},{4,2},{6,4},{3,1},{5,3},{7,5},{10,8},{12,10},{14,12},{11,9},... | collective-permute-start | bytes 589832 | tf_op jit(solution)/shard_map/ppermute | solution.py:398
  20.7 1.7 copy-done.12
  22.6 3.8 %token_slopes.1 = (f32[1536,256]{1,0:T(8,128)S(1)}, bf16[768,1536]{1,0:T(8,128)(2,1)S(1)}) custom-call(bf16[256,768]{1,0:T(8,128)(2,1)S(1)} %get-tuple-element.33.x_ref, bf16[1536,768]{1,0:T(8,128)(2,1)} %collective-permute-done.5.w_ref), custom_call_target="tpu_custom_call" | custom-call | flops 603979776 | bytes 6291456 | tf_op jit(solution)/shard_map/token_slopes/pallas_call | solution.py:168
  26.4 3.3 %turn.6 = bf16[768,128]{1,0:T(8,128)(2,1)S(1)} custom-call(bf16[768,128]{1,0:T(8,128)(2,1)S(1)} %collective-permute-done.3.refs_0_, bf16[1536,768]{1,0:T(8,128)(2,1)S(1)} %bitcast.11, bf16[1536,768]{1,0:T(8,128)(2,1)S(1)} %kept.1.refs_2_, bf16[768,1536]{1,0:T(8,128)(2,1)S(1)} %get-tuple-element.27.refs_2_.refs_3_, ...), custom_call_target="tpu_custom_call" | custom-call | flops 1207959552 | bytes 11010048 | tf_op jit(solution)/shard_map/turn/pallas_call | solution.py:218
  29.7 1.9 collective-permute-start.6
  31.7 3.3 %turn.8 = bf16[768,128]{1,0:T(8,128)(2,1)S(1)} custom-call(bf16[768,128]{1,0:T(8,128)(2,1)S(1)} %collective-permute-done.9.refs_0_, bf16[1536,768]{1,0:T(8,128)(2,1)S(1)} %bitcast.12, bf16[1536,768]{1,0:T(8,128)(2,1)S(1)} %kept.1.refs_2_, bf16[768,1536]{1,0:T(8,128)(2,1)S(1)} %get-tuple-element.27.refs_2_.refs_3_, ...), custom_call_target="tpu_custom_call" | custom-call | flops 1207959552 | bytes 11010048 | tf_op jit(solution)/shard_map/turn/pallas_call | solution.py:218
  35.1 1.9 collective-permute-start.10
  38.1 3.3 %turn.7 = bf16[768,128]{1,0:T(8,128)(2,1)S(1)} custom-call(bf16[768,128]{1,0:T(8,128)(2,1)S(1)} %collective-permute-done.6.refs_0_, bf16[1536,768]{1,0:T(8,128)(2,1)S(1)} %bitcast.13, bf16[1536,768]{1,0:T(8,128)(2,1)S(1)} %kept.1.refs_2_, bf16[768,1536]{1,0:T(8,128)(2,1)S(1)} %get-tuple-element.27.refs_2_.refs_3_, ...), custom_call_target="tpu_custom_call" | custom-call | flops 1207959552 | bytes 11010048 | tf_op jit(solution)/shard_map/turn/pallas_call | solution.py:218
  41.4 2.2 collective-permute-start.7
  43.7 3.3 %turn.9 = bf16[768,128]{1,0:T(8,128)(2,1)S(1)} custom-call(bf16[768,128]{1,0:T(8,128)(2,1)S(1)} %collective-permute-done.10.refs_0_, bf16[1536,768]{1,0:T(8,128)(2,1)S(1)} %bitcast.14, bf16[1536,768]{1,0:T(8,128)(2,1)S(1)} %kept.1.refs_2_, bf16[768,1536]{1,0:T(8,128)(2,1)S(1)} %get-tuple-element.27.refs_2_.refs_3_, ...), custom_call_target="tpu_custom_call" | custom-call | flops 1207959552 | bytes 11010048 | tf_op jit(solution)/shard_map/turn/pallas_call | solution.py:218
  47.1 2.2 collective-permute-start.11
  49.4 5.2 %collective-permute-done.11.refs_0_ = bf16[768,128]{1,0:T(8,128)(2,1)S(1)} collective-permute-done((bf16[768,128]{1,0:T(8,128)(2,1)S(1)}, bf16[768,128]{1,0:T(8,128)(2,1)S(1)}, u32[]{:S(2)}, u32[]{:S(2)}) %collective-permute-start.11) | collective-permute-done | bytes 196640 | tf_op jit(solution)/shard_map/ppermute | solution.py:398
  56.4 5.0 %update.1 = bf16[32,2,48,768]{3,2,1,0:T(8,128)(2,1)} custom-call(bf16[768,128]{1,0:T(8,128)(2,1)S(1)} %add_add_fusion.2.refs_0_, bf16[768,128]{1,0:T(8,128)(2,1)S(1)} %add_add_fusion.1.refs_1_, bf16[768,128]{1,0:T(8,128)(2,1)S(1)} %collective-permute-done.12.refs_2_, bf16[768,128]{1,0:T(8,128)(2,1)S(1)} %collective-permute-done.13.refs_3_, ...), custom_call_target="tpu_custom_call" | custom-call | flops 3623878656 | bytes 14155776 | tf_op jit(solution)/shard_map/update/pallas_call | solution.py:287
  61.5 9.7 %all-to-all-start = ((bf16[32,2,48,768]{3,2,1,0:T(8,128)(2,1)}), bf16[32,2,48,768]{3,2,1,0:T(8,128)(2,1)}, u32[]{:S(2)}, u32[]{:S(2)}) async-start(bf16[32,2,48,768]{3,2,1,0:T(8,128)(2,1)} %update.1), calls=%async_computation | async-start | bytes 9437184 | tf_op jit(solution)/shard_map/all_to_all | solution.py:406
  71.6 105.0 %all-to-all-done.u_ref = bf16[32,2,48,768]{3,2,1,0:T(8,128)(2,1)} async-done(((bf16[32,2,48,768]{3,2,1,0:T(8,128)(2,1)}), bf16[32,2,48,768]{3,2,1,0:T(8,128)(2,1)}, u32[]{:S(2)}, u32[]{:S(2)}) %all-to-all-start) | async-done | bytes 4718624 | tf_op jit(solution)/shard_map/all_to_all | solution.py:406
  176.6 6.3 %mix.1 = bf16[32,2,48,768]{3,2,1,0:T(8,128)(2,1)} custom-call(bf16[512,512]{1,0:T(8,128)(2,1)S(1)} %spread.1.m_ref, bf16[32,2,48,768]{3,2,1,0:T(8,128)(2,1)} %all-to-all-done.u_ref), custom_call_target="tpu_custom_call" | custom-call | flops 2415919104 | bytes 9961472 | tf_op jit(solution)/shard_map/mix/pallas_call | solution.py:321
  183.0 9.5 %all-to-all-start.1 = ((bf16[32,2,48,768]{3,2,1,0:T(8,128)(2,1)}), bf16[32,2,48,768]{3,2,1,0:T(8,128)(2,1)}, u32[]{:S(2)}, u32[]{:S(2)}) async-start(bf16[32,2,48,768]{3,2,1,0:T(8,128)(2,1)} %mix.1), calls=%async_computation.1 | async-start | bytes 9437184 | tf_op jit(solution)/shard_map/all_to_all | solution.py:406
  193.1 1.7 copy-done.2
  200.9 3.3 %turn.11 = bf16[768,128]{1,0:T(8,128)(2,1)S(1)} custom-call(bf16[768,128]{1,0:T(8,128)(2,1)S(1)} %copy-done.15, bf16[1536,768]{1,0:T(8,128)(2,1)S(1)} %bitcast.16, bf16[1536,768]{1,0:T(8,128)(2,1)S(1)} %copy-done.4, bf16[768,1536]{1,0:T(8,128)(2,1)S(1)} %copy-done.2, bf16[768,1536]{1,0:T(8,128)(2,1)S(1)} %copy-done.6, f32[1536,256]{1,0:T(8,128)S(1)} %copy-done.8, ...), custom_call_target="tpu_custom_call" | custom-call | flops 1207959552 | bytes 11010048 | tf_op jit(solution)/shard_map/turn/pallas_call | solution.py:218
  204.3 3.3 %turn.10 = bf16[768,128]{1,0:T(8,128)(2,1)S(1)} custom-call(bf16[768,128]{1,0:T(8,128)(2,1)S(1)} %collective-permute-done.7.refs_0_, bf16[1536,768]{1,0:T(8,128)(2,1)S(1)} %bitcast.17, bf16[1536,768]{1,0:T(8,128)(2,1)S(1)} %copy-done.4, bf16[768,1536]{1,0:T(8,128)(2,1)S(1)} %copy-done.2, bf16[768,1536]{1,0:T(8,128)(2,1)S(1)} %copy-done.6, ...), custom_call_target="tpu_custom_call" | custom-call | flops 1207959552 | bytes 11010048 | tf_op jit(solution)/shard_map/turn/pallas_call | solution.py:218
  210.9 86.5 %all-to-all-done.1.u_ref = bf16[32,2,48,768]{3,2,1,0:T(8,128)(2,1)} async-done(((bf16[32,2,48,768]{3,2,1,0:T(8,128)(2,1)}), bf16[32,2,48,768]{3,2,1,0:T(8,128)(2,1)}, u32[]{:S(2)}, u32[]{:S(2)}) %all-to-all-start.1) | async-done | bytes 4718624 | tf_op jit(solution)/shard_map/all_to_all | solution.py:406
  297.4 4.1 %landed.1 = (bf16[32,48,768]{2,1,0:T(8,128)(2,1)}, bf16[32,48,768]{2,1,0:T(8,128)(2,1)}) custom-call(bf16[32,2,48,768]{3,2,1,0:T(8,128)(2,1)} %all-to-all-done.1.u_ref, bf16[16,128]{1,0:T(8,128)(2,1)S(1)} %slice.9.after_ref), custom_call_target="tpu_custom_call" | custom-call | bytes 9437184 | tf_op jit(solution)/shard_map/landed/pallas_call | solution.py:380
  (88 shorter events, 22.3 us)
Async XLA Ops:
  0.6 2.0 collective-permute-start
  0.7 2.5 collective-permute-start.1
  3.2 16.1 %collective-permute-start.4 = (bf16[1536,768]{1,0:T(8,128)(2,1)}, bf16[1536,768]{1,0:T(8,128)(2,1)S(1)}, u32[]{:S(2)}, u32[]{:S(2)}) collective-permute-start(bf16[1536,768]{1,0:T(8,128)(2,1)} %bitcast.8), channel_id=1, source_target_pairs={{0,1},{1,0},{2,3},{3,2},{4,5},{5,4},{6,7},{7,6},{8,9},{9,8},{10,11... | collective-permute-start | bytes 7077896 | tf_op jit(solution)/shard_map/ppermute | solution.py:402
  3.4 19.2 %collective-permute-start.5 = (bf16[1536,768]{1,0:T(8,128)(2,1)}, bf16[1536,768]{1,0:T(8,128)(2,1)}, u32[]{:S(2)}, u32[]{:S(2)}) collective-permute-start(bf16[1536,768]{1,0:T(8,128)(2,1)} %bitcast.18), channel_id=1, source_target_pairs={{0,1},{1,0},{2,3},{3,2},{4,5},{5,4},{6,7},{7,6},{8,9},{9,8},{10,11... | collective-permute-start | bytes 7077896 | tf_op jit(solution)/shard_map/ppermute | solution.py:402
  8.8 34.9 %copy-start.1 = (bf16[768,1536]{1,0:T(8,128)(2,1)}, bf16[768,1536]{1,0:T(8,128)(2,1)S(1)}, u32[]{:S(2)}) copy-start(bf16[768,1536]{1,0:T(8,128)(2,1)S(1)} %get-tuple-element.27.refs_2_.refs_3_) | copy-start | bytes 7077892
  8.8 34.9 %copy-start.7 = (f32[1536,256]{1,0:T(8,128)}, f32[1536,256]{1,0:T(8,128)S(1)}, u32[]{:S(2)}) copy-start(f32[1536,256]{1,0:T(8,128)S(1)} %get-tuple-element.36.refs_5_) | copy-start | bytes 4718596
  10.3 2.2 collective-permute-start.2
  12.0 2.9 collective-permute-start.8
  12.6 13.8 %collective-permute-start.3 = (bf16[768,128]{1,0:T(8,128)(2,1)S(1)}, bf16[768,128]{1,0:T(8,128)(2,1)S(1)}, u32[]{:S(2)}, u32[]{:S(2)}) collective-permute-start(bf16[768,128]{1,0:T(8,128)(2,1)S(1)} %both_parts.2), channel_id=1, source_target_pairs={{2,0},{4,2},{6,4},{3,1},{5,3},{7,5},{10,8},{12,10},{14,12},{11,9},... | collective-permute-start | bytes 589832 | tf_op jit(solution)/shard_map/ppermute | solution.py:398
  15.0 16.7 %collective-permute-start.9 = (bf16[768,128]{1,0:T(8,128)(2,1)S(1)}, bf16[768,128]{1,0:T(8,128)(2,1)S(1)}, u32[]{:S(2)}, u32[]{:S(2)}) collective-permute-start(bf16[768,128]{1,0:T(8,128)(2,1)S(1)} %both_parts.3), channel_id=1, source_target_pairs={{2,0},{4,2},{6,4},{3,1},{5,3},{7,5},{10,8},{12,10},{14,12},{11,9},... | collective-permute-start | bytes 589832 | tf_op jit(solution)/shard_map/ppermute | solution.py:398
  22.5 21.1 %copy-start.3 = (bf16[1536,768]{1,0:T(8,128)(2,1)}, bf16[1536,768]{1,0:T(8,128)(2,1)S(1)}, u32[]{:S(2)}) copy-start(bf16[1536,768]{1,0:T(8,128)(2,1)S(1)} %kept.1.refs_2_) | copy-start | bytes 7077892
  26.4 17.3 %copy-start.5 = (bf16[768,1536]{1,0:T(8,128)(2,1)}, bf16[768,1536]{1,0:T(8,128)(2,1)S(1)}, u32[]{:S(2)}) copy-start(bf16[768,1536]{1,0:T(8,128)(2,1)S(1)} %get-tuple-element.35.refs_4_) | copy-start | bytes 7077892
  26.4 17.3 %copy-start.9 = (f32[1536,256]{1,0:T(8,128)}, f32[1536,256]{1,0:T(8,128)S(1)}, u32[]{:S(2)}) copy-start(f32[1536,256]{1,0:T(8,128)S(1)} %get-tuple-element.37.refs_6_) | copy-start | bytes 4718596
  29.7 8.3 %collective-permute-start.6 = (bf16[768,128]{1,0:T(8,128)(2,1)S(1)}, bf16[768,128]{1,0:T(8,128)(2,1)S(1)}, u32[]{:S(2)}, u32[]{:S(2)}) collective-permute-start(bf16[768,128]{1,0:T(8,128)(2,1)S(1)} %turn.6), channel_id=1, source_target_pairs={{2,0},{4,2},{6,4},{3,1},{5,3},{7,5},{10,8},{12,10},{14,12},{11,9},... | collective-permute-start | bytes 589832 | tf_op jit(solution)/shard_map/ppermute | solution.py:398
  35.1 8.6 %collective-permute-start.10 = (bf16[768,128]{1,0:T(8,128)(2,1)S(1)}, bf16[768,128]{1,0:T(8,128)(2,1)S(1)}, u32[]{:S(2)}, u32[]{:S(2)}) collective-permute-start(bf16[768,128]{1,0:T(8,128)(2,1)S(1)} %turn.8), channel_id=1, source_target_pairs={{2,0},{4,2},{6,4},{3,1},{5,3},{7,5},{10,8},{12,10},{14,12},{11,9},... | collective-permute-start | bytes 589832 | tf_op jit(solution)/shard_map/ppermute | solution.py:398
  41.4 7.9 %collective-permute-start.7 = (bf16[768,128]{1,0:T(8,128)(2,1)S(1)}, bf16[768,128]{1,0:T(8,128)(2,1)S(1)}, u32[]{:S(2)}, u32[]{:S(2)}) collective-permute-start(bf16[768,128]{1,0:T(8,128)(2,1)S(1)} %turn.7), channel_id=1, source_target_pairs={{2,0},{4,2},{6,4},{3,1},{5,3},{7,5},{10,8},{12,10},{14,12},{11,9},... | collective-permute-start | bytes 589832 | tf_op jit(solution)/shard_map/ppermute | solution.py:398
  43.7 12.7 %copy-start.13 = (bf16[1,1,1536,768]{3,2,1,0:T(8,128)(2,1)S(1)}, bf16[1,1,1536,768]{3,2,1,0:T(8,128)(2,1)}, u32[]{:S(2)}) copy-start(bf16[1,1,1536,768]{3,2,1,0:T(8,128)(2,1)} %param.7) | copy-start | bytes 7077892
  47.1 7.6 %collective-permute-start.11 = (bf16[768,128]{1,0:T(8,128)(2,1)S(1)}, bf16[768,128]{1,0:T(8,128)(2,1)S(1)}, u32[]{:S(2)}, u32[]{:S(2)}) collective-permute-start(bf16[768,128]{1,0:T(8,128)(2,1)S(1)} %turn.9), channel_id=1, source_target_pairs={{2,0},{4,2},{6,4},{3,1},{5,3},{7,5},{10,8},{12,10},{14,12},{11,9},... | collective-permute-start | bytes 589832 | tf_op jit(solution)/shard_map/ppermute | solution.py:398
  49.3 5.7 %collective-permute-start.12 = (bf16[768,128]{1,0:T(8,128)(2,1)S(1)}, bf16[768,128]{1,0:T(8,128)(2,1)S(1)}, u32[]{:S(2)}, u32[]{:S(2)}) collective-permute-start(bf16[768,128]{1,0:T(8,128)(2,1)S(1)} %add_add_fusion.2.refs_0_), channel_id=1, source_target_pairs={{0,1},{1,0},{2,3},{3,2},{4,5},{5,4},{6,7},{7,6},{8,9},{9,8},{10,11... | collective-permute-start | bytes 589832 | tf_op jit(solution)/shard_map/ppermute | solution.py:402
  54.7 1.7 collective-permute-start.13
  61.5 115.1 %all-to-all-start = ((bf16[32,2,48,768]{3,2,1,0:T(8,128)(2,1)}), bf16[32,2,48,768]{3,2,1,0:T(8,128)(2,1)}, u32[]{:S(2)}, u32[]{:S(2)}) async-start(bf16[32,2,48,768]{3,2,1,0:T(8,128)(2,1)} %update.1), calls=%async_computation | async-start | bytes 9437184 | tf_op jit(solution)/shard_map/all_to_all | solution.py:406
  182.9 10.2 %copy-start.15 = (bf16[768,128]{1,0:T(8,128)(2,1)S(1)}, bf16[768,128]{1,0:T(8,128)(2,1)}, u32[]{:S(2)}) copy-start(bf16[768,128]{1,0:T(8,128)(2,1)} %copy-done.14) | copy-start | bytes 589828
  183.0 114.4 %all-to-all-start.1 = ((bf16[32,2,48,768]{3,2,1,0:T(8,128)(2,1)}), bf16[32,2,48,768]{3,2,1,0:T(8,128)(2,1)}, u32[]{:S(2)}, u32[]{:S(2)}) async-start(bf16[32,2,48,768]{3,2,1,0:T(8,128)(2,1)} %mix.1), calls=%async_computation.1 | async-start | bytes 9437184 | tf_op jit(solution)/shard_map/all_to_all | solution.py:406
  207.8 1.5 collective-permute-start.14
  (20 other events, 66.6 us)

commit v10 on v8

--- a/solution.py
+++ b/solution.py
@@ -178,21 +178,16 @@
 
 def kept_kernel(*refs):
     count = len(refs) // 2
-    sems = refs[-1]
-    copies = [pltpu.make_async_copy(refs[i], refs[count + i], sems.at[i]) for i in range(count)]
-    for copy in copies:
-        copy.start()
-    for copy in copies:
-        copy.wait()
+    for i in range(count):
+        refs[count + i][...] = refs[i][...]
 
 
 def kept(*arrays, mib=20):
     return pl.pallas_call(
         kept_kernel,
         out_shape=[pltpu.VMEM(array.shape, BF) for array in arrays],
-        in_specs=[ANY] * len(arrays),
+        in_specs=[VMEM] * len(arrays),
         out_specs=[VMEM] * len(arrays),
-        scratch_shapes=[pltpu.SemaphoreType.DMA((len(arrays),))],
         compiler_params=params(mib),
         cost_estimate=cost(0, 4 * sum(array.size for array in arrays)),
         name="kept",

time: 305 us -> 305 us (level)
  no operation moved by 1% of the time
where the time goes in v10:
time: 305 us; the launch traced here: 301 us
  waiting for transfers between devices  203 us (67%)
  Pallas kernels  48 us (16%)
  starting transfers between devices  36.1 us (12%)
  local copies, waits for them, and re-layouts  12.6 us (4%)
    all_to_all x2, waiting for transfers between devices, sent_out(): return lax.all_to_all(block, 'rep', split_axis=0, concat_axis=0, tiled=True)  192 us
    pallas_call x6, Pallas kernels, turn(): pl.pallas_call(lambda *refs: turn_kernel(col0, *refs), out_shape=jax.Shap...  20 us
    all_to_all x2, starting transfers between devices, sent_out(): return lax.all_to_all(block, 'rep', split_axis=0, concat_axis=0, tiled=True)  19 us
    ppermute x6, starting transfers between devices, passed_along(): lax.ppermute(shard, 'section', [(i, i - 1) for i in range(1, length)])  14.9 us
    unnamed x54, local copies, waits for them, and re-layouts  11.2 us
    pallas_call x1, Pallas kernels, mix(): pl.pallas_call(mix_kernel, out_shape=pltpu.HBM(pieces.shape, BF), in_spec...  6.42 us
    ppermute x6, waiting for transfers between devices, passed_along(): lax.ppermute(shard, 'section', [(i, i - 1) for i in range(1, length)])  6.27 us
  transfers between devices with their start and end apart: 17, of which 8 were waited for; matrix products, arithmetic and copies ran while one was open for 1% of the time, Pallas kernels for 11%

profile of v10, /device:TPU:16, one launch (start us, length us, event | category | flops | bytes accessed | tf_op | source)
XLA Modules:
  0.0 301.0 jit_solution(11454227142742959752)
XLA Ops:
  4.0 4.8 %opening.1 = (bf16[512,768]{1,0:T(8,128)(2,1)S(1)}, bf16[256,768]{1,0:T(8,128)(2,1)S(1)}, bf16[768,512]{1,0:T(8,128)(2,1)S(1)}, bf16[1536,512]{1,0:T(8,128)(2,1)...) custom-call(bf16[512,384]{1,0:T(8,128)(2,1)} %bitcast.25, ...), custom_call_target="tpu_custom_call" | custom-call | flops 1207959552 | bytes 13369344 | tf_op jit(solution)/shard_map/opening/pallas_call | solution.py:95
  12.6 2.4 collective-permute-start.3
  15.0 4.3 %collective-permute-start.9 = (bf16[768,128]{1,0:T(8,128)(2,1)S(1)}, bf16[768,128]{1,0:T(8,128)(2,1)S(1)}, u32[]{:S(2)}, u32[]{:S(2)}) collective-permute-start(bf16[768,128]{1,0:T(8,128)(2,1)S(1)} %both_parts.3), channel_id=1, source_target_pairs={{2,0},{4,2},{6,4},{3,1},{5,3},{7,5},{10,8},{12,10},{14,12},{11,9},... | collective-permute-start | bytes 589832 | tf_op jit(solution)/shard_map/ppermute | solution.py:393
  20.7 1.7 copy-done.12
  22.4 2.0 kept.1
  25.7 3.3 %turn.6 = bf16[768,128]{1,0:T(8,128)(2,1)S(1)} custom-call(bf16[768,128]{1,0:T(8,128)(2,1)S(1)} %collective-permute-done.3.refs_0_, bf16[1536,768]{1,0:T(8,128)(2,1)S(1)} %bitcast.11, bf16[1536,768]{1,0:T(8,128)(2,1)S(1)} %get-tuple-element.36.refs_2_, bf16[768,1536]{1,0:T(8,128)(2,1)S(1)} %get-tuple-element.29.refs_2_.refs_3_, ...), custom_call_target="tpu_custom_call" | custom-call | flops 1207959552 | bytes 11010048 | tf_op jit(solution)/shard_map/turn/pallas_call | solution.py:213
  29.0 1.9 collective-permute-start.6
  31.0 3.3 %turn.8 = bf16[768,128]{1,0:T(8,128)(2,1)S(1)} custom-call(bf16[768,128]{1,0:T(8,128)(2,1)S(1)} %collective-permute-done.9.refs_0_, bf16[1536,768]{1,0:T(8,128)(2,1)S(1)} %bitcast.12, bf16[1536,768]{1,0:T(8,128)(2,1)S(1)} %get-tuple-element.36.refs_2_, bf16[768,1536]{1,0:T(8,128)(2,1)S(1)} %get-tuple-element.29.refs_2_.refs_3_, ...), custom_call_target="tpu_custom_call" | custom-call | flops 1207959552 | bytes 11010048 | tf_op jit(solution)/shard_map/turn/pallas_call | solution.py:213
  34.3 1.9 collective-permute-start.10
  37.3 3.3 %turn.7 = bf16[768,128]{1,0:T(8,128)(2,1)S(1)} custom-call(bf16[768,128]{1,0:T(8,128)(2,1)S(1)} %collective-permute-done.6.refs_0_, bf16[1536,768]{1,0:T(8,128)(2,1)S(1)} %bitcast.13, bf16[1536,768]{1,0:T(8,128)(2,1)S(1)} %get-tuple-element.36.refs_2_, bf16[768,1536]{1,0:T(8,128)(2,1)S(1)} %get-tuple-element.29.refs_2_.refs_3_, ...), custom_call_target="tpu_custom_call" | custom-call | flops 1207959552 | bytes 11010048 | tf_op jit(solution)/shard_map/turn/pallas_call | solution.py:213
  40.7 2.2 collective-permute-start.7
  43.0 3.3 %turn.9 = bf16[768,128]{1,0:T(8,128)(2,1)S(1)} custom-call(bf16[768,128]{1,0:T(8,128)(2,1)S(1)} %collective-permute-done.10.refs_0_, bf16[1536,768]{1,0:T(8,128)(2,1)S(1)} %bitcast.14, bf16[1536,768]{1,0:T(8,128)(2,1)S(1)} %get-tuple-element.36.refs_2_, bf16[768,1536]{1,0:T(8,128)(2,1)S(1)} %get-tuple-element.29.refs_2_.refs_3_, ...), custom_call_target="tpu_custom_call" | custom-call | flops 1207959552 | bytes 11010048 | tf_op jit(solution)/shard_map/turn/pallas_call | solution.py:213
  46.3 2.2 collective-permute-start.11
  48.7 5.2 %collective-permute-done.11.refs_0_ = bf16[768,128]{1,0:T(8,128)(2,1)S(1)} collective-permute-done((bf16[768,128]{1,0:T(8,128)(2,1)S(1)}, bf16[768,128]{1,0:T(8,128)(2,1)S(1)}, u32[]{:S(2)}, u32[]{:S(2)}) %collective-permute-start.11) | collective-permute-done | bytes 196640 | tf_op jit(solution)/shard_map/ppermute | solution.py:393
  55.7 5.1 %update.1 = bf16[32,2,48,768]{3,2,1,0:T(8,128)(2,1)} custom-call(bf16[768,128]{1,0:T(8,128)(2,1)S(1)} %add_add_fusion.2.refs_0_, bf16[768,128]{1,0:T(8,128)(2,1)S(1)} %add_add_fusion.1.refs_1_, bf16[768,128]{1,0:T(8,128)(2,1)S(1)} %collective-permute-done.12.refs_2_, bf16[768,128]{1,0:T(8,128)(2,1)S(1)} %collective-permute-done.13.refs_3_, ...), custom_call_target="tpu_custom_call" | custom-call | flops 3623878656 | bytes 14155776 | tf_op jit(solution)/shard_map/update/pallas_call | solution.py:282
  60.8 9.7 %all-to-all-start = ((bf16[32,2,48,768]{3,2,1,0:T(8,128)(2,1)}), bf16[32,2,48,768]{3,2,1,0:T(8,128)(2,1)}, u32[]{:S(2)}, u32[]{:S(2)}) async-start(bf16[32,2,48,768]{3,2,1,0:T(8,128)(2,1)} %update.1), calls=%async_computation | async-start | bytes 9437184 | tf_op jit(solution)/shard_map/all_to_all | solution.py:401
  70.9 105.0 %all-to-all-done.u_ref = bf16[32,2,48,768]{3,2,1,0:T(8,128)(2,1)} async-done(((bf16[32,2,48,768]{3,2,1,0:T(8,128)(2,1)}), bf16[32,2,48,768]{3,2,1,0:T(8,128)(2,1)}, u32[]{:S(2)}, u32[]{:S(2)}) %all-to-all-start) | async-done | bytes 4718624 | tf_op jit(solution)/shard_map/all_to_all | solution.py:401
  175.9 6.4 %mix.1 = bf16[32,2,48,768]{3,2,1,0:T(8,128)(2,1)} custom-call(bf16[512,512]{1,0:T(8,128)(2,1)S(1)} %spread.1.m_ref, bf16[32,2,48,768]{3,2,1,0:T(8,128)(2,1)} %all-to-all-done.u_ref), custom_call_target="tpu_custom_call" | custom-call | flops 2415919104 | bytes 9961472 | tf_op jit(solution)/shard_map/mix/pallas_call | solution.py:316
  182.4 9.3 %all-to-all-start.1 = ((bf16[32,2,48,768]{3,2,1,0:T(8,128)(2,1)}), bf16[32,2,48,768]{3,2,1,0:T(8,128)(2,1)}, u32[]{:S(2)}, u32[]{:S(2)}) async-start(bf16[32,2,48,768]{3,2,1,0:T(8,128)(2,1)} %mix.1), calls=%async_computation.1 | async-start | bytes 9437184 | tf_op jit(solution)/shard_map/all_to_all | solution.py:401
  192.3 1.7 copy-done.2
  200.1 3.3 %turn.11 = bf16[768,128]{1,0:T(8,128)(2,1)S(1)} custom-call(bf16[768,128]{1,0:T(8,128)(2,1)S(1)} %copy-done.15, bf16[1536,768]{1,0:T(8,128)(2,1)S(1)} %bitcast.16, bf16[1536,768]{1,0:T(8,128)(2,1)S(1)} %copy-done.4, bf16[768,1536]{1,0:T(8,128)(2,1)S(1)} %copy-done.2, bf16[768,1536]{1,0:T(8,128)(2,1)S(1)} %copy-done.6, f32[1536,256]{1,0:T(8,128)S(1)} %copy-done.8, ...), custom_call_target="tpu_custom_call" | custom-call | flops 1207959552 | bytes 11010048 | tf_op jit(solution)/shard_map/turn/pallas_call | solution.py:213
  203.5 3.3 %turn.10 = bf16[768,128]{1,0:T(8,128)(2,1)S(1)} custom-call(bf16[768,128]{1,0:T(8,128)(2,1)S(1)} %collective-permute-done.7.refs_0_, bf16[1536,768]{1,0:T(8,128)(2,1)S(1)} %bitcast.17, bf16[1536,768]{1,0:T(8,128)(2,1)S(1)} %copy-done.4, bf16[768,1536]{1,0:T(8,128)(2,1)S(1)} %copy-done.2, bf16[768,1536]{1,0:T(8,128)(2,1)S(1)} %copy-done.6, ...), custom_call_target="tpu_custom_call" | custom-call | flops 1207959552 | bytes 11010048 | tf_op jit(solution)/shard_map/turn/pallas_call | solution.py:213
  210.2 86.5 %all-to-all-done.1.u_ref = bf16[32,2,48,768]{3,2,1,0:T(8,128)(2,1)} async-done(((bf16[32,2,48,768]{3,2,1,0:T(8,128)(2,1)}), bf16[32,2,48,768]{3,2,1,0:T(8,128)(2,1)}, u32[]{:S(2)}, u32[]{:S(2)}) %all-to-all-start.1) | async-done | bytes 4718624 | tf_op jit(solution)/shard_map/all_to_all | solution.py:401
  296.7 4.1 %landed.1 = (bf16[32,48,768]{2,1,0:T(8,128)(2,1)}, bf16[32,48,768]{2,1,0:T(8,128)(2,1)}) custom-call(bf16[32,2,48,768]{3,2,1,0:T(8,128)(2,1)} %all-to-all-done.1.u_ref, bf16[16,128]{1,0:T(8,128)(2,1)S(1)} %slice.9.after_ref), custom_call_target="tpu_custom_call" | custom-call | bytes 9437184 | tf_op jit(solution)/shard_map/landed/pallas_call | solution.py:375
  (88 shorter events, 23.3 us)
Async XLA Ops:
  0.6 2.0 collective-permute-start
  0.7 2.5 collective-permute-start.1
  3.2 16.1 %collective-permute-start.4 = (bf16[1536,768]{1,0:T(8,128)(2,1)}, bf16[1536,768]{1,0:T(8,128)(2,1)S(1)}, u32[]{:S(2)}, u32[]{:S(2)}) collective-permute-start(bf16[1536,768]{1,0:T(8,128)(2,1)} %bitcast.18), channel_id=1, source_target_pairs={{0,1},{1,0},{2,3},{3,2},{4,5},{5,4},{6,7},{7,6},{8,9},{9,8},{10,11... | collective-permute-start | bytes 7077896 | tf_op jit(solution)/shard_map/ppermute | solution.py:397
  3.4 17.3 %collective-permute-start.5 = (bf16[1536,768]{1,0:T(8,128)(2,1)}, bf16[1536,768]{1,0:T(8,128)(2,1)}, u32[]{:S(2)}, u32[]{:S(2)}) collective-permute-start(bf16[1536,768]{1,0:T(8,128)(2,1)} %bitcast.8), channel_id=1, source_target_pairs={{0,1},{1,0},{2,3},{3,2},{4,5},{5,4},{6,7},{7,6},{8,9},{9,8},{10,11... | collective-permute-start | bytes 7077896 | tf_op jit(solution)/shard_map/ppermute | solution.py:397
  8.8 34.2 %copy-start.1 = (bf16[768,1536]{1,0:T(8,128)(2,1)}, bf16[768,1536]{1,0:T(8,128)(2,1)S(1)}, u32[]{:S(2)}) copy-start(bf16[768,1536]{1,0:T(8,128)(2,1)S(1)} %get-tuple-element.29.refs_2_.refs_3_) | copy-start | bytes 7077892
  8.8 34.2 %copy-start.7 = (f32[1536,256]{1,0:T(8,128)}, f32[1536,256]{1,0:T(8,128)S(1)}, u32[]{:S(2)}) copy-start(f32[1536,256]{1,0:T(8,128)S(1)} %get-tuple-element.40.refs_5_) | copy-start | bytes 4718596
  10.3 2.2 collective-permute-start.2
  12.0 2.9 collective-permute-start.8
  12.6 13.1 %collective-permute-start.3 = (bf16[768,128]{1,0:T(8,128)(2,1)S(1)}, bf16[768,128]{1,0:T(8,128)(2,1)S(1)}, u32[]{:S(2)}, u32[]{:S(2)}) collective-permute-start(bf16[768,128]{1,0:T(8,128)(2,1)S(1)} %both_parts.2), channel_id=1, source_target_pairs={{2,0},{4,2},{6,4},{3,1},{5,3},{7,5},{10,8},{12,10},{14,12},{11,9},... | collective-permute-start | bytes 589832 | tf_op jit(solution)/shard_map/ppermute | solution.py:393
  15.0 15.9 %collective-permute-start.9 = (bf16[768,128]{1,0:T(8,128)(2,1)S(1)}, bf16[768,128]{1,0:T(8,128)(2,1)S(1)}, u32[]{:S(2)}, u32[]{:S(2)}) collective-permute-start(bf16[768,128]{1,0:T(8,128)(2,1)S(1)} %both_parts.3), channel_id=1, source_target_pairs={{2,0},{4,2},{6,4},{3,1},{5,3},{7,5},{10,8},{12,10},{14,12},{11,9},... | collective-permute-start | bytes 589832 | tf_op jit(solution)/shard_map/ppermute | solution.py:393
  24.3 18.6 %copy-start.3 = (bf16[1536,768]{1,0:T(8,128)(2,1)}, bf16[1536,768]{1,0:T(8,128)(2,1)S(1)}, u32[]{:S(2)}) copy-start(bf16[1536,768]{1,0:T(8,128)(2,1)S(1)} %get-tuple-element.36.refs_2_) | copy-start | bytes 7077892
  25.6 17.3 %copy-start.5 = (bf16[768,1536]{1,0:T(8,128)(2,1)}, bf16[768,1536]{1,0:T(8,128)(2,1)S(1)}, u32[]{:S(2)}) copy-start(bf16[768,1536]{1,0:T(8,128)(2,1)S(1)} %get-tuple-element.39.refs_4_) | copy-start | bytes 7077892
  25.6 17.3 %copy-start.9 = (f32[1536,256]{1,0:T(8,128)}, f32[1536,256]{1,0:T(8,128)S(1)}, u32[]{:S(2)}) copy-start(f32[1536,256]{1,0:T(8,128)S(1)} %get-tuple-element.41.refs_6_) | copy-start | bytes 4718596
  29.0 8.3 %collective-permute-start.6 = (bf16[768,128]{1,0:T(8,128)(2,1)S(1)}, bf16[768,128]{1,0:T(8,128)(2,1)S(1)}, u32[]{:S(2)}, u32[]{:S(2)}) collective-permute-start(bf16[768,128]{1,0:T(8,128)(2,1)S(1)} %turn.6), channel_id=1, source_target_pairs={{2,0},{4,2},{6,4},{3,1},{5,3},{7,5},{10,8},{12,10},{14,12},{11,9},... | collective-permute-start | bytes 589832 | tf_op jit(solution)/shard_map/ppermute | solution.py:393
  34.3 8.6 %collective-permute-start.10 = (bf16[768,128]{1,0:T(8,128)(2,1)S(1)}, bf16[768,128]{1,0:T(8,128)(2,1)S(1)}, u32[]{:S(2)}, u32[]{:S(2)}) collective-permute-start(bf16[768,128]{1,0:T(8,128)(2,1)S(1)} %turn.8), channel_id=1, source_target_pairs={{2,0},{4,2},{6,4},{3,1},{5,3},{7,5},{10,8},{12,10},{14,12},{11,9},... | collective-permute-start | bytes 589832 | tf_op jit(solution)/shard_map/ppermute | solution.py:393
  40.7 7.8 %collective-permute-start.7 = (bf16[768,128]{1,0:T(8,128)(2,1)S(1)}, bf16[768,128]{1,0:T(8,128)(2,1)S(1)}, u32[]{:S(2)}, u32[]{:S(2)}) collective-permute-start(bf16[768,128]{1,0:T(8,128)(2,1)S(1)} %turn.7), channel_id=1, source_target_pairs={{2,0},{4,2},{6,4},{3,1},{5,3},{7,5},{10,8},{12,10},{14,12},{11,9},... | collective-permute-start | bytes 589832 | tf_op jit(solution)/shard_map/ppermute | solution.py:393
  43.0 12.7 %copy-start.13 = (bf16[1,1,1536,768]{3,2,1,0:T(8,128)(2,1)S(1)}, bf16[1,1,1536,768]{3,2,1,0:T(8,128)(2,1)}, u32[]{:S(2)}) copy-start(bf16[1,1,1536,768]{3,2,1,0:T(8,128)(2,1)} %param.7) | copy-start | bytes 7077892
  46.3 7.6 %collective-permute-start.11 = (bf16[768,128]{1,0:T(8,128)(2,1)S(1)}, bf16[768,128]{1,0:T(8,128)(2,1)S(1)}, u32[]{:S(2)}, u32[]{:S(2)}) collective-permute-start(bf16[768,128]{1,0:T(8,128)(2,1)S(1)} %turn.9), channel_id=1, source_target_pairs={{2,0},{4,2},{6,4},{3,1},{5,3},{7,5},{10,8},{12,10},{14,12},{11,9},... | collective-permute-start | bytes 589832 | tf_op jit(solution)/shard_map/ppermute | solution.py:393
  48.6 5.7 %collective-permute-start.12 = (bf16[768,128]{1,0:T(8,128)(2,1)S(1)}, bf16[768,128]{1,0:T(8,128)(2,1)S(1)}, u32[]{:S(2)}, u32[]{:S(2)}) collective-permute-start(bf16[768,128]{1,0:T(8,128)(2,1)S(1)} %add_add_fusion.2.refs_0_), channel_id=1, source_target_pairs={{0,1},{1,0},{2,3},{3,2},{4,5},{5,4},{6,7},{7,6},{8,9},{9,8},{10,11... | collective-permute-start | bytes 589832 | tf_op jit(solution)/shard_map/ppermute | solution.py:397
  53.9 1.7 collective-permute-start.13
  60.8 115.2 %all-to-all-start = ((bf16[32,2,48,768]{3,2,1,0:T(8,128)(2,1)}), bf16[32,2,48,768]{3,2,1,0:T(8,128)(2,1)}, u32[]{:S(2)}, u32[]{:S(2)}) async-start(bf16[32,2,48,768]{3,2,1,0:T(8,128)(2,1)} %update.1), calls=%async_computation | async-start | bytes 9437184 | tf_op jit(solution)/shard_map/all_to_all | solution.py:401
  182.4 10.0 %copy-start.15 = (bf16[768,128]{1,0:T(8,128)(2,1)S(1)}, bf16[768,128]{1,0:T(8,128)(2,1)}, u32[]{:S(2)}) copy-start(bf16[768,128]{1,0:T(8,128)(2,1)} %copy-done.14) | copy-start | bytes 589828
  182.4 114.3 %all-to-all-start.1 = ((bf16[32,2,48,768]{3,2,1,0:T(8,128)(2,1)}), bf16[32,2,48,768]{3,2,1,0:T(8,128)(2,1)}, u32[]{:S(2)}, u32[]{:S(2)}) async-start(bf16[32,2,48,768]{3,2,1,0:T(8,128)(2,1)} %mix.1), calls=%async_computation.1 | async-start | bytes 9437184 | tf_op jit(solution)/shard_map/all_to_all | solution.py:401
  207.1 1.5 collective-permute-start.14
  (20 other events, 69.2 us)
